TPU v7x, 32 devices: a whole 2x2x4 slice. The times are simulated.
32 devices in a mesh: ax: 8 (over y, x, core), xs: 4 (over z).
Axes of the slice: x: 2, y: 2, z: 4, core: 2. Of those that a mesh axis runs over, the one named last changes fastest.
Arguments:
- populations: float32 [19, 32, 256, 256], P(None, 'ax', 'xs'), may hold values from 0.001 to 0.75, as said below
- fluid_mask: int32 [32, 256, 256], P('ax', 'xs'), may hold values 0 or 1
- patch_voxel: int32 [256, 512], P(('ax', 'xs')), may hold values from 0 to 65535
- patch_owner: int32 [256], P(('ax', 'xs')), may hold values from 0 to 3, as said below
- positions: float32 [256, 3, 512], P(('ax', 'xs')), may hold values from 0 to 5.5
- velocities: float32 [256, 3, 512], P(('ax', 'xs')), may hold values from -6 to 6
- pair_tiles: int32 [256, 8, 2], P(('ax', 'xs')), may hold values from 0 to 3
- pair_noise: bfloat16 [256, 8, 128, 128], P(('ax', 'xs')), may hold values from -6 to 6
Outputs:
- populations_out: float32 [19, 32, 256, 256], P(None, 'ax', 'xs')
- new_positions: float32 [256, 3, 512], P(('ax', 'xs'))
- new_velocities: float32 [256, 3, 512], P(('ax', 'xs'))
- drag_field: float32 [3, 32, 256, 256], P(None, 'ax', 'xs')
Inputs may be any that keep to these rules, and one draw needn't show every extreme that they name: `patch_owner`: among the 8 patches of every device, each index along xs is named exactly 2 times. `populations`: every distribution is positive.
All inputs are finite; a program needn't handle non-finite values. No bound on the sum of `fluid_mask` on one device may be relied on, other than what follows from the above.
Results may differ from a plain program's by a relative error of at most 0.0003.
Values sent between devices are 32-bit elements; how exact they have to be, the bound alone decides.
No kernel may reach another device: no remote copies, remote signals or barrier semaphores. Data moves between devices by JAX's collectives and lax.ppermute only.
A program may use at most 128 MiB of HBM per device.

v0:
```python
import jax
import jax.numpy as jnp
from jax import lax
from jax.sharding import PartitionSpec as P

LATTICE_DIRS = [
    (0, 0, 0),
    (1, 0, 0),
    (-1, 0, 0),
    (0, 1, 0),
    (0, -1, 0),
    (0, 0, 1),
    (0, 0, -1),
    (1, 1, 0),
    (-1, -1, 0),
    (1, -1, 0),
    (-1, 1, 0),
    (1, 0, 1),
    (-1, 0, -1),
    (1, 0, -1),
    (-1, 0, 1),
    (0, 1, 1),
    (0, -1, -1),
    (0, 1, -1),
    (0, -1, 1),
]
LATTICE_WEIGHTS = [1.0 / 3.0] + [1.0 / 18.0] * 6 + [1.0 / 36.0] * 12
OPPOSITE_DIR = [0, 2, 1, 4, 3, 6, 5, 8, 7, 10, 9, 12, 11, 14, 13, 16, 15, 18, 17]
RELAX_TIME = 0.8
TIME_STEP = 0.04
REPULSION = 25.0
FRICTION = 4.5
NOISE_AMP = 3.0
DRAG_COEFF = 12.5
VELOCITY_SCALE = 20.0
SOFTENING = 0.01


def padded_2(cells, sides, width, closed):
    for axis, dim in sides:
        count = lax.axis_size(axis)
        ends = count if closed else count - 1
        head = lax.slice_in_dim(cells, 0, width, axis=dim)
        tail = lax.slice_in_dim(cells, cells.shape[dim] - width, cells.shape[dim], axis=dim)
        cells = jnp.concatenate(
            [
                lax.ppermute(tail, axis, [(i, (i + 1) % count) for i in range(ends)]),
                cells,
                lax.ppermute(head, axis, [((i + 1) % count, i) for i in range(ends)]),
            ],
            axis=dim,
        )
    return cells


def moments(dist):
    density = jnp.sum(dist, axis=0)
    comps = []
    for axis in range(3):
        total = jnp.zeros_like(density)
        for index in range(19):
            sign = LATTICE_DIRS[index][axis]
            if sign != 0:
                total = total + sign * dist[index]
        comps.append(total / density)
    return (density, comps)


def collide(dist):
    density, comps = moments(dist)
    speed_sq = comps[0] * comps[0] + comps[1] * comps[1] + comps[2] * comps[2]
    out = []
    for index in range(19):
        dirx, diry, dirz = LATTICE_DIRS[index]
        proj = dirx * comps[0] + diry * comps[1] + dirz * comps[2]
        equil = (
            LATTICE_WEIGHTS[index]
            * density
            * (1.0 + 3.0 * proj + 4.5 * proj * proj - 1.5 * speed_sq)
        )
        out.append(dist[index] - (dist[index] - equil) / RELAX_TIME)
    return jnp.stack(out)


def stream_padded(padded, post):
    size_x, size_y, size_z = (post.shape[1], post.shape[2], post.shape[3])
    out = []
    for index in range(19):
        dirx, diry, dirz = LATTICE_DIRS[index]
        start_x, start_y, start_z = (1 - dirx, 1 - diry, 1 - dirz)
        source = padded[
            index,
            start_x : start_x + size_x,
            start_y : start_y + size_y,
            start_z : start_z + size_z,
        ]
        source_mask = padded[
            19, start_x : start_x + size_x, start_y : start_y + size_y, start_z : start_z + size_z
        ]
        out.append(jnp.where(source_mask > 0.5, source, post[OPPOSITE_DIR[index]]))
    return jnp.stack(out)


def pad_depth(block):
    return jnp.pad(block, ((0, 0), (0, 0), (0, 0), (1, 1)))


def lattice_step(dist, fluid):
    post = collide(dist)
    stacked = jnp.concatenate([post, fluid[None]], axis=0)
    axial = padded_2(stacked, (("ax", 1),), 1, True)
    full = padded_2(axial, (("xs", 2),), 1, False)
    return stream_padded(pad_depth(full), post)


def pair_forces(position, velocity, pair_list, noise):
    tile = noise.shape[-1]
    count = position.shape[1] // tile
    pos_tiles = position.reshape(3, count, tile)
    vel_tiles = velocity.reshape(3, count, tile)

    def one_pair(carry, item):
        pair, noise_tile = item
        pos_a = lax.dynamic_index_in_dim(pos_tiles, pair[0], 1, keepdims=False)
        pos_b = lax.dynamic_index_in_dim(pos_tiles, pair[1], 1, keepdims=False)
        vel_a = lax.dynamic_index_in_dim(vel_tiles, pair[0], 1, keepdims=False)
        vel_b = lax.dynamic_index_in_dim(vel_tiles, pair[1], 1, keepdims=False)
        delta = pos_a[:, :, None] - pos_b[:, None, :]
        distance = jnp.sqrt(jnp.sum(delta * delta, axis=0) + SOFTENING)
        weight = jnp.maximum(0.0, 1.0 - distance)
        unit = delta / distance
        along = jnp.sum(unit * (vel_a[:, :, None] - vel_b[:, None, :]), axis=0)
        scalar = (
            REPULSION * weight
            - FRICTION * weight * weight * along
            + NOISE_AMP * weight * noise_tile.astype(jnp.float32) / jnp.sqrt(TIME_STEP)
        )
        force = jnp.sum(scalar[None] * unit, axis=2)
        current = lax.dynamic_index_in_dim(carry, pair[0], 1, keepdims=False)
        carry = lax.dynamic_update_index_in_dim(carry, current + force, pair[0], 1)
        return (carry, None)

    start = jnp.zeros((3, count, tile), jnp.float32)
    total, unused = lax.scan(one_pair, start, (pair_list, noise))
    return total.reshape(3, count * tile)


def patch_step(item):
    position, velocity, flow, pair_list, noise = item
    drag = DRAG_COEFF * (flow - velocity)
    new_vel = velocity + TIME_STEP * (pair_forces(position, velocity, pair_list, noise) + drag)
    new_pos = position + TIME_STEP * new_vel
    return (new_pos, new_vel, -TIME_STEP * drag)


def per_device(
    populations, fluid_mask, patch_voxel, patch_owner, positions, velocities, pair_tiles, pair_noise
):
    fluid = fluid_mask.astype(jnp.float32)
    dist = populations
    for step in range(2):
        dist = lattice_step(dist, fluid)
    density, comps = moments(dist)
    cells = dist.shape[1] * dist.shape[2] * dist.shape[3]
    velocity_flat = VELOCITY_SCALE * jnp.stack(comps).reshape(3, cells)
    patch_count, bead_count = patch_voxel.shape
    owners = lax.axis_size("xs")
    share = patch_count // owners
    at_beads = jnp.transpose(velocity_flat[:, patch_voxel], (1, 0, 2))
    order = jnp.argsort(patch_owner, stable=True)
    grouped = at_beads[order].reshape(owners, share, 3, bead_count)
    received = lax.all_to_all(grouped, "xs", split_axis=0, concat_axis=0, tiled=True).reshape(
        patch_count, 3, bead_count
    )
    new_pos, new_vel, reaction = lax.map(
        patch_step, (positions, velocities, received, pair_tiles, pair_noise)
    )
    returned = lax.all_to_all(
        reaction.reshape(owners, share, 3, bead_count),
        "xs",
        split_axis=0,
        concat_axis=0,
        tiled=True,
    )
    returned = returned.reshape(patch_count, 3, bead_count)
    back = returned[jnp.argsort(order)]
    flat_ids = patch_voxel.reshape(-1)
    field = jnp.stack(
        [
            jax.ops.segment_sum(back[:, comp, :].reshape(-1), flat_ids, num_segments=cells)
            for comp in range(3)
        ]
    )
    return (dist, new_pos, new_vel, field.reshape(3, dist.shape[1], dist.shape[2], dist.shape[3]))


def solution(mesh):
    return jax.shard_map(
        per_device,
        mesh=mesh,
        in_specs=(
            P(None, "ax", "xs", None),
            P("ax", "xs", None),
            P(("ax", "xs"), None),
            P(("ax", "xs")),
            P(("ax", "xs"), None, None),
            P(("ax", "xs"), None, None),
            P(("ax", "xs"), None, None),
            P(("ax", "xs"), None, None, None),
        ),
        out_specs=(
            P(None, "ax", "xs", None),
            P(("ax", "xs"), None, None),
            P(("ax", "xs"), None, None),
            P(None, "ax", "xs", None),
        ),
        check_vma=False,
    )
```

profile of v0, /device:TPU:0, one launch (start us, length us, event | category | flops | bytes accessed | tf_op | source)
XLA Modules:
  0.0 682.2 jit_solution(8997776063943167558)
XLA Ops:
  0.6 2.8 reduce_sum.2318
  3.4 3.8 constant_dynamic-update-slice_fusion.18
  17.7 2.9 collective-permute-start.1
  20.6 26.6 %collective-permute-done = f32[20,1,64,256]{3,2,1,0:T(8,128)S(1)} collective-permute-done((f32[20,1,64,256]{3,2,1,0:T(8,128)S(1)}, f32[20,1,64,256]{3,2,1,0:T(8,128)S(1)}, u32[]{:S(2)}, u32[]{:S(2)}) %collective-permute-start) | collective-permute-done | bytes 1310752 | tf_op jit(solution)/shard_map/ppermute | solution.py:47
  47.2 1.5 collective-permute-done.1
  49.0 3.5 collective-permute-start.2
  53.8 2.1 collective-permute-done.2
  56.0 4.6 collective-permute-done.3
  60.8 8.1 %select_maximum_fusion.4 = f32[20,6,66,258]{3,2,1,0:T(8,128)S(1)} fusion(f32[20,6,1,256]{3,2,1,0:T(1,128)S(1)} %copy.136, f32[20,6,1,256]{3,2,1,0:T(1,128)S(1)} %copy.134, f32[20,1,64,256]{3,2,1,0:T(8,128)S(1)} %collective-permute-done.1, f32[20,4,64,256]{3,2,1,0:T(8,128)S(1)} %bitcast_dynamic-update-slice_fusion.1, ...), kind=kLoop, calls=%fused_computation.47 | loop fusion | flops 24520320 | bytes 16283520 | tf_op jit(solution)/shard_map/concatenate | solution.py:45
  68.9 5.3 constant_dynamic-update-slice_fusion.37
  74.2 1.9 constant_dynamic-update-slice_fusion.36
  76.0 1.8 constant_dynamic-update-slice_fusion.35
  77.9 1.8 constant_dynamic-update-slice_fusion.34
  92.4 2.3 copy-done
  94.7 1.7 fusion.301
  96.4 1.5 collective-permute-start.5
  100.0 27.3 %collective-permute-done.5 = f32[20,1,64,256]{3,2,1,0:T(8,128)S(1)} collective-permute-done((f32[20,1,64,256]{3,2,1,0:T(8,128)}, f32[20,1,64,256]{3,2,1,0:T(8,128)S(1)}, u32[]{:S(2)}, u32[]{:S(2)}) %collective-permute-start.5) | collective-permute-done | bytes 1310752 | tf_op jit(solution)/shard_map/ppermute | solution.py:49
  128.1 1.5 pad_maximum_fusion.19
  130.9 5.2 collective-permute-start.6
  139.5 11.6 %select_maximum_fusion = f32[20,6,66,258]{3,2,1,0:T(8,128)} fusion(f32[20,6,1,256]{3,2,1,0:T(1,128)S(1)} %copy.142, f32[20,6,1,256]{3,2,1,0:T(1,128)S(1)} %copy.140, f32[20,1,64,256]{3,2,1,0:T(8,128)S(1)} %collective-permute-done.5, f32[20,4,64,256]{3,2,1,0:T(8,128)} %copy-done, f32[20,1,64,256]{3,2,1,0:T(8,128)S(1)} %collective-permute-done.4), kind=kLoop, calls=%fused_computation.43 | loop fusion | flops 24520320 | bytes 16283520 | tf_op jit(solution)/shard_map/concatenate | solution.py:45
  151.1 8.4 %add_divide_fusion.2 = (f32[1,4,64,256]{3,2,1,0:T(8,128)}, f32[1,4,64,256]{3,2,1,0:T(8,128)}, f32[1,4,64,256]{3,2,1,0:T(8,128)S(1)}, f32[1,4,64,256]{3,2,1,0:T(8...) fusion(f32[1,4,64,256]{3,2,1,0:T(8,128)S(1)} %get-tuple-element, ...), kind=kLoop, calls=%fused_computation.419 | loop fusion | flops 7143424 | bytes 23576576 | tf_op jit(solution)/shard_map/div | solution.py:65
  159.6 1.8 constant_dynamic-update-slice_fusion.55
  161.4 1.7 constant_dynamic-update-slice_fusion.54
  163.1 1.7 constant_dynamic-update-slice_fusion.53
  164.8 1.7 constant_dynamic-update-slice_fusion.52
  166.5 1.7 constant_dynamic-update-slice_fusion.51
  168.1 1.7 constant_dynamic-update-slice_fusion.50
  169.8 1.7 constant_dynamic-update-slice_fusion.49
  171.5 1.7 constant_dynamic-update-slice_fusion.48
  173.2 1.7 constant_dynamic-update-slice_fusion.47
  174.9 1.7 constant_dynamic-update-slice_fusion.46
  182.8 15.9 %copy.145 = f32[3,65536]{0,1:T(8,128)} copy(f32[3,65536]{1,0:T(4,128)S(1)} %maximum_multiply_fusion) | data formatting | bytes 1572864 | tf_op jit(solution)/shard_map/mul | solution.py:165
  198.7 21.3 %gather_fusion = f32[4096,3]{1,0:T(8,128)S(1)} fusion(f32[3,65536]{0,1:T(8,128)} %copy.145, s32[4096]{0:T(1024)S(1)} %broadcast_clamp_fusion), kind=kCustom, calls=%fused_computation | custom fusion | bytes 114688 | tf_op jit(solution)/shard_map/gather | solution.py:169
  221.9 5.5 all-to-all-start
  228.2 5.0 all-to-all-done
  233.2 371.2 %while.36 = (s32[]{:T(128)}, f32[8,3,512]{2,0,1:T(8,128)}, f32[8,3,512]{2,0,1:T(8,128)}, f32[8,3,512]{2,1,0:T(4,128)S(1)}, f32[8,3,512]{2,0,1:T(8,128)}, /*index...) while((s32[]{:T(128)}, f32[8,3,512]{2,0,1:T(8,128)}, ...), condition=%wide.region_8.9_spmd, body=%wide.region_2.8_spmd.sunk | while | flops 798730 | bytes 1402974 | solution.py:175
  235.7 40.9 %while.37 = (s32[]{:T(128)}, f32[3,4,128]{2,0,1:T(4,128)S(1)}, s32[8,2]{0,1:T(2,128)S(1)}, f32[3,4,128]{2,0,1:T(4,128)S(1)}, f32[3,4,128]{2,0,1:T(4,128)S(1)}, /...) while((s32[]{:T(128)}, f32[3,4,128]{2,0,1:T(4,128)S(1)}, s32[8,2]{0,1:T(2,128)S(1)}, ...), condition=%wide.region_7.7_spmd, body=%wide.region_3.0_spmd.sunk | while | flops 786440 | bytes 720605 | solution.py:144
  276.7 1.4 dynamic_update_slice.28
  278.2 1.4 dynamic_update_slice.29
  282.1 40.9 %while.37 = (s32[]{:T(128)}, f32[3,4,128]{2,0,1:T(4,128)S(1)}, s32[8,2]{0,1:T(2,128)S(1)}, f32[3,4,128]{2,0,1:T(4,128)S(1)}, f32[3,4,128]{2,0,1:T(4,128)S(1)}, /...) while((s32[]{:T(128)}, f32[3,4,128]{2,0,1:T(4,128)S(1)}, s32[8,2]{0,1:T(2,128)S(1)}, ...), condition=%wide.region_7.7_spmd, body=%wide.region_3.0_spmd.sunk | while | flops 786440 | bytes 720605 | solution.py:144
  323.1 1.4 dynamic_update_slice.28
  324.6 1.4 dynamic_update_slice.29
  328.5 40.9 %while.37 = (s32[]{:T(128)}, f32[3,4,128]{2,0,1:T(4,128)S(1)}, s32[8,2]{0,1:T(2,128)S(1)}, f32[3,4,128]{2,0,1:T(4,128)S(1)}, f32[3,4,128]{2,0,1:T(4,128)S(1)}, /...) while((s32[]{:T(128)}, f32[3,4,128]{2,0,1:T(4,128)S(1)}, s32[8,2]{0,1:T(2,128)S(1)}, ...), condition=%wide.region_7.7_spmd, body=%wide.region_3.0_spmd.sunk | while | flops 786440 | bytes 720605 | solution.py:144
  369.5 1.4 dynamic_update_slice.28
  370.9 1.4 dynamic_update_slice.29
  374.9 40.9 %while.37 = (s32[]{:T(128)}, f32[3,4,128]{2,0,1:T(4,128)S(1)}, s32[8,2]{0,1:T(2,128)S(1)}, f32[3,4,128]{2,0,1:T(4,128)S(1)}, f32[3,4,128]{2,0,1:T(4,128)S(1)}, /...) while((s32[]{:T(128)}, f32[3,4,128]{2,0,1:T(4,128)S(1)}, s32[8,2]{0,1:T(2,128)S(1)}, ...), condition=%wide.region_7.7_spmd, body=%wide.region_3.0_spmd.sunk | while | flops 786440 | bytes 720605 | solution.py:144
  415.9 1.4 dynamic_update_slice.28
  417.3 1.4 dynamic_update_slice.29
  421.3 40.9 %while.37 = (s32[]{:T(128)}, f32[3,4,128]{2,0,1:T(4,128)S(1)}, s32[8,2]{0,1:T(2,128)S(1)}, f32[3,4,128]{2,0,1:T(4,128)S(1)}, f32[3,4,128]{2,0,1:T(4,128)S(1)}, /...) while((s32[]{:T(128)}, f32[3,4,128]{2,0,1:T(4,128)S(1)}, s32[8,2]{0,1:T(2,128)S(1)}, ...), condition=%wide.region_7.7_spmd, body=%wide.region_3.0_spmd.sunk | while | flops 786440 | bytes 720605 | solution.py:144
  462.3 1.4 dynamic_update_slice.28
  463.7 1.4 dynamic_update_slice.29
  467.7 40.9 %while.37 = (s32[]{:T(128)}, f32[3,4,128]{2,0,1:T(4,128)S(1)}, s32[8,2]{0,1:T(2,128)S(1)}, f32[3,4,128]{2,0,1:T(4,128)S(1)}, f32[3,4,128]{2,0,1:T(4,128)S(1)}, /...) while((s32[]{:T(128)}, f32[3,4,128]{2,0,1:T(4,128)S(1)}, s32[8,2]{0,1:T(2,128)S(1)}, ...), condition=%wide.region_7.7_spmd, body=%wide.region_3.0_spmd.sunk | while | flops 786440 | bytes 720605 | solution.py:144
  508.7 1.4 dynamic_update_slice.28
  510.1 1.4 dynamic_update_slice.29
  514.1 40.9 %while.37 = (s32[]{:T(128)}, f32[3,4,128]{2,0,1:T(4,128)S(1)}, s32[8,2]{0,1:T(2,128)S(1)}, f32[3,4,128]{2,0,1:T(4,128)S(1)}, f32[3,4,128]{2,0,1:T(4,128)S(1)}, /...) while((s32[]{:T(128)}, f32[3,4,128]{2,0,1:T(4,128)S(1)}, s32[8,2]{0,1:T(2,128)S(1)}, ...), condition=%wide.region_7.7_spmd, body=%wide.region_3.0_spmd.sunk | while | flops 786440 | bytes 720605 | solution.py:144
  555.1 1.4 dynamic_update_slice.28
  556.5 1.4 dynamic_update_slice.29
  560.5 40.9 %while.37 = (s32[]{:T(128)}, f32[3,4,128]{2,0,1:T(4,128)S(1)}, s32[8,2]{0,1:T(2,128)S(1)}, f32[3,4,128]{2,0,1:T(4,128)S(1)}, f32[3,4,128]{2,0,1:T(4,128)S(1)}, /...) while((s32[]{:T(128)}, f32[3,4,128]{2,0,1:T(4,128)S(1)}, s32[8,2]{0,1:T(2,128)S(1)}, ...), condition=%wide.region_7.7_spmd, body=%wide.region_3.0_spmd.sunk | while | flops 786440 | bytes 720605 | solution.py:144
  601.5 1.4 dynamic_update_slice.28
  605.0 3.3 all-to-all-start.1
  609.0 4.9 all-to-all-done.1
  614.6 22.1 %scatter_custom_fusion.2 = f32[65536]{0:T(1024)S(1)} fusion(s32[4096]{0:T(1024)} %bitcast.180, f32[4096]{0:T(1024)S(1)} %bitcast.185, f32[]{:T(128)} %constant.149.clone.1), kind=kCustom, calls=%fused_computation.436 | custom fusion | flops 4096 | bytes 262656 | tf_op jit(solution)/shard_map/scatter-add | solution.py:190
  636.8 22.1 %scatter_custom_fusion.1 = f32[65536]{0:T(1024)S(1)} fusion(s32[4096]{0:T(1024)} %bitcast.181, f32[4096]{0:T(1024)S(1)} %bitcast.184, f32[]{:T(128)} %constant.149.clone.1), kind=kCustom, calls=%fused_computation.438 | custom fusion | flops 4096 | bytes 262656 | tf_op jit(solution)/shard_map/scatter-add | solution.py:190
  659.0 22.1 %scatter_custom_fusion = f32[65536]{0:T(1024)S(1)} fusion(s32[4096]{0:T(1024)} %bitcast.182, f32[4096]{0:T(1024)S(1)} %bitcast.183, f32[]{:T(128)} %constant.149.clone.1), kind=kCustom, calls=%fused_computation.440 | custom fusion | flops 4096 | bytes 262656 | tf_op jit(solution)/shard_map/scatter-add | solution.py:190
  (815 shorter events, 147.2 us)
Async XLA Ops:
  3.4 3.9 copy-start.1
  12.7 4.2 copy-start.30
  17.2 30.1 %collective-permute-start = (f32[20,1,64,256]{3,2,1,0:T(8,128)S(1)}, f32[20,1,64,256]{3,2,1,0:T(8,128)S(1)}, u32[]{:S(2)}, u32[]{:S(2)}) collective-permute-start(f32[20,1,64,256]{3,2,1,0:T(8,128)S(1)} %get-tuple-element.434), channel_id=1, source_target_pairs={{0,4},{4,8},{8,12},{12,16},{16,20},{20,24},{24,28},{28,0},{1,5},{5... | collective-permute-start | bytes 3932168 | tf_op jit(solution)/shard_map/ppermute | solution.py:47
  17.7 31.1 %collective-permute-start.1 = (f32[20,1,64,256]{3,2,1,0:T(8,128)S(1)}, f32[20,1,64,256]{3,2,1,0:T(8,128)S(1)}, u32[]{:S(2)}, u32[]{:S(2)}) collective-permute-start(f32[20,1,64,256]{3,2,1,0:T(8,128)S(1)} %get-tuple-element.433), channel_id=1, source_target_pairs={{4,0},{8,4},{12,8},{16,12},{20,16},{24,20},{28,24},{0,28},{5,1},{9... | collective-permute-start | bytes 3932168 | tf_op jit(solution)/shard_map/ppermute | solution.py:49
  49.0 6.9 %collective-permute-start.2 = (f32[20,6,1,256]{3,0,2,1:T(8,128)S(1)}, f32[20,6,1,256]{3,0,2,1:T(8,128)S(1)}, u32[]{:S(2)}, u32[]{:S(2)}) collective-permute-start(f32[20,6,1,256]{3,0,2,1:T(8,128)S(1)} %copy.133), channel_id=1, source_target_pairs={{0,1},{1,2},{2,3},{4,5},{5,6},{6,7},{8,9},{9,10},{10,11},{12,13},{... | collective-permute-start | bytes 368648 | tf_op jit(solution)/shard_map/ppermute | solution.py:47
  52.5 8.2 %collective-permute-start.3 = (f32[20,6,1,256]{3,0,2,1:T(8,128)S(1)}, f32[20,6,1,256]{3,0,2,1:T(8,128)S(1)}, u32[]{:S(2)}, u32[]{:S(2)}) collective-permute-start(f32[20,6,1,256]{3,0,2,1:T(8,128)S(1)} %copy.135), channel_id=1, source_target_pairs={{1,0},{2,1},{3,2},{5,4},{6,5},{7,6},{9,8},{10,9},{11,10},{13,12},{... | collective-permute-start | bytes 368648 | tf_op jit(solution)/shard_map/ppermute | solution.py:49
  74.2 5.6 copy-start.29
  74.2 6.4 copy-start.28
  74.2 7.3 %copy-start.27 = (f32[1,4,64,256]{3,2,1,0:T(8,128)S(1)}, f32[1,4,64,256]{3,2,1,0:T(8,128)}, u32[]{:S(2)}) copy-start(f32[1,4,64,256]{3,2,1,0:T(8,128)} %get-tuple-element.361) | copy-start | bytes 786436
  76.0 6.3 copy-start.26
  77.9 5.2 copy-start.25
  79.7 4.2 copy-start.24
  80.6 4.2 copy-start.23
  81.5 4.2 copy-start.22
  82.3 4.2 copy-start.21
  83.1 4.2 copy-start.20
  84.0 4.2 copy-start.19
  84.8 4.2 copy-start.18
  85.7 4.2 copy-start.17
  86.5 4.2 copy-start.16
  87.4 4.2 copy-start.15
  88.2 4.2 copy-start.31
  90.7 7.2 %copy-start.33 = (s32[8,512]{1,0:T(8,128)S(1)}, s32[8,512]{1,0:T(8,128)}, u32[]{:S(2)}) copy-start(s32[8,512]{1,0:T(8,128)} %param.14) | copy-start | bytes 49156
  90.7 7.3 %copy-start.34 = (s32[8]{0:T(128)S(1)}, s32[8]{0:T(128)}, u32[]{:S(2)}) copy-start(s32[8]{0:T(128)} %param.15) | copy-start | bytes 100
  92.4 2.3 copy-start
  96.4 30.8 %collective-permute-start.5 = (f32[20,1,64,256]{3,2,1,0:T(8,128)}, f32[20,1,64,256]{3,2,1,0:T(8,128)S(1)}, u32[]{:S(2)}, u32[]{:S(2)}) collective-permute-start(f32[20,1,64,256]{3,2,1,0:T(8,128)} %get-tuple-element.432), channel_id=1, source_target_pairs={{4,0},{8,4},{12,8},{16,12},{20,16},{24,20},{28,24},{0,28},{5,1},{9... | collective-permute-start | bytes 3932168 | tf_op jit(solution)/shard_map/ppermute | solution.py:49
  98.0 30.1 %collective-permute-start.4 = (f32[20,1,64,256]{3,2,1,0:T(8,128)}, f32[20,1,64,256]{3,2,1,0:T(8,128)S(1)}, u32[]{:S(2)}, u32[]{:S(2)}) collective-permute-start(f32[20,1,64,256]{3,2,1,0:T(8,128)} %get-tuple-element.431), channel_id=1, source_target_pairs={{0,4},{4,8},{8,12},{12,16},{16,20},{20,24},{24,28},{28,0},{1,5},{5... | collective-permute-start | bytes 3932168 | tf_op jit(solution)/shard_map/ppermute | solution.py:47
  129.5 7.9 %collective-permute-start.7 = (f32[20,6,1,256]{3,0,2,1:T(8,128)S(1)}, f32[20,6,1,256]{3,0,2,1:T(8,128)S(1)}, u32[]{:S(2)}, u32[]{:S(2)}) collective-permute-start(f32[20,6,1,256]{3,0,2,1:T(8,128)S(1)} %copy.141), channel_id=1, source_target_pairs={{1,0},{2,1},{3,2},{5,4},{6,5},{7,6},{9,8},{10,9},{11,10},{13,12},{... | collective-permute-start | bytes 368648 | tf_op jit(solution)/shard_map/ppermute | solution.py:49
  130.9 7.2 %collective-permute-start.6 = (f32[20,6,1,256]{3,0,2,1:T(8,128)S(1)}, f32[20,6,1,256]{3,0,2,1:T(8,128)}, u32[]{:S(2)}, u32[]{:S(2)}) collective-permute-start(f32[20,6,1,256]{3,0,2,1:T(8,128)S(1)} %copy.139), channel_id=1, source_target_pairs={{0,1},{1,2},{2,3},{4,5},{5,6},{6,7},{8,9},{9,10},{10,11},{12,13},{... | collective-permute-start | bytes 368648 | tf_op jit(solution)/shard_map/ppermute | solution.py:47
  137.4 13.6 %slice-start = ((s8[5242880]{0:T(1024)(128)(4,1)}), s8[4194304]{0:T(1024)(128)(4,1)S(1)}, s32[]{:S(2)}) async-start(s8[5242880]{0:T(1024)(128)(4,1)} %bitcast.162), calls=%async_computation.2 | async-start | bytes 8388608
  139.4 11.6 %copy-start.11 = (f32[20,6,1,256]{3,2,1,0:T(1,128)}, f32[20,6,1,256]{3,2,1,0:T(1,128)S(1)}, u32[]{:S(2)}) copy-start(f32[20,6,1,256]{3,2,1,0:T(1,128)S(1)} %copy.140) | copy-start | bytes 368644
  139.5 11.6 %slice-start.1 = ((s8[5242880]{0:T(1024)(128)(4,1)}), s8[1048576]{0:T(1024)(128)(4,1)S(1)}, s32[]{:S(2)}) async-start(s8[5242880]{0:T(1024)(128)(4,1)} %bitcast.162), calls=%async_computation.3 | async-start | bytes 2097152
  159.5 17.0 %copy-start.2 = (f32[1,4,64,256]{3,2,1,0:T(8,128)S(1)}, f32[1,4,64,256]{3,2,1,0:T(8,128)}, u32[]{:S(2)}) copy-start(f32[1,4,64,256]{3,2,1,0:T(8,128)} %get-tuple-element.302) | copy-start | bytes 786436
  159.5 17.8 %copy-start.3 = (f32[1,4,64,256]{3,2,1,0:T(8,128)S(1)}, f32[1,4,64,256]{3,2,1,0:T(8,128)}, u32[]{:S(2)}) copy-start(f32[1,4,64,256]{3,2,1,0:T(8,128)} %get-tuple-element.303) | copy-start | bytes 786436
  159.5 17.8 %copy-start.4 = (f32[1,4,64,256]{3,2,1,0:T(8,128)S(1)}, f32[1,4,64,256]{3,2,1,0:T(8,128)}, u32[]{:S(2)}) copy-start(f32[1,4,64,256]{3,2,1,0:T(8,128)} %get-tuple-element.304) | copy-start | bytes 786436
  159.5 17.7 %copy-start.5 = (f32[1,4,64,256]{3,2,1,0:T(8,128)S(1)}, f32[1,4,64,256]{3,2,1,0:T(8,128)}, u32[]{:S(2)}) copy-start(f32[1,4,64,256]{3,2,1,0:T(8,128)} %get-tuple-element.305) | copy-start | bytes 786436
  159.5 17.7 %copy-start.6 = (f32[1,4,64,256]{3,2,1,0:T(8,128)S(1)}, f32[1,4,64,256]{3,2,1,0:T(8,128)}, u32[]{:S(2)}) copy-start(f32[1,4,64,256]{3,2,1,0:T(8,128)} %get-tuple-element.306) | copy-start | bytes 786436
  159.5 17.7 %copy-start.7 = (f32[1,4,64,256]{3,2,1,0:T(8,128)S(1)}, f32[1,4,64,256]{3,2,1,0:T(8,128)}, u32[]{:S(2)}) copy-start(f32[1,4,64,256]{3,2,1,0:T(8,128)} %get-tuple-element.307) | copy-start | bytes 786436
  159.6 17.7 %copy-start.8 = (f32[1,4,64,256]{3,2,1,0:T(8,128)S(1)}, f32[1,4,64,256]{3,2,1,0:T(8,128)}, u32[]{:S(2)}) copy-start(f32[1,4,64,256]{3,2,1,0:T(8,128)} %get-tuple-element.308) | copy-start | bytes 786436
  159.6 17.7 %copy-start.9 = (f32[1,4,64,256]{3,2,1,0:T(8,128)S(1)}, f32[1,4,64,256]{3,2,1,0:T(8,128)}, u32[]{:S(2)}) copy-start(f32[1,4,64,256]{3,2,1,0:T(8,128)} %get-tuple-element.309) | copy-start | bytes 786436
  159.6 17.7 %copy-start.10 = (f32[1,4,64,256]{3,2,1,0:T(8,128)S(1)}, f32[1,4,64,256]{3,2,1,0:T(8,128)}, u32[]{:S(2)}) copy-start(f32[1,4,64,256]{3,2,1,0:T(8,128)} %get-tuple-element.310) | copy-start | bytes 786436
  159.6 17.7 %copy-start.12 = (f32[1,4,64,256]{3,2,1,0:T(8,128)S(1)}, f32[1,4,64,256]{3,2,1,0:T(8,128)}, u32[]{:S(2)}) copy-start(f32[1,4,64,256]{3,2,1,0:T(8,128)} %get-tuple-element.294) | copy-start | bytes 786436
  159.6 17.7 %copy-start.13 = (f32[1,4,64,256]{3,2,1,0:T(8,128)S(1)}, f32[1,4,64,256]{3,2,1,0:T(8,128)}, u32[]{:S(2)}) copy-start(f32[1,4,64,256]{3,2,1,0:T(8,128)} %get-tuple-element.301) | copy-start | bytes 786436
  171.5 10.3 %copy-start.14 = (f32[1,4,64,256]{3,2,1,0:T(8,128)S(1)}, f32[1,4,64,256]{3,2,1,0:T(8,128)}, u32[]{:S(2)}) copy-start(f32[1,4,64,256]{3,2,1,0:T(8,128)} %get-tuple-element.293) | copy-start | bytes 786436
  182.8 50.4 %copy-start.32 = (f32[8,3,512]{2,1,0:T(4,128)S(1)}, f32[8,3,512]{2,1,0:T(4,128)}, u32[]{:S(2)}) copy-start(f32[8,3,512]{2,1,0:T(4,128)} %custom-call.11) | copy-start | bytes 147460
  221.9 11.2 %all-to-all-start = ((f32[4,2,3,512]{3,1,2,0:T(2,128)}), f32[4,2,3,512]{3,1,2,0:T(2,128)S(1)}, u32[]{:S(2)}, u32[]{:S(2)}) async-start(f32[4,2,3,512]{3,1,2,0:T(2,128)} %copy.148), calls=%async_computation | async-start | bytes 98304 | tf_op jit(solution)/shard_map/all_to_all | solution.py:172
  605.0 8.9 %all-to-all-start.1 = ((f32[4,2,3,512]{3,1,2,0:T(2,128)}), f32[4,2,3,512]{3,1,2,0:T(2,128)S(1)}, u32[]{:S(2)}, u32[]{:S(2)}) async-start(f32[4,2,3,512]{3,1,2,0:T(2,128)} %copy.154), calls=%async_computation.1 | async-start | bytes 98304 | tf_op jit(solution)/shard_map/all_to_all | solution.py:178
where the time goes:
time: 688 us; the launch traced here: 682 us
  loops' own time  247 us (36%)
  other arithmetic  179 us (26%)
  local copies, waits for them, and re-layouts  157 us (23%)
  waiting for transfers between devices  73.4 us (11%)
  starting transfers between devices  25.1 us (4%)
    another operation x8, loops' own time, pair_forces(): total, unused = lax.scan(one_pair, start, (pair_list, noise))  246 us
    scatter-add x3, other arithmetic, per_device(): jax.ops.segment_sum(back[:, comp, :].reshape(-1), flat_ids, num_segments=...  66.4 us
    slice x64, local copies, waits for them, and re-layouts, one_pair(): pos_b = lax.dynamic_index_in_dim(pos_tiles, pair[1], 1, keepdims=False)  37.1 us
    unnamed x40, other arithmetic  36.8 us
    ppermute x4, waiting for transfers between devices, padded_2(): lax.ppermute(head, axis, [((i + 1) % count, i) for i in range(ends)])  33.4 us
    ppermute x4, waiting for transfers between devices, padded_2(): lax.ppermute(tail, axis, [(i, (i + 1) % count) for i in range(ends)])  30.1 us
    unnamed x96, local copies, waits for them, and re-layouts  25.9 us
    dynamic_update_slice x32, local copies, waits for them, and re-layouts, per_device(): lax.map(patch_step, (positions, velocities, received, pair_tiles, pair_no...  23.2 us
  transfers between devices with their start and end apart: 10, of which 9 were waited for; matrix products, arithmetic and copies ran while one was open for 1% of the time, Pallas kernels for 0%

commit v1 on v0

v1 whole, which is shorter than its diff:
```python
import functools

import jax
import jax.numpy as jnp
from jax import lax
from jax.experimental import pallas as pl
from jax.experimental.pallas import tpu as pltpu
from jax.sharding import PartitionSpec as P

DIRS = [
    (0, 0, 0),
    (1, 0, 0),
    (-1, 0, 0),
    (0, 1, 0),
    (0, -1, 0),
    (0, 0, 1),
    (0, 0, -1),
    (1, 1, 0),
    (-1, -1, 0),
    (1, -1, 0),
    (-1, 1, 0),
    (1, 0, 1),
    (-1, 0, -1),
    (1, 0, -1),
    (-1, 0, 1),
    (0, 1, 1),
    (0, -1, -1),
    (0, 1, -1),
    (0, -1, 1),
]
OPP = [0, 2, 1, 4, 3, 6, 5, 8, 7, 10, 9, 12, 11, 14, 13, 16, 15, 18, 17]
CX_PLUS = [k for k in range(19) if DIRS[k][0] == 1]
CX_MINUS = [k for k in range(19) if DIRS[k][0] == -1]
CY_PLUS = [k for k in range(19) if DIRS[k][1] == 1]
CY_MINUS = [k for k in range(19) if DIRS[k][1] == -1]
F32 = jnp.float32
BF16 = jnp.bfloat16
I32 = jnp.int32
VMEM_SPEC = pl.BlockSpec(memory_space=pltpu.VMEM)
SMEM_SPEC = pl.BlockSpec(memory_space=pltpu.SMEM)
ANY_SPEC = pl.BlockSpec(memory_space=pl.ANY)

ROWS = 64
PAD = 88
TILES = ROWS // 8


def params(mib=48):
    return pltpu.CompilerParams(vmem_limit_bytes=mib * 1024 * 1024)


def cost(flops, bytes_accessed):
    return pl.CostEstimate(flops=flops, bytes_accessed=bytes_accessed, transcendentals=0)


def velocity_of(f):
    diff = [None] + [f[k] - f[k + 1] for k in range(1, 19, 2)]
    rho = f[0]
    for k in range(1, 19):
        rho = rho + f[k]
    m1, m3, m5, m7, m9, m11, m13, m15, m17 = diff[1:]
    jx = m1 + m7 + m9 + m11 + m13
    jy = m3 + m7 - m9 + m15 + m17
    jz = m5 + m11 - m13 + m15 - m17
    inv = 1.0 / rho
    return rho, jx * inv, jy * inv, jz * inv


def collide(f):
    rho, ux, uy, uz = velocity_of(f)
    base = (1.25 * rho) * (1.0 - 1.5 * (ux * ux + uy * uy + uz * uz))
    ux, uy, uz = 1.5 * ux, 1.5 * uy, 1.5 * uz
    even1, even2 = base * (1.0 / 18.0), base * (1.0 / 36.0)
    odd1, odd2 = rho * (2.5 / 18.0), rho * (2.5 / 36.0)
    out = [None] * 19
    out[0] = base * (1.0 / 3.0) - 0.25 * f[0]
    for k in range(1, 19, 2):
        dx, dy, dz = DIRS[k]
        proj = None
        for sign, comp in ((dx, ux), (dy, uy), (dz, uz)):
            if sign == 0:
                continue
            if proj is None:
                proj = comp
            else:
                proj = proj + comp if sign > 0 else proj - comp
        even, odd = (even1, odd1) if k < 7 else (even2, odd2)
        odd = odd * proj
        even = even + odd * proj
        out[k] = (even + odd) - 0.25 * f[k]
        out[k + 1] = (even - odd) - 0.25 * f[k + 1]
    return out


def shifted(read, tile, dy, dz):
    here = read(tile)
    if dy != 0:
        sub = lax.broadcasted_iota(I32, here.shape, 0)
        if dy > 0:
            here = pltpu.roll(jnp.where(sub == 7, read(tile - 1), here), 1, 0)
        else:
            here = pltpu.roll(jnp.where(sub == 0, read(tile + 1), here), 7, 0)
    if dz != 0:
        here = pltpu.roll(here, 1 if dz > 0 else here.shape[1] - 1, 1)
    return here


def rows_of(tile):
    return pl.ds(pl.multiple_of(8 + 8 * tile, 8), 8)


def open_bits(read_mask, tile):
    bits = None
    cache = {}
    for k in range(1, 19):
        dx, dy, dz = DIRS[k]
        if (dx, dy) not in cache:
            cache[(dx, dy)] = shifted(functools.partial(read_mask, dx), tile, dy, 0)
        m = cache[(dx, dy)]
        if dz != 0:
            lane = lax.broadcasted_iota(I32, m.shape, 1)
            last = m.shape[1] - 1
            m = pltpu.roll(m, 1 if dz > 0 else last, 1)
            m = jnp.where(lane == (0 if dz > 0 else last), 0, m)
        m = m << k
        bits = m if bits is None else bits | m
    return bits


def stream(read, own, bits, tile):
    out = [own[0]]
    for k in range(1, 19):
        dx, dy, dz = DIRS[k]
        source = shifted(functools.partial(read, k, dx), tile, dy, dz)
        out.append(jnp.where((bits & (1 << k)) != 0, source, own[OPP[k]]))
    return out


def collide_kernel(n, per, pop, mask, vel, post, fwd, bwd, up, down, *others):
    x = pl.program_id(0)
    last = pl.num_programs(0) - 1

    def body(t, carry):
        rows = pl.ds(pl.multiple_of(8 * t, 8), 8)
        out = collide([pop[k, 0, rows, :] for k in range(19)])
        for k in range(19):
            post[k, 0, rows, :] = out[k]
        return carry

    lax.fori_loop(0, TILES, body, 0)
    for ref, near, beyond, dirs in ((up, ROWS - 1, ROWS - 2, CY_PLUS), (down, 0, 1, CY_MINUS)):
        for k in range(19):
            ref[x, k : k + 1, :] = post[k, 0, near : near + 1, :]
        for j, k in enumerate(dirs):
            ref[x, 19 + j : 20 + j, :] = post[k, 0, beyond : beyond + 1, :]
        ref[x, 24:25, :] = mask[0, near : near + 1, :].astype(F32)
        ref[x, 25:26, :] = mask[0, beyond : beyond + 1, :].astype(F32)

    def faces(ref, dirs):
        for j, k in enumerate(dirs):
            ref[j * ROWS : (j + 1) * ROWS, :] = post[k, 0]
        ref[5 * ROWS : 6 * ROWS, :] = mask[0].astype(F32)

    @pl.when(x == last)
    def _():
        faces(fwd, CX_PLUS)

    @pl.when(x == 0)
    def _():
        faces(bwd, CX_MINUS)
        me = lax.axis_index("xs")
        for d in range(1, n):
            target = lax.rem(me + d, n)
            for r in range(per):
                rows = vel[target * per + r]
                for c in range(3):
                    for half in range(2):
                        i = (r * 3 + c) * 2 + half
                        piece = rows[c : c + 1, half * 256 : (half + 1) * 256]
                        if d in (1, n - 1):
                            ref = up if d == 1 else down
                            ref[i // 3, 26 + i % 3 : 27 + i % 3, :] = piece
                        else:
                            others[d - 2][i : i + 1, :] = piece


def sent_velocity(refs, n, d, r, c):
    out = []
    for half in range(2):
        i = (r * 3 + c) * 2 + half
        if d in (1, n - 1):
            out.append(refs[d - 1][i // 3, 26 + i % 3 : 27 + i % 3, :])
        else:
            out.append(refs[d - 1][i : i + 1, :])
    return jnp.concatenate(out, axis=1)


def border_flags(n):
    me = lax.axis_index("xs")
    return (me > 0).astype(F32), (me < n - 1).astype(F32)


def edges_kernel(n, nx, fwd_in, bwd_in, below, above, fwd, bwd, rows, sems):
    has_below, has_above = border_flags(n)
    for i, (x, dirs, far_below, far_above) in enumerate(
        ((nx - 1, CX_PLUS, 7, 9), (0, CX_MINUS, 10, 8))
    ):
        for j, k in enumerate(dirs):
            rows[i, j : j + 1, :] = below[x, k : k + 1, :]
            rows[i, 8 + j : 9 + j, :] = above[x, k : k + 1, :]
        j = 19 + CY_PLUS.index(far_below)
        rows[i, 5:6, :] = below[x, j : j + 1, :]
        j = 19 + CY_MINUS.index(far_above)
        rows[i, 13:14, :] = above[x, j : j + 1, :]
        rows[i, 6:8, :] = below[x, 24:26, :] * has_below
        rows[i, 14:16, :] = above[x, 24:26, :] * has_above
    copies = [
        pltpu.make_async_copy(rows.at[i], ref.at[pl.ds(6 * ROWS, 16)], sems.at[i])
        for i, ref in enumerate((fwd, bwd))
    ]
    for copy in copies:
        copy.start()
    for copy in copies:
        copy.wait()


def fill_edges(pad, below, above, layers):
    for x, dirs in layers:
        for k in dirs:
            pad[k, x, 79:80, :] = below[x, k : k + 1, :]
            pad[k, x, 72:73, :] = above[x, k : k + 1, :]
            if k in CY_PLUS:
                j = 19 + CY_PLUS.index(k)
                pad[k, x, 7:8, :] = below[x, k : k + 1, :]
                pad[k, x, 78:79, :] = below[x, j : j + 1, :]
            if k in CY_MINUS:
                j = 19 + CY_MINUS.index(k)
                pad[k, x, 73:74, :] = above[x, j : j + 1, :]
                pad[k, x, 80:81, :] = pad[k, x, 8:9, :]


def fill_mask(n, nx, pad, mask, below, above):
    has_below, has_above = border_flags(n)
    for x in range(nx):
        pad[x, 8:72, :] = mask[x]
        near = (below[x, 24:25, :] * has_below).astype(I32)
        pad[x, 79:80, :] = near
        pad[x, 7:8, :] = near
        pad[x, 78:79, :] = (below[x, 25:26, :] * has_below).astype(I32)
        pad[x, 72:73, :] = (above[x, 24:25, :] * has_above).astype(I32)
        pad[x, 73:74, :] = (above[x, 25:26, :] * has_above).astype(I32)
        pad[x, 80:81, :] = mask[x, 0:1, :]


def run_copies(copies):
    for copy in copies:
        copy.start()
    for copy in copies:
        copy.wait()


def middle_kernel(n, nx, post, mask, below, above, post2, bits_out, pad, flags, sems):
    run_copies(
        [
            pltpu.make_async_copy(post.at[:, x], pad.at[:, x, pl.ds(8, ROWS)], sems.at[x])
            for x in range(nx)
        ]
    )
    fill_edges(pad, below, above, [(x, range(19)) for x in range(nx)])
    fill_mask(n, nx, flags, mask, below, above)
    for x in range(1, nx - 1):

        def body(t, carry, x=x):
            bits = open_bits(lambda dx, tile: flags[x - dx, rows_of(tile), :], t)
            own = [pad[k, x, rows_of(t), :] for k in range(19)]
            f = stream(lambda k, dx, tile: pad[k, x - dx, rows_of(tile), :], own, bits, t)
            out = collide(f)
            for k in range(19):
                post2[k, x - 1, rows_of(t), :] = out[k]
            bits_out[x - 1, pl.ds(pl.multiple_of(8 * t, 8), 8), :] = bits
            return carry

        lax.fori_loop(0, TILES + 1, body, 0)
        for k in CY_PLUS:
            post2[k, x - 1, 7:8, :] = post2[k, x - 1, 79:80, :]


def outer_kernel(
    n, nx, post, mask, below, above, before, after, post2, bits_out, fwd2, bwd2, pad, halo, flags, halo_flags, edge, sems
):
    last = nx - 1
    copies = []

    def add(src, dst):
        copies.append(pltpu.make_async_copy(src, dst, sems.at[len(copies)]))

    body_rows = pl.ds(8, ROWS)
    add(post.at[:, 0], pad.at[:, 0, body_rows])
    add(post.at[:, last], pad.at[:, last, body_rows])
    for x, dirs in ((1, CX_MINUS), (last - 1, CX_PLUS)):
        for k in dirs:
            add(post.at[k, x], pad.at[k, x, body_rows])
    for i, ref in enumerate((before, after)):
        for j in range(5):
            add(ref.at[pl.ds(j * ROWS, ROWS)], halo.at[i, j, body_rows])
        add(ref.at[pl.ds(5 * ROWS, ROWS)], halo_flags.at[i, body_rows])
        add(ref.at[pl.ds(6 * ROWS, 16)], edge.at[i])
    run_copies(copies)
    fill_edges(
        pad, below, above, [(0, range(19)), (last, range(19)), (1, CX_MINUS), (last - 1, CX_PLUS)]
    )
    fill_mask(n, nx, flags, mask, below, above)
    for i, (dirs, far_below, far_above) in enumerate(((CX_PLUS, 7, 9), (CX_MINUS, 10, 8))):
        for j, k in enumerate(dirs):
            halo[i, j, 79:80, :] = edge[i, j : j + 1, :]
            halo[i, j, 72:73, :] = edge[i, 8 + j : 9 + j, :]
            if k == far_below:
                halo[i, j, 7:8, :] = edge[i, j : j + 1, :]
                halo[i, j, 78:79, :] = edge[i, 5:6, :]
            if k == far_above:
                halo[i, j, 73:74, :] = edge[i, 13:14, :]
                halo[i, j, 80:81, :] = halo[i, j, 8:9, :]
        halo_flags[i, 79:80, :] = edge[i, 6:7, :]
        halo_flags[i, 7:8, :] = edge[i, 6:7, :]
        halo_flags[i, 78:79, :] = edge[i, 7:8, :]
        halo_flags[i, 72:73, :] = edge[i, 14:15, :]
        halo_flags[i, 73:74, :] = edge[i, 15:16, :]
        halo_flags[i, 80:81, :] = halo_flags[i, 8:9, :]
    for i, x in enumerate((0, last)):

        def read(k, dx, tile, i=i, x=x):
            if x - dx < 0:
                return halo[0, CX_PLUS.index(k), rows_of(tile), :]
            if x - dx > last:
                return halo[1, CX_MINUS.index(k), rows_of(tile), :]
            return pad[k, x - dx, rows_of(tile), :]

        def read_mask(dx, tile, i=i, x=x):
            if x - dx < 0 or x - dx > last:
                return halo_flags[0 if x - dx < 0 else 1, rows_of(tile), :].astype(I32)
            return flags[x - dx, rows_of(tile), :]

        def body(t, carry, i=i, x=x, read=read, read_mask=read_mask):
            bits = open_bits(read_mask, t)
            own = [pad[k, x, rows_of(t), :] for k in range(19)]
            out = collide(stream(read, own, bits, t))
            for k in range(19):
                post2[k, i, rows_of(t), :] = out[k]
            bits_out[i, pl.ds(pl.multiple_of(8 * t, 8), 8), :] = bits
            return carry

        lax.fori_loop(0, TILES + 1, body, 0)
        for k in CY_PLUS:
            post2[k, i, 7:8, :] = post2[k, i, 79:80, :]
    for i, ref, dirs, k_below, k_above in ((1, fwd2, CX_PLUS, 7, 9), (0, bwd2, CX_MINUS, 10, 8)):
        for j, k in enumerate(dirs):
            ref[j * ROWS : (j + 1) * ROWS, :] = post2[k, i, 8:72, :]
        ref[320:321, :] = post2[k_below, i, 79:80, :]
        ref[321:322, :] = post2[k_above, i, 72:73, :]


def store_flow(flow, i, t, f):
    rho, ux, uy, uz = velocity_of(f)
    rows = pl.ds(pl.multiple_of(8 * t, 8), 8)
    flow[0, i, rows, :] = ux
    flow[1, i, rows, :] = uy
    flow[2, i, rows, :] = uz


def final_middle_kernel(nx, post2, outer, bits, out, flow, halo, result, sems):
    copies = [
        pltpu.make_async_copy(outer.at[k, i], halo.at[i, j], sems.at[i * 5 + j])
        for i, dirs in ((0, CX_PLUS), (1, CX_MINUS))
        for j, k in enumerate(dirs)
    ]
    run_copies(copies)
    stores = []
    for x in range(1, nx - 1):

        def read(k, dx, tile, x=x):
            if x - dx == 0:
                return halo[0, CX_PLUS.index(k), rows_of(tile), :]
            if x - dx == nx - 1:
                return halo[1, CX_MINUS.index(k), rows_of(tile), :]
            return post2[k, x - dx - 1, rows_of(tile), :]

        def body(t, carry, x=x, read=read):
            rows = pl.ds(pl.multiple_of(8 * t, 8), 8)
            own = [post2[k, x - 1, rows_of(t), :] for k in range(19)]
            f = stream(read, own, bits[x - 1, rows, :], t)
            for k in range(19):
                result[k, x - 1, rows, :] = f[k]
            store_flow(flow, x - 1, t, f)
            return carry

        lax.fori_loop(0, TILES, body, 0)
        copy = pltpu.make_async_copy(result.at[:, x - 1], out.at[:, x], sems.at[10 + x])
        copy.start()
        stores.append(copy)
    for copy in stores:
        copy.wait()


def final_outer_kernel(nx, out_in, post2, middle, bits, before, after, out, flow, halo, near, result, sems):
    last = nx - 1
    copies = []

    def add(src, dst):
        copies.append(pltpu.make_async_copy(src, dst, sems.at[len(copies)]))

    for i, ref in enumerate((before, after)):
        for j in range(5):
            add(ref.at[pl.ds(j * ROWS, ROWS)], halo.at[i, j, pl.ds(8, ROWS)])
        add(ref.at[pl.ds(5 * ROWS, 8)], halo.at[i, 5, pl.ds(8, 8)])
    for i, (x, dirs) in enumerate(((1, CX_MINUS), (last - 1, CX_PLUS))):
        for j, k in enumerate(dirs):
            add(middle.at[k, x - 1], near.at[i, j])
    run_copies(copies)
    for i, (dirs, k_below, k_above) in enumerate(((CX_PLUS, 7, 9), (CX_MINUS, 10, 8))):
        halo[i, dirs.index(k_below), 7:8, :] = halo[i, 5, 8:9, :]
        halo[i, dirs.index(k_above), 72:73, :] = halo[i, 5, 9:10, :]
    stores = []
    for i, x in enumerate((0, last)):

        def read(k, dx, tile, i=i, x=x):
            if x - dx < 0:
                return halo[0, CX_PLUS.index(k), rows_of(tile), :]
            if x - dx > last:
                return halo[1, CX_MINUS.index(k), rows_of(tile), :]
            if dx == 0:
                return post2[k, i, rows_of(tile), :]
            dirs = CX_MINUS if x == 0 else CX_PLUS
            return near[i, dirs.index(k), rows_of(tile), :]

        def body(t, carry, i=i, x=x, read=read):
            rows = pl.ds(pl.multiple_of(8 * t, 8), 8)
            own = [post2[k, i, rows_of(t), :] for k in range(19)]
            f = stream(read, own, bits[i, rows, :], t)
            for k in range(19):
                result[k, i, rows, :] = f[k]
            store_flow(flow, i, t, f)
            return carry

        lax.fori_loop(0, TILES, body, 0)
        copy = pltpu.make_async_copy(result.at[:, i], out.at[:, x], sems.at[len(copies) + i])
        copy.start()
        stores.append(copy)
    for copy in stores:
        copy.wait()


def pair_kernel(pair_tiles, pos, vel, noise, base, rows, cols, acc):
    g = pl.program_id(0)
    tile = noise.shape[-1]
    count = pos.shape[-1] // tile
    pairs = noise.shape[1]
    x, v = pos[0], vel[0]
    both = jnp.concatenate([x, 4.5 * v, jnp.zeros((2, x.shape[1]), F32)], axis=0)
    turned = both.T
    for c in range(6):
        for j in range(count):
            part = turned[j * tile : (j + 1) * tile, c : c + 1]
            cols[c, j] = jnp.broadcast_to(part, (tile, tile))
            rows[c, j] = jnp.broadcast_to(both[c : c + 1, j * tile : (j + 1) * tile], (8, tile))
    acc[...] = jnp.zeros_like(acc)
    eye = lax.broadcasted_iota(I32, (tile, tile), 0) == lax.broadcasted_iota(I32, (tile, tile), 1)
    scale = jnp.where(eye, 15.0, 0.0).astype(BF16)

    def one_pair(p, carry):
        first = pair_tiles[g, p, 0]
        second = pair_tiles[g, p, 1]
        theta = lax.dot_general(
            scale, noise[0, p], (((1,), (1,)), ((), ())), preferred_element_type=F32
        )
        mine = [rows[c, first] for c in range(6)]
        total = [acc[first, c] for c in range(3)]
        for s in range(tile // 8):
            part = slice(8 * s, 8 * s + 8)
            dx, dy, dz = [mine[c] - cols[c, second, part, :] for c in range(3)]
            vx, vy, vz = [mine[c] - cols[c, second, part, :] for c in range(3, 6)]
            square = (dx * dx + 0.01) + (dy * dy + dz * dz)
            close = jnp.maximum(lax.rsqrt(square) - 1.0, 0.0)
            along = dx * vx + dy * vy + dz * vz
            force = close * ((theta[part, :] + 25.0) - close * along)
            total = [total[0] + force * dx, total[1] + force * dy, total[2] + force * dz]
        for c in range(3):
            acc[first, c] = total[c]
        return carry

    lax.fori_loop(0, pairs, one_pair, 0)
    for j in range(count):
        lanes = slice(j * tile, (j + 1) * tile)
        for c in range(3):
            force = jnp.sum(acc[j, c], axis=0, keepdims=True)
            base[0, c : c + 1, lanes] = 0.5 * v[c : c + 1, lanes] + 0.04 * force


def split(value):
    high = value.astype(BF16)
    return high, (value - high.astype(F32)).astype(BF16)


def ranks(owner, count):
    out = []
    for g in range(count):
        rank = jnp.int32(0)
        for h in range(g):
            rank = rank + (owner[h] == owner[g]).astype(I32)
        out.append(rank)
    return out


def one_hot(index, extent):
    want = index.astype(F32).astype(BF16)
    place = lax.broadcasted_iota(I32, (extent, index.shape[1]), 0).astype(F32).astype(BF16)
    return place == want


def scatter_kernel(n, per, owner, voxel, vel, *refs):
    sent, out, table = refs[: n - 1], refs[n - 1], refs[n]
    me = lax.axis_index("xs")
    beads = voxel.shape[1]
    for r in range(per):
        table[me, r, 0:3, :] = vel[me * per + r]
        for d in range(1, n):
            source = lax.rem(me + n - d, n)
            for c in range(3):
                table[source, r, c : c + 1, :] = sent_velocity(sent, n, d, r, c)
    out[...] = jnp.zeros_like(out)
    rank = ranks(owner, voxel.shape[0])
    one, zero = BF16(1), BF16(0)
    for g in range(voxel.shape[0]):
        index = voxel[g : g + 1, :]
        lanes = jnp.where(one_hot(index & 255, 256), one, zero)
        at_row = one_hot(index >> 8, out.shape[1])
        values = table[owner[g], rank[g]]
        lanes2 = jnp.concatenate([lanes, lanes], axis=1)
        for c in range(3):
            high, low = split(values[c : c + 1, :])
            left = jnp.concatenate(
                [jnp.where(at_row, high, zero), jnp.where(at_row, low, zero)], axis=1
            )
            out[c] += lax.dot_general(
                left, lanes2, (((1,), (1,)), ((), ())), preferred_element_type=F32
            )
        out[3] += lax.dot_general(
            jnp.where(at_row, one, zero), lanes, (((1,), (1,)), ((), ())), preferred_element_type=F32
        )


def gather_kernel(n, per, owner, voxel, middle, outer, *refs):
    outs, table, field = refs[:n], refs[n], refs[n + 1]
    me = lax.axis_index("xs")
    patches = voxel.shape[0]
    inner = middle.shape[1]
    rows = (inner + 2) * ROWS
    for c in range(3):
        layers = [outer[c, 0]] + [middle[c, i] for i in range(inner)] + [outer[c, 1]]
        for x, layer in enumerate(layers):
            high, low = split(layer)
            field[c, x * ROWS : (x + 1) * ROWS, 0:256] = high
            field[c, x * ROWS : (x + 1) * ROWS, 256:512] = low
    one, zero = BF16(1), BF16(0)
    for g in range(patches):
        index = voxel[g : g + 1, :]
        lanes = jnp.where(one_hot(index & 255, 256), one, zero)
        lanes2 = jnp.concatenate([lanes, lanes], axis=0)
        at_row = lax.broadcasted_iota(I32, (rows, index.shape[1]), 0) == (index >> 8)
        for c in range(3):
            found = lax.dot_general(
                field[c], lanes2, (((1,), (0,)), ((), ())), preferred_element_type=F32
            )
            table[g, c : c + 1, :] = jnp.sum(jnp.where(at_row, found, 0.0), axis=0, keepdims=True)
    rank = ranks(owner, patches)
    for d in range(n):
        target = lax.rem(me + d, n)
        for r in range(per):
            found = jnp.int32(0)
            for g in range(patches):
                found = jnp.where((owner[g] == target) & (rank[g] == r), g, found)
            outs[d][r] = table[found, 0:3, :]


def field_kernel(total, middle, outer, field):
    nx = field.shape[1]
    for x in range(nx):
        rows = slice(x * ROWS, (x + 1) * ROWS)
        number = 10.0 * total[3, rows, :]
        for c in range(3):
            if x == 0 or x == nx - 1:
                speed = outer[c, 0 if x == 0 else 1]
            else:
                speed = middle[c, x - 1]
            field[c, x] = 0.5 * total[c, rows, :] - number * speed


def final_kernel(n, per, pos, base, *refs):
    flows, new_pos, new_vel = refs[:n], refs[n], refs[n + 1]
    me = lax.axis_index("xs")
    for d in range(n):
        source = lax.rem(me + n - d, n)
        for r in range(per):
            i = source * per + r
            speed = base[i] + 10.0 * flows[d][r]
            new_vel[i] = speed
            new_pos[i] = pos[i] + 0.04 * speed


def shift(value, axis, by):
    n = lax.axis_size(axis)
    return lax.ppermute(value, axis, [(i, (i + by) % n) for i in range(n)])


def per_device(
    populations, fluid_mask, patch_voxel, patch_owner, positions, velocities, pair_tiles, pair_noise
):
    n = lax.axis_size("xs")
    patches, beads = patch_voxel.shape
    per = patches // n
    nx = populations.shape[1]
    lanes = populations.shape[3]
    sds = jax.ShapeDtypeStruct
    vmem, dma = pltpu.VMEM, pltpu.SemaphoreType.DMA

    layer = lambda x: (0, x, 0, 0)
    whole2 = lambda x: (0, 0)
    whole3 = lambda x: (0, 0, 0)
    post, fwd, bwd, *sending = pl.pallas_call(
        functools.partial(collide_kernel, n, per),
        grid=(nx,),
        in_specs=[
            pl.BlockSpec((19, 1, ROWS, lanes), layer),
            pl.BlockSpec((1, ROWS, lanes), lambda x: (x, 0, 0)),
            pl.BlockSpec((patches, 3, beads), whole3),
        ],
        out_specs=[
            pl.BlockSpec((19, 1, ROWS, lanes), layer),
            pl.BlockSpec((400, lanes), whole2),
            pl.BlockSpec((400, lanes), whole2),
            pl.BlockSpec((nx, 32, lanes), whole3),
            pl.BlockSpec((nx, 32, lanes), whole3),
        ]
        + [pl.BlockSpec((16, lanes), whole2)] * (n - 3),
        out_shape=[
            sds(populations.shape, F32),
            sds((400, lanes), F32),
            sds((400, lanes), F32),
            sds((nx, 32, lanes), F32),
            sds((nx, 32, lanes), F32),
        ]
        + [sds((16, lanes), F32)] * (n - 3),
        compiler_params=params(),
        cost_estimate=cost(12_000_000, 11_000_000),
        name="collide_first",
    )(populations, fluid_mask, velocities)
    up, down, *others = sending
    below = shift(up, "xs", 1)
    above = shift(down, "xs", -1)
    sent = [below] + [shift(other, "xs", d + 2) for d, other in enumerate(others)] + [above]

    base = pl.pallas_call(
        pair_kernel,
        grid_spec=pltpu.PrefetchScalarGridSpec(
            num_scalar_prefetch=1,
            grid=(patches,),
            in_specs=[
                pl.BlockSpec((1, 3, beads), lambda g, s: (g, 0, 0)),
                pl.BlockSpec((1, 3, beads), lambda g, s: (g, 0, 0)),
                pl.BlockSpec((1,) + pair_noise.shape[1:], lambda g, s: (g, 0, 0, 0)),
            ],
            out_specs=pl.BlockSpec((1, 3, beads), lambda g, s: (g, 0, 0)),
            scratch_shapes=[
                vmem((6, beads // 128, 8, 128), F32),
                vmem((6, beads // 128, 128, 128), F32),
                vmem((beads // 128, 3, 8, 128), F32),
            ],
        ),
        out_shape=sds(positions.shape, F32),
        compiler_params=params(),
        cost_estimate=cost(30_000_000, 2_500_000),
        name="pair_forces",
    )(pair_tiles, positions, velocities, pair_noise)

    fwd, bwd = pl.pallas_call(
        functools.partial(edges_kernel, n, nx),
        in_specs=[ANY_SPEC, ANY_SPEC, VMEM_SPEC, VMEM_SPEC],
        out_specs=[ANY_SPEC, ANY_SPEC],
        out_shape=[sds(fwd.shape, F32), sds(bwd.shape, F32)],
        input_output_aliases={0: 0, 1: 1},
        scratch_shapes=[vmem((2, 16, lanes), F32), dma((2,))],
        compiler_params=params(),
        cost_estimate=cost(1000, 100_000),
        name="face_edges",
    )(fwd, bwd, below, above)
    before = shift(fwd, "ax", 1)
    after = shift(bwd, "ax", -1)

    total = pl.pallas_call(
        functools.partial(scatter_kernel, n, per),
        in_specs=[SMEM_SPEC] + [VMEM_SPEC] * (n + 1),
        out_specs=VMEM_SPEC,
        out_shape=sds((4, nx * ROWS, lanes), F32),
        scratch_shapes=[vmem((n, per, 8, beads), F32)],
        compiler_params=params(),
        cost_estimate=cost(3_000_000_000, 1_500_000),
        name="bead_sums",
    )(patch_owner, patch_voxel, velocities, *sent)

    inner = nx - 2
    post2, bits = pl.pallas_call(
        functools.partial(middle_kernel, n, nx),
        in_specs=[ANY_SPEC, VMEM_SPEC, VMEM_SPEC, VMEM_SPEC],
        out_specs=[VMEM_SPEC, VMEM_SPEC],
        out_shape=[sds((19, inner, PAD, lanes), F32), sds((inner, 72, lanes), I32)],
        scratch_shapes=[
            vmem((19, nx, PAD, lanes), F32),
            vmem((nx, PAD, lanes), I32),
            dma((nx,)),
        ],
        compiler_params=params(),
        cost_estimate=cost(12_000_000, 9_000_000),
        name="middle_layers",
    )(post, fluid_mask, below, above)

    post2_outer, bits_outer, fwd2, bwd2 = pl.pallas_call(
        functools.partial(outer_kernel, n, nx),
        in_specs=[ANY_SPEC, VMEM_SPEC, VMEM_SPEC, VMEM_SPEC, ANY_SPEC, ANY_SPEC],
        out_specs=[VMEM_SPEC] * 4,
        out_shape=[
            sds((19, 2, PAD, lanes), F32),
            sds((2, 72, lanes), I32),
            sds((328, lanes), F32),
            sds((328, lanes), F32),
        ],
        scratch_shapes=[
            vmem((19, nx, PAD, lanes), F32),
            vmem((2, 5, PAD, lanes), F32),
            vmem((nx, PAD, lanes), I32),
            vmem((2, PAD, lanes), F32),
            vmem((2, 16, lanes), F32),
            dma((26,)),
        ],
        compiler_params=params(),
        cost_estimate=cost(12_000_000, 9_000_000),
        name="outer_layers",
    )(post, fluid_mask, below, above, before, after)
    before2 = shift(fwd2, "ax", 1)
    after2 = shift(bwd2, "ax", -1)

    out, flow = pl.pallas_call(
        functools.partial(final_middle_kernel, nx),
        in_specs=[VMEM_SPEC, ANY_SPEC, VMEM_SPEC],
        out_specs=[ANY_SPEC, VMEM_SPEC],
        out_shape=[sds(populations.shape, F32), sds((3, inner, ROWS, lanes), F32)],
        scratch_shapes=[
            vmem((2, 5, PAD, lanes), F32),
            vmem((19, inner, ROWS, lanes), F32),
            dma((10 + nx,)),
        ],
        compiler_params=params(),
        cost_estimate=cost(6_000_000, 7_000_000),
        name="final_middle",
    )(post2, post2_outer, bits)

    out, flow_outer = pl.pallas_call(
        functools.partial(final_outer_kernel, nx),
        in_specs=[ANY_SPEC, VMEM_SPEC, ANY_SPEC, VMEM_SPEC, ANY_SPEC, ANY_SPEC],
        out_specs=[ANY_SPEC, VMEM_SPEC],
        out_shape=[sds(populations.shape, F32), sds((3, 2, ROWS, lanes), F32)],
        input_output_aliases={0: 0},
        scratch_shapes=[
            vmem((2, 6, PAD, lanes), F32),
            vmem((2, 5, PAD, lanes), F32),
            vmem((19, 2, ROWS, lanes), F32),
            dma((24,)),
        ],
        compiler_params=params(),
        cost_estimate=cost(6_000_000, 7_000_000),
        name="final_outer",
    )(out, post2_outer, post2, bits_outer, before2, after2)

    flows = pl.pallas_call(
        functools.partial(gather_kernel, n, per),
        in_specs=[SMEM_SPEC] + [VMEM_SPEC] * 3,
        out_specs=[VMEM_SPEC] * n,
        out_shape=[sds((per, 3, beads), F32)] * n,
        scratch_shapes=[
            vmem((patches, 8, beads), F32),
            vmem((3, nx * ROWS, 2 * lanes), BF16),
        ],
        compiler_params=params(),
        cost_estimate=cost(3_000_000_000, 1_500_000),
        name="bead_flow",
    )(patch_owner, patch_voxel, flow, flow_outer)
    flows = [flows[0]] + [shift(flows[d], "xs", d) for d in range(1, n)]

    field = pl.pallas_call(
        field_kernel,
        in_specs=[VMEM_SPEC] * 3,
        out_specs=VMEM_SPEC,
        out_shape=sds((3, nx, ROWS, lanes), F32),
        compiler_params=params(),
        cost_estimate=cost(400_000, 2_500_000),
        name="drag_field",
    )(total, flow, flow_outer)

    new_pos, new_vel = pl.pallas_call(
        functools.partial(final_kernel, n, per),
        in_specs=[VMEM_SPEC] * (n + 2),
        out_specs=[VMEM_SPEC] * 2,
        out_shape=[sds(positions.shape, F32)] * 2,
        compiler_params=params(),
        cost_estimate=cost(50_000, 300_000),
        name="bead_update",
    )(positions, base, *flows)
    return out, new_pos, new_vel, field


def solution(mesh):
    return jax.shard_map(
        per_device,
        mesh=mesh,
        in_specs=(
            P(None, "ax", "xs", None),
            P("ax", "xs", None),
            P(("ax", "xs"), None),
            P(("ax", "xs")),
            P(("ax", "xs"), None, None),
            P(("ax", "xs"), None, None),
            P(("ax", "xs"), None, None),
            P(("ax", "xs"), None, None, None),
        ),
        out_specs=(
            P(None, "ax", "xs", None),
            P(("ax", "xs"), None, None),
            P(("ax", "xs"), None, None),
            P(None, "ax", "xs", None),
        ),
        check_vma=False,
    )
```

time: 688 us -> 90.8 us (0.13)
  loops' own time: 247 us -> 0 us
  other arithmetic: 179 us -> 0 us
  local copies, waits for them, and re-layouts: 157 us -> 4.96 us
  waiting for transfers between devices: 73.4 us -> 13.8 us
  Pallas kernels: 0 us -> 54.3 us
  starting transfers between devices: 25.1 us -> 16.5 us
    another operation x9 -> x0, loops' own time: 247 us -> none  [the longest x8 246 us: pair_forces(): total, unused = lax.scan(one_pair, start, (pair_list, noise))]
    scatter-add x3 -> x0, other arithmetic: 66.4 us -> none  [per_device(): jax.ops.segment_sum(back[:, comp, :].reshape(-1), flat_ids, num_segments=...]
    pallas_call x0 -> x11, Pallas kernels: none -> 54.3 us  [the longest x1 17.3 us: per_device(): pl.pallas_call(pair_kernel, grid_spec=pltpu.PrefetchScalarGridSpec(num_sc...]
    ppermute x8 -> x10, waiting for transfers between devices: 63.5 us -> 13.8 us  [shift(): return lax.ppermute(value, axis, [(i, (i + by) % n) for i in range(n)])]
    slice x71 -> x0, local copies, waits for them, and re-layouts: 39.1 us -> none  [the longest x64 37.1 us: one_pair(): pos_b = lax.dynamic_index_in_dim(pos_tiles, pair[1], 1, keepdims=False)]
    unnamed x40 -> x0, other arithmetic: 36.8 us -> none
    reduce_sum x193 -> x0, other arithmetic: 35.4 us -> none  [the longest x64 14.5 us: one_pair(): force = jnp.sum(scalar[None] * unit, axis=2)]
    dynamic_update_slice x32 -> x0, local copies, waits for them, and re-layouts: 23.2 us -> none  [per_device(): lax.map(patch_step, (positions, velocities, received, pair_tiles, pair_no...]
  transfers between devices with their start and end apart: 10 -> 10, of which waited for: 9 -> 3; matrix products, arithmetic and copies ran while one was open for 1% -> 0% of each run, Pallas kernels for 0% -> 47%
where the time goes in v1:
time: 90.8 us; the launch traced here: 90.4 us
  Pallas kernels  54.3 us (60%)
  starting transfers between devices  16.5 us (18%)
  waiting for transfers between devices  13.8 us (15%)
  local copies, waits for them, and re-layouts  4.96 us (5%)
    pallas_call x1, Pallas kernels, per_device(): pl.pallas_call(pair_kernel, grid_spec=pltpu.PrefetchScalarGridSpec(num_sc...  17.3 us
    ppermute x10, starting transfers between devices, shift(): return lax.ppermute(value, axis, [(i, (i + by) % n) for i in range(n)])  16.5 us
    ppermute x10, waiting for transfers between devices, shift(): return lax.ppermute(value, axis, [(i, (i + by) % n) for i in range(n)])  13.8 us
    pallas_call x1, Pallas kernels, per_device(): pl.pallas_call(functools.partial(collide_kernel, n, per), grid=(nx,), in_...  6.25 us
    pallas_call x1, Pallas kernels, per_device(): pl.pallas_call(functools.partial(middle_kernel, n, nx), in_specs=[ANY_SPE...  5.75 us
    pallas_call x1, Pallas kernels, per_device(): pl.pallas_call(functools.partial(outer_kernel, n, nx), in_specs=[ANY_SPEC...  5.18 us
    pallas_call x1, Pallas kernels, per_device(): pl.pallas_call(functools.partial(final_outer_kernel, nx), in_specs=[ANY_S...  4.98 us
    unnamed x25, local copies, waits for them, and re-layouts  4.96 us
  transfers between devices with their start and end apart: 10, of which 3 were waited for; matrix products, arithmetic and copies ran while one was open for 0% of the time, Pallas kernels for 47%

profile of v1, /device:TPU:0, one launch (start us, length us, event | category | flops | bytes accessed | tf_op | source)
XLA Modules:
  0.0 90.4 jit_solution(17458280057018430260)
XLA Ops:
  0.6 0.8 copy.15.vel
  1.5 0.0 copy-start.3
  1.5 0.9 %copy-done.3 = s32[4,64,256]{2,1,0:T(8,128)S(1)} copy-done((s32[4,64,256]{2,1,0:T(8,128)S(1)}, s32[4,64,256]{2,1,0:T(8,128)}, u32[]{:S(2)}) %copy-start.3) | copy-done | bytes 262168
  2.4 0.0 copy-start.4
  2.4 6.2 %collide_first.1 = (f32[19,4,64,256]{3,2,1,0:T(8,128)}, f32[400,256]{1,0:T(8,128)S(1)}, f32[400,256]{1,0:T(8,128)S(1)}, f32[4,32,256]{2,1,0:T(8,128)S(1)}, f32[4...) custom-call(f32[19,4,64,256]{3,2,1,0:T(8,128)} %pop.1, s32[4,64,256]{2,1,0:T(8,128)S(1)} %copy-done.3, f32[8,3,512]{2,1,0:T(4,128)S(1)} %copy.15.vel), custom_call_target="tpu_custom_call" | custom-call | flops 12000000 | bytes 11000000 | tf_op jit(solution)/shard_map/collide_first/pallas_call | solution.py:628
  8.7 0.0 copy-start.8
  8.7 0.0 copy-start.9
  8.7 3.0 %collective-permute-start = (f32[4,32,256]{2,1,0:T(8,128)S(1)}, f32[4,32,256]{2,1,0:T(8,128)S(1)}, u32[]{:S(2)}, u32[]{:S(2)}) collective-permute-start(f32[4,32,256]{2,1,0:T(8,128)S(1)} %get-tuple-element.29), channel_id=1, source_target_pairs={{0,1},{1,2},{2,3},{3,0},{4,5},{5,6},{6,7},{7,4},{8,9},{9,10},{10,1... | collective-permute-start | bytes 393224 | tf_op jit(solution)/shard_map/ppermute | solution.py:611
  11.7 2.1 %collective-permute-start.1 = (f32[4,32,256]{2,1,0:T(8,128)S(1)}, f32[4,32,256]{2,1,0:T(8,128)S(1)}, u32[]{:S(2)}, u32[]{:S(2)}) collective-permute-start(f32[4,32,256]{2,1,0:T(8,128)S(1)} %get-tuple-element.30), channel_id=1, source_target_pairs={{0,3},{1,0},{2,1},{3,2},{4,7},{5,4},{6,5},{7,6},{8,11},{9,8},{10,9... | collective-permute-start | bytes 393224 | tf_op jit(solution)/shard_map/ppermute | solution.py:611
  13.8 4.3 %collective-permute-done.below.refs_0_ = f32[4,32,256]{2,1,0:T(8,128)S(1)} collective-permute-done((f32[4,32,256]{2,1,0:T(8,128)S(1)}, f32[4,32,256]{2,1,0:T(8,128)S(1)}, u32[]{:S(2)}, u32[]{:S(2)}) %collective-permute-start) | collective-permute-done | bytes 131104 | tf_op jit(solution)/shard_map/ppermute | solution.py:611
  18.1 1.4 %collective-permute-done.1.above.refs_2_ = f32[4,32,256]{2,1,0:T(8,128)S(1)} collective-permute-done((f32[4,32,256]{2,1,0:T(8,128)S(1)}, f32[4,32,256]{2,1,0:T(8,128)S(1)}, u32[]{:S(2)}, u32[]{:S(2)}) %collective-permute-start.1) | collective-permute-done | bytes 131104 | tf_op jit(solution)/shard_map/ppermute | solution.py:611
  19.5 0.1 face_edges.1
  19.6 0.1 collective-permute-start.2
  19.6 2.6 %collective-permute-start.3 = (f32[400,256]{1,0:T(8,128)S(1)}, f32[400,256]{1,0:T(8,128)S(1)}, u32[]{:S(2)}, u32[]{:S(2)}) collective-permute-start(f32[400,256]{1,0:T(8,128)S(1)} %get-tuple-element.35), channel_id=1, source_target_pairs={{0,28},{4,0},{8,4},{12,8},{16,12},{20,16},{24,20},{28,24},{1,29},{... | collective-permute-start | bytes 1228808 | tf_op jit(solution)/shard_map/ppermute | solution.py:611
  22.3 8.1 %collective-permute-done.2.before = f32[400,256]{1,0:T(8,128)S(1)} collective-permute-done((f32[400,256]{1,0:T(8,128)S(1)}, f32[400,256]{1,0:T(8,128)S(1)}, u32[]{:S(2)}, u32[]{:S(2)}) %collective-permute-start.2) | collective-permute-done | bytes 409632 | tf_op jit(solution)/shard_map/ppermute | solution.py:611
  30.4 0.0 collective-permute-done.3.after
  30.4 0.0 copy-done.4
  30.4 5.2 %outer_layers.1 = (f32[19,2,88,256]{3,2,1,0:T(8,128)S(1)}, s32[2,72,256]{2,1,0:T(8,128)S(1)}, f32[328,256]{1,0:T(8,128)S(1)}, f32[328,256]{1,0:T(8,128)S(1)}) custom-call(f32[19,4,64,256]{3,2,1,0:T(8,128)} %get-tuple-element.28.post, s32[4,64,256]{2,1,0:T(8,128)S(1)} %copy-done.4, f32[4,32,256]{2,1,0:T(8,128)S(1)} %collective-permute-done.below.refs_0_, ...), custom_call_target="tpu_custom_call" | custom-call | flops 12000000 | bytes 9000000 | tf_op jit(solution)/shard_map/outer_layers/pallas_call | solution.py:725
  35.6 0.0 copy-start
  35.6 1.7 %copy-done = f32[19,2,88,256]{3,2,1,0:T(8,128)} copy-done((f32[19,2,88,256]{3,2,1,0:T(8,128)}, f32[19,2,88,256]{3,2,1,0:T(8,128)S(1)}, u32[]{:S(2)}) %copy-start) | copy-done | bytes 3424280
  37.3 1.8 %collective-permute-start.4 = (f32[328,256]{1,0:T(8,128)S(1)}, f32[328,256]{1,0:T(8,128)S(1)}, u32[]{:S(2)}, u32[]{:S(2)}) collective-permute-start(f32[328,256]{1,0:T(8,128)S(1)} %get-tuple-element.40), channel_id=1, source_target_pairs={{0,4},{4,8},{8,12},{12,16},{16,20},{20,24},{24,28},{28,0},{1,5},{5... | collective-permute-start | bytes 1007624 | tf_op jit(solution)/shard_map/ppermute | solution.py:611
  39.1 1.0 %collective-permute-start.5 = (f32[328,256]{1,0:T(8,128)S(1)}, f32[328,256]{1,0:T(8,128)S(1)}, u32[]{:S(2)}, u32[]{:S(2)}) collective-permute-start(f32[328,256]{1,0:T(8,128)S(1)} %get-tuple-element.41), channel_id=1, source_target_pairs={{0,28},{4,0},{8,4},{12,8},{16,12},{20,16},{24,20},{28,24},{1,29},{... | collective-permute-start | bytes 1007624 | tf_op jit(solution)/shard_map/ppermute | solution.py:611
  40.1 1.3 %collective-permute-start.9 = (f32[16,256]{1,0:T(8,128)S(1)}, f32[16,256]{1,0:T(8,128)S(1)}, u32[]{:S(2)}, u32[]{:S(2)}) collective-permute-start(f32[16,256]{1,0:T(8,128)S(1)} %get-tuple-element.51), channel_id=1, source_target_pairs={{0,2},{1,3},{2,0},{3,1},{4,6},{5,7},{6,4},{7,5},{8,10},{9,11},{10,... | collective-permute-start | bytes 49160 | tf_op jit(solution)/shard_map/ppermute | solution.py:611
  41.4 0.0 copy-done.8
  41.4 0.0 copy-done.9
  41.5 0.1 copy.16.pair_tiles
  41.6 0.0 copy-start.1
  41.6 5.8 %middle_layers.1 = (f32[19,2,88,256]{3,2,1,0:T(8,128)S(1)}, s32[2,72,256]{2,1,0:T(8,128)S(1)}) custom-call(f32[19,4,64,256]{3,2,1,0:T(8,128)} %get-tuple-element.28.post, s32[4,64,256]{2,1,0:T(8,128)S(1)} %copy-done.4, f32[4,32,256]{2,1,0:T(8,128)S(1)} %collective-permute-done.below.refs_0_, f32[4,32,256]{2,1,0:T(8,128)S(1)} %collective-permute-done.1.above.refs_2_), custom_call_target="tpu_custom_call" | custom-call | flops 12000000 | bytes 9000000 | tf_op jit(solution)/shard_map/middle_layers/pallas_call | solution.py:710
  47.3 0.0 copy-start.2
  47.3 4.9 %final_middle.1 = (f32[19,4,64,256]{3,2,1,0:T(8,128)}, f32[3,2,64,256]{3,2,1,0:T(8,128)S(1)}) custom-call(f32[19,2,88,256]{3,2,1,0:T(8,128)S(1)} %get-tuple-element.31.post2.middle, f32[19,2,88,256]{3,2,1,0:T(8,128)} %copy-done, s32[2,72,256]{2,1,0:T(8,128)S(1)} %get-tuple-element.37.bits), custom_call_target="tpu_custom_call" | custom-call | flops 6000000 | bytes 7000000 | tf_op jit(solution)/shard_map/final_middle/pallas_call | solution.py:750
  52.3 0.0 collective-permute-done.4.before
  52.3 0.0 collective-permute-done.5.after
  52.3 0.0 copy-done.2
  52.3 0.0 copy-done.1
  52.3 0.0 copy-start.6
  52.3 0.0 copy-start.7
  52.3 5.0 %final_outer.1 = (f32[19,4,64,256]{3,2,1,0:T(8,128)}, f32[3,2,64,256]{3,2,1,0:T(8,128)S(1)}) custom-call(f32[19,4,64,256]{3,2,1,0:T(8,128)} %get-tuple-element.38.out_in, f32[19,2,88,256]{3,2,1,0:T(8,128)S(1)} %copy-done.1, f32[19,2,88,256]{3,2,1,0:T(8,128)} %copy-done.2, s32[2,72,256]{2,1,0:T(8,128)S(1)} %get-tuple-element.39.bits, ...), custom_call_target="tpu_custom_call", output_to_operand_aliasing={{0}: (0, {})} | custom-call | flops 6000000 | bytes 7000000 | tf_op jit(solution)/shard_map/final_outer/pallas_call | solution.py:765
  57.3 0.0 copy-done.6
  57.3 0.0 copy-done.7
  57.4 4.3 %bead_flow.1 = (f32[2,3,512]{2,1,0:T(4,128)S(1)}, f32[2,3,512]{2,1,0:T(4,128)S(1)}, f32[2,3,512]{2,1,0:T(4,128)S(1)}, f32[2,3,512]{2,1,0:T(4,128)S(1)}) custom-call(s32[8]{0:T(128)S(1)} %copy-done.7, s32[8,512]{1,0:T(8,128)S(1)} %copy-done.6, f32[3,2,64,256]{3,2,1,0:T(8,128)S(1)} %get-tuple-element.43.middle, f32[3,2,64,256]{3,2,1,0:T(8,128)S(1)} %get-tuple-element.44.outer), custom_call_target="tpu_custom_call" | custom-call | flops 3000000000 | bytes 1500000 | tf_op jit(solution)/shard_map/bead_flow/pallas_call | solution.py:782
  61.7 1.6 %collective-permute-start.6 = (f32[2,3,512]{2,1,0:T(4,128)S(1)}, f32[2,3,512]{2,1,0:T(4,128)S(1)}, u32[]{:S(2)}, u32[]{:S(2)}) collective-permute-start(f32[2,3,512]{2,1,0:T(4,128)S(1)} %get-tuple-element.46), channel_id=1, source_target_pairs={{0,1},{1,2},{2,3},{3,0},{4,5},{5,6},{6,7},{7,4},{8,9},{9,10},{10,1... | collective-permute-start | bytes 36872 | tf_op jit(solution)/shard_map/ppermute | solution.py:611
  63.3 1.2 %collective-permute-start.7 = (f32[2,3,512]{2,1,0:T(4,128)S(1)}, f32[2,3,512]{2,1,0:T(4,128)S(1)}, u32[]{:S(2)}, u32[]{:S(2)}) collective-permute-start(f32[2,3,512]{2,1,0:T(4,128)S(1)} %get-tuple-element.47), channel_id=1, source_target_pairs={{0,2},{1,3},{2,0},{3,1},{4,6},{5,7},{6,4},{7,5},{8,10},{9,11},{10,... | collective-permute-start | bytes 36872 | tf_op jit(solution)/shard_map/ppermute | solution.py:611
  64.5 0.0 copy-start.5
  64.5 1.8 %collective-permute-start.8 = (f32[2,3,512]{2,1,0:T(4,128)S(1)}, f32[2,3,512]{2,1,0:T(4,128)S(1)}, u32[]{:S(2)}, u32[]{:S(2)}) collective-permute-start(f32[2,3,512]{2,1,0:T(4,128)S(1)} %get-tuple-element.48), channel_id=1, source_target_pairs={{0,3},{1,0},{2,1},{3,2},{4,7},{5,4},{6,5},{7,6},{8,11},{9,8},{10,9... | collective-permute-start | bytes 36872 | tf_op jit(solution)/shard_map/ppermute | solution.py:611
  66.3 0.0 collective-permute-done.9.refs_1_
  66.3 4.5 %bead_sums.1.total = f32[4,256,256]{2,1,0:T(8,128)S(1)} custom-call(s32[8]{0:T(128)S(1)} %copy-done.7, s32[8,512]{1,0:T(8,128)S(1)} %copy-done.6, f32[8,3,512]{2,1,0:T(4,128)S(1)} %copy.15.vel, f32[4,32,256]{2,1,0:T(8,128)S(1)} %collective-permute-done.below.refs_0_, f32[16,256]{1,0:T(8,128)S(1)} %collective-permute-done.9.refs_1_, ...), custom_call_target="tpu_custom_call" | custom-call | flops 3000000000 | bytes 1500000 | tf_op jit(solution)/shard_map/bead_sums/pallas_call | solution.py:698
  70.8 0.0 copy-done.5
  70.8 17.3 %pair_forces.1.base = f32[8,3,512]{2,1,0:T(4,128)S(1)} custom-call(s32[8,8,2]{2,1,0:T(8,128)S(1)} %copy.16.pair_tiles, f32[8,3,512]{2,1,0:T(4,128)S(1)} %copy.19.pos, f32[8,3,512]{2,1,0:T(4,128)S(1)} %copy.15.vel, bf16[8,8,128,128]{3,2,1,0:T(8,128)(2,1)S(1)} %copy-done.5), custom_call_target="tpu_custom_call" | custom-call | flops 30000000 | bytes 2500000 | tf_op jit(solution)/shard_map/pair_forces/pallas_call | solution.py:661
  88.1 1.0 %drag_field.1 = f32[3,4,64,256]{3,2,1,0:T(8,128)} custom-call(f32[4,256,256]{2,1,0:T(8,128)S(1)} %bead_sums.1.total, f32[3,2,64,256]{3,2,1,0:T(8,128)S(1)} %get-tuple-element.43.middle, f32[3,2,64,256]{3,2,1,0:T(8,128)S(1)} %get-tuple-element.44.outer), custom_call_target="tpu_custom_call" | custom-call | flops 400000 | bytes 2500000 | tf_op jit(solution)/shard_map/drag_field/pallas_call | solution.py:797
  89.1 0.0 collective-permute-done.6.refs_1_
  89.1 0.0 collective-permute-done.7.refs_2_
  89.1 0.0 collective-permute-done.8.refs_3_
  89.1 0.6 copy.21
  89.8 0.6 copy.22
  (2 shorter events, 0.1 us)
Async XLA Ops:
  1.5 1.0 %copy-start.3 = (s32[4,64,256]{2,1,0:T(8,128)S(1)}, s32[4,64,256]{2,1,0:T(8,128)}, u32[]{:S(2)}) copy-start(s32[4,64,256]{2,1,0:T(8,128)} %mask.5) | copy-start | bytes 786436
  2.4 28.0 %copy-start.4 = (s32[4,64,256]{2,1,0:T(8,128)S(1)}, s32[4,64,256]{2,1,0:T(8,128)}, u32[]{:S(2)}) copy-start(s32[4,64,256]{2,1,0:T(8,128)} %mask.5) | copy-start | bytes 786436
  8.7 32.7 %copy-start.8 = (f32[8,3,512]{2,0,1:T(8,128)S(1)}, f32[8,3,512]{2,0,1:T(8,128)}, u32[]{:S(2)}) copy-start(f32[8,3,512]{2,0,1:T(8,128)} %param.12) | copy-start | bytes 147460
  8.7 32.8 %copy-start.9 = (s32[8,8,2]{1,2,0:T(2,128)S(1)}, s32[8,8,2]{1,2,0:T(2,128)}, u32[]{:S(2)}) copy-start(s32[8,8,2]{1,2,0:T(2,128)} %param.14) | copy-start | bytes 1540
  8.7 9.4 %collective-permute-start = (f32[4,32,256]{2,1,0:T(8,128)S(1)}, f32[4,32,256]{2,1,0:T(8,128)S(1)}, u32[]{:S(2)}, u32[]{:S(2)}) collective-permute-start(f32[4,32,256]{2,1,0:T(8,128)S(1)} %get-tuple-element.29), channel_id=1, source_target_pairs={{0,1},{1,2},{2,3},{3,0},{4,5},{5,6},{6,7},{7,4},{8,9},{9,10},{10,1... | collective-permute-start | bytes 393224 | tf_op jit(solution)/shard_map/ppermute | solution.py:611
  11.7 7.8 %collective-permute-start.1 = (f32[4,32,256]{2,1,0:T(8,128)S(1)}, f32[4,32,256]{2,1,0:T(8,128)S(1)}, u32[]{:S(2)}, u32[]{:S(2)}) collective-permute-start(f32[4,32,256]{2,1,0:T(8,128)S(1)} %get-tuple-element.30), channel_id=1, source_target_pairs={{0,3},{1,0},{2,1},{3,2},{4,7},{5,4},{6,5},{7,6},{8,11},{9,8},{10,9... | collective-permute-start | bytes 393224 | tf_op jit(solution)/shard_map/ppermute | solution.py:611
  19.6 10.8 %collective-permute-start.2 = (f32[400,256]{1,0:T(8,128)S(1)}, f32[400,256]{1,0:T(8,128)S(1)}, u32[]{:S(2)}, u32[]{:S(2)}) collective-permute-start(f32[400,256]{1,0:T(8,128)S(1)} %get-tuple-element.34), channel_id=1, source_target_pairs={{0,4},{4,8},{8,12},{12,16},{16,20},{20,24},{24,28},{28,0},{1,5},{5... | collective-permute-start | bytes 1228808 | tf_op jit(solution)/shard_map/ppermute | solution.py:611
  19.6 10.8 %collective-permute-start.3 = (f32[400,256]{1,0:T(8,128)S(1)}, f32[400,256]{1,0:T(8,128)S(1)}, u32[]{:S(2)}, u32[]{:S(2)}) collective-permute-start(f32[400,256]{1,0:T(8,128)S(1)} %get-tuple-element.35), channel_id=1, source_target_pairs={{0,28},{4,0},{8,4},{12,8},{16,12},{20,16},{24,20},{28,24},{1,29},{... | collective-permute-start | bytes 1228808 | tf_op jit(solution)/shard_map/ppermute | solution.py:611
  35.6 1.7 %copy-start = (f32[19,2,88,256]{3,2,1,0:T(8,128)}, f32[19,2,88,256]{3,2,1,0:T(8,128)S(1)}, u32[]{:S(2)}) copy-start(f32[19,2,88,256]{3,2,1,0:T(8,128)S(1)} %get-tuple-element.36.outer.post2) | copy-start | bytes 10272772
  37.3 15.0 %collective-permute-start.4 = (f32[328,256]{1,0:T(8,128)S(1)}, f32[328,256]{1,0:T(8,128)S(1)}, u32[]{:S(2)}, u32[]{:S(2)}) collective-permute-start(f32[328,256]{1,0:T(8,128)S(1)} %get-tuple-element.40), channel_id=1, source_target_pairs={{0,4},{4,8},{8,12},{12,16},{16,20},{20,24},{24,28},{28,0},{1,5},{5... | collective-permute-start | bytes 1007624 | tf_op jit(solution)/shard_map/ppermute | solution.py:611
  39.1 13.2 %collective-permute-start.5 = (f32[328,256]{1,0:T(8,128)S(1)}, f32[328,256]{1,0:T(8,128)S(1)}, u32[]{:S(2)}, u32[]{:S(2)}) collective-permute-start(f32[328,256]{1,0:T(8,128)S(1)} %get-tuple-element.41), channel_id=1, source_target_pairs={{0,28},{4,0},{8,4},{12,8},{16,12},{20,16},{24,20},{28,24},{1,29},{... | collective-permute-start | bytes 1007624 | tf_op jit(solution)/shard_map/ppermute | solution.py:611
  40.1 26.2 %collective-permute-start.9 = (f32[16,256]{1,0:T(8,128)S(1)}, f32[16,256]{1,0:T(8,128)S(1)}, u32[]{:S(2)}, u32[]{:S(2)}) collective-permute-start(f32[16,256]{1,0:T(8,128)S(1)} %get-tuple-element.51), channel_id=1, source_target_pairs={{0,2},{1,3},{2,0},{3,1},{4,6},{5,7},{6,4},{7,5},{8,10},{9,11},{10,... | collective-permute-start | bytes 49160 | tf_op jit(solution)/shard_map/ppermute | solution.py:611
  41.6 10.7 %copy-start.1 = (f32[19,2,88,256]{3,2,1,0:T(8,128)S(1)}, f32[19,2,88,256]{3,2,1,0:T(8,128)}, u32[]{:S(2)}) copy-start(f32[19,2,88,256]{3,2,1,0:T(8,128)} %copy-done) | copy-start | bytes 10272772
  47.3 5.0 %copy-start.2 = (f32[19,2,88,256]{3,2,1,0:T(8,128)}, f32[19,2,88,256]{3,2,1,0:T(8,128)S(1)}, u32[]{:S(2)}) copy-start(f32[19,2,88,256]{3,2,1,0:T(8,128)S(1)} %get-tuple-element.31.post2.middle) | copy-start | bytes 10272772
  52.3 5.0 %copy-start.6 = (s32[8,512]{1,0:T(8,128)S(1)}, s32[8,512]{1,0:T(8,128)}, u32[]{:S(2)}) copy-start(s32[8,512]{1,0:T(8,128)} %voxel.3) | copy-start | bytes 49156
  52.3 5.0 %copy-start.7 = (s32[8]{0:T(128)S(1)}, s32[8]{0:T(128)}, u32[]{:S(2)}) copy-start(s32[8]{0:T(128)} %owner.3) | copy-start | bytes 100
  61.7 27.4 %collective-permute-start.6 = (f32[2,3,512]{2,1,0:T(4,128)S(1)}, f32[2,3,512]{2,1,0:T(4,128)S(1)}, u32[]{:S(2)}, u32[]{:S(2)}) collective-permute-start(f32[2,3,512]{2,1,0:T(4,128)S(1)} %get-tuple-element.46), channel_id=1, source_target_pairs={{0,1},{1,2},{2,3},{3,0},{4,5},{5,6},{6,7},{7,4},{8,9},{9,10},{10,1... | collective-permute-start | bytes 36872 | tf_op jit(solution)/shard_map/ppermute | solution.py:611
  63.3 25.8 %collective-permute-start.7 = (f32[2,3,512]{2,1,0:T(4,128)S(1)}, f32[2,3,512]{2,1,0:T(4,128)S(1)}, u32[]{:S(2)}, u32[]{:S(2)}) collective-permute-start(f32[2,3,512]{2,1,0:T(4,128)S(1)} %get-tuple-element.47), channel_id=1, source_target_pairs={{0,2},{1,3},{2,0},{3,1},{4,6},{5,7},{6,4},{7,5},{8,10},{9,11},{10,... | collective-permute-start | bytes 36872 | tf_op jit(solution)/shard_map/ppermute | solution.py:611
  64.5 6.3 %copy-start.5 = (bf16[8,8,128,128]{3,2,1,0:T(8,128)(2,1)S(1)}, bf16[8,8,128,128]{3,2,1,0:T(8,128)(2,1)}, u32[]{:S(2)}) copy-start(bf16[8,8,128,128]{3,2,1,0:T(8,128)(2,1)} %noise.1) | copy-start | bytes 6291460
  64.5 24.6 %collective-permute-start.8 = (f32[2,3,512]{2,1,0:T(4,128)S(1)}, f32[2,3,512]{2,1,0:T(4,128)S(1)}, u32[]{:S(2)}, u32[]{:S(2)}) collective-permute-start(f32[2,3,512]{2,1,0:T(4,128)S(1)} %get-tuple-element.48), channel_id=1, source_target_pairs={{0,3},{1,0},{2,1},{3,2},{4,7},{5,4},{6,5},{7,6},{8,11},{9,8},{10,9... | collective-permute-start | bytes 36872 | tf_op jit(solution)/shard_map/ppermute | solution.py:611

commit v2 on v0

v2 whole, which is shorter than its diff:
```python
import functools

import jax
import jax.numpy as jnp
from jax import lax
from jax.experimental import pallas as pl
from jax.experimental.pallas import tpu as pltpu
from jax.sharding import PartitionSpec as P

DIRS = [
    (0, 0, 0),
    (1, 0, 0),
    (-1, 0, 0),
    (0, 1, 0),
    (0, -1, 0),
    (0, 0, 1),
    (0, 0, -1),
    (1, 1, 0),
    (-1, -1, 0),
    (1, -1, 0),
    (-1, 1, 0),
    (1, 0, 1),
    (-1, 0, -1),
    (1, 0, -1),
    (-1, 0, 1),
    (0, 1, 1),
    (0, -1, -1),
    (0, 1, -1),
    (0, -1, 1),
]
OPP = [0, 2, 1, 4, 3, 6, 5, 8, 7, 10, 9, 12, 11, 14, 13, 16, 15, 18, 17]
CX_PLUS = [k for k in range(19) if DIRS[k][0] == 1]
CX_MINUS = [k for k in range(19) if DIRS[k][0] == -1]
CY_PLUS = [k for k in range(19) if DIRS[k][1] == 1]
CY_MINUS = [k for k in range(19) if DIRS[k][1] == -1]
F32 = jnp.float32
BF16 = jnp.bfloat16
I32 = jnp.int32
VMEM_SPEC = pl.BlockSpec(memory_space=pltpu.VMEM)
SMEM_SPEC = pl.BlockSpec(memory_space=pltpu.SMEM)
ANY_SPEC = pl.BlockSpec(memory_space=pl.ANY)
HBM_SPEC = pl.BlockSpec(memory_space=pltpu.HBM)

ROWS = 64
PAD = 88
TILES = ROWS // 8


def params(mib=16):
    return pltpu.CompilerParams(vmem_limit_bytes=mib * 1024 * 1024)


def cost(flops, bytes_accessed):
    return pl.CostEstimate(flops=flops, bytes_accessed=bytes_accessed, transcendentals=0)


def call(kernel, ins, out_shape, name, estimate, after=(), specs=None, **kwargs):
    specs = specs or {}
    count, extra = len(ins), len(after)

    def body(*refs):
        kernel(*refs[:count], *refs[count + extra :])

    return pl.pallas_call(
        body,
        in_specs=[specs.get(i, VMEM_SPEC) for i in range(count)] + [ANY_SPEC] * extra,
        out_shape=out_shape,
        cost_estimate=estimate,
        name=name,
        **{"compiler_params": params(), **kwargs},
    )(*ins, *after)


def tree(values):
    while len(values) > 1:
        values = [
            values[i] + values[i + 1] if i + 1 < len(values) else values[i]
            for i in range(0, len(values), 2)
        ]
    return values[0]


def velocity_of(f):
    diff = [None] + [f[k] - f[k + 1] for k in range(1, 19, 2)]
    rho = tree([f[k] for k in range(1, 19)] + [f[0]])
    m1, m3, m5, m7, m9, m11, m13, m15, m17 = diff[1:]
    jx = m1 + ((m7 + m9) + (m11 + m13))
    jy = m3 + ((m7 - m9) + (m15 + m17))
    jz = m5 + ((m11 - m13) + (m15 - m17))
    inv = 1.0 / rho
    return rho, jx * inv, jy * inv, jz * inv


def collide(f):
    rho, ux, uy, uz = velocity_of(f)
    base = (1.25 * rho) * (1.0 - 1.5 * (ux * ux + uy * uy + uz * uz))
    ux, uy, uz = 1.5 * ux, 1.5 * uy, 1.5 * uz
    even1, even2 = base * (1.0 / 18.0), base * (1.0 / 36.0)
    odd1, odd2 = rho * (2.5 / 18.0), rho * (2.5 / 36.0)
    out = [None] * 19
    out[0] = base * (1.0 / 3.0) - 0.25 * f[0]
    for k in range(1, 19, 2):
        dx, dy, dz = DIRS[k]
        proj = None
        for sign, comp in ((dx, ux), (dy, uy), (dz, uz)):
            if sign == 0:
                continue
            if proj is None:
                proj = comp
            else:
                proj = proj + comp if sign > 0 else proj - comp
        even, odd = (even1, odd1) if k < 7 else (even2, odd2)
        odd = odd * proj
        even = even + odd * proj
        out[k] = (even + odd) - 0.25 * f[k]
        out[k + 1] = (even - odd) - 0.25 * f[k + 1]
    return out


def shifted(read, tile, dy, dz):
    here = read(tile)
    if dy != 0:
        sub = lax.broadcasted_iota(I32, here.shape, 0)
        if dy > 0:
            here = pltpu.roll(jnp.where(sub == 7, read(tile - 1), here), 1, 0)
        else:
            here = pltpu.roll(jnp.where(sub == 0, read(tile + 1), here), 7, 0)
    if dz != 0:
        here = pltpu.roll(here, 1 if dz > 0 else here.shape[1] - 1, 1)
    return here


def rows_of(tile):
    return pl.ds(pl.multiple_of(8 + 8 * tile, 8), 8)


def open_bits(read_mask, tile):
    bits = None
    cache = {}
    for k in range(1, 19):
        dx, dy, dz = DIRS[k]
        if (dx, dy) not in cache:
            cache[(dx, dy)] = shifted(functools.partial(read_mask, dx), tile, dy, 0)
        m = cache[(dx, dy)]
        if dz != 0:
            lane = lax.broadcasted_iota(I32, m.shape, 1)
            last = m.shape[1] - 1
            m = pltpu.roll(m, 1 if dz > 0 else last, 1)
            m = jnp.where(lane == (0 if dz > 0 else last), 0, m)
        m = m << k
        bits = m if bits is None else bits | m
    return bits


def stream(read, own, bits, tile):
    out = [own[0]]
    for k in range(1, 19):
        dx, dy, dz = DIRS[k]
        source = shifted(functools.partial(read, k, dx), tile, dy, dz)
        out.append(jnp.where((bits & (1 << k)) != 0, source, own[OPP[k]]))
    return out


def tile_rows(t):
    return pl.ds(pl.multiple_of(8 * t, 8), 8)


def collide_kernel(n, per, nx, pop, mask, vel, post, fwd, bwd, up, down, *rest):
    others, (here, flags, sems) = rest[: n - 3], rest[n - 3 :]
    copies = [pltpu.make_async_copy(pop.at[:, x], here.at[x], sems.at[x]) for x in range(nx)]
    copies.append(pltpu.make_async_copy(mask, flags, sems.at[nx]))
    for copy in copies:
        copy.start()
    me = lax.axis_index("xs")
    for d in range(1, n):
        target = lax.rem(me + d, n)
        for r in range(per):
            for c in range(3):
                row = vel[c, pl.ds(target * per + r, 1), :]
                for half in range(2):
                    i = (r * 3 + c) * 2 + half
                    piece = row[:, half * 256 : (half + 1) * 256]
                    if d in (1, n - 1):
                        ref = up if d == 1 else down
                        ref[i // 3, 26 + i % 3 : 27 + i % 3, :] = piece
                    else:
                        others[d - 2][i : i + 1, :] = piece
    copies[nx].wait()
    for x in range(nx):
        copies[x].wait()

        def body(t, carry, x=x):
            rows = tile_rows(t)
            out = collide([here[x, k, rows, :] for k in range(19)])
            for k in range(19):
                post[k, x, rows_of(t), :] = out[k]
            return carry

        lax.fori_loop(0, TILES, body, 0)
        for ref, near, beyond, dirs in ((up, ROWS - 1, ROWS - 2, CY_PLUS), (down, 0, 1, CY_MINUS)):
            for k in range(19):
                ref[x, k : k + 1, :] = post[k, x, 8 + near : 9 + near, :]
            for j, k in enumerate(dirs):
                ref[x, 19 + j : 20 + j, :] = post[k, x, 8 + beyond : 9 + beyond, :]
            ref[x, 24:25, :] = flags[x, near : near + 1, :].astype(F32)
            ref[x, 25:26, :] = flags[x, beyond : beyond + 1, :].astype(F32)
    for x, ref, dirs in ((nx - 1, fwd, CX_PLUS), (0, bwd, CX_MINUS)):
        for j, k in enumerate(dirs):
            ref[j * ROWS : (j + 1) * ROWS, :] = post[k, x, 8:72, :]
        ref[5 * ROWS : 6 * ROWS, :] = flags[x].astype(F32)


def sent_velocity(refs, n, d, r, c):
    out = []
    for half in range(2):
        i = (r * 3 + c) * 2 + half
        if d in (1, n - 1):
            out.append(refs[d - 1][i // 3, 26 + i % 3 : 27 + i % 3, :])
        else:
            out.append(refs[d - 1][i : i + 1, :])
    return jnp.concatenate(out, axis=1)


def edges_kernel(n, nx, post_in, fwd_in, bwd_in, mask, below, above, post, fwd, bwd, flags):
    me = lax.axis_index("xs")
    has_below, has_above = (me > 0).astype(F32), (me < n - 1).astype(F32)
    for x in range(nx):
        for k in range(19):
            post[k, x, 79:80, :] = below[x, k : k + 1, :]
            post[k, x, 72:73, :] = above[x, k : k + 1, :]
        for j, k in enumerate(CY_PLUS):
            post[k, x, 7:8, :] = below[x, k : k + 1, :]
            post[k, x, 78:79, :] = below[x, 19 + j : 20 + j, :]
        for j, k in enumerate(CY_MINUS):
            post[k, x, 73:74, :] = above[x, 19 + j : 20 + j, :]
            post[k, x, 80:81, :] = post[k, x, 8:9, :]
        flags[x, 8:72, :] = mask[x]
        near = (below[x, 24:25, :] * has_below).astype(I32)
        flags[x, 79:80, :] = near
        flags[x, 7:8, :] = near
        flags[x, 78:79, :] = (below[x, 25:26, :] * has_below).astype(I32)
        flags[x, 72:73, :] = (above[x, 24:25, :] * has_above).astype(I32)
        flags[x, 73:74, :] = (above[x, 25:26, :] * has_above).astype(I32)
        flags[x, 80:81, :] = mask[x, 0:1, :]
    for rows, x, dirs, far_below, far_above in (
        (fwd, nx - 1, CX_PLUS, 7, 9),
        (bwd, 0, CX_MINUS, 10, 8),
    ):
        e = 6 * ROWS
        for j, k in enumerate(dirs):
            rows[e + j : e + j + 1, :] = below[x, k : k + 1, :]
            rows[e + 8 + j : e + 9 + j, :] = above[x, k : k + 1, :]
        j = 19 + CY_PLUS.index(far_below)
        rows[e + 5 : e + 6, :] = below[x, j : j + 1, :]
        j = 19 + CY_MINUS.index(far_above)
        rows[e + 13 : e + 14, :] = above[x, j : j + 1, :]
        rows[e + 6 : e + 8, :] = below[x, 24:26, :] * has_below
        rows[e + 14 : e + 16, :] = above[x, 24:26, :] * has_above


def step_layer(x, read, read_mask, post, post2, bits_out):
    def body(t, carry):
        bits = open_bits(read_mask, t)
        own = [post[k, x, rows_of(t), :] for k in range(19)]
        out = collide(stream(read, own, bits, t))
        for k in range(19):
            post2[k, x, rows_of(t), :] = out[k]
        bits_out[x, tile_rows(t), :] = bits
        return carry

    lax.fori_loop(0, TILES + 1, body, 0)
    for k in CY_PLUS:
        post2[k, x, 7:8, :] = post2[k, x, 79:80, :]


def middle_kernel(nx, post, flags, post2, bits_out):
    for x in range(1, nx - 1):
        step_layer(
            x,
            lambda k, dx, tile, x=x: post[k, x - dx, rows_of(tile), :],
            lambda dx, tile, x=x: flags[x - dx, rows_of(tile), :],
            post,
            post2,
            bits_out,
        )


def outer_kernel(
    nx, post, flags, before, after, post2_in, bits_in, post2, bits_out, fwd2, bwd2, halo, halo_flags
):
    last = nx - 1
    e = 6 * ROWS
    for i, (ref, dirs, far_below, far_above) in enumerate(
        ((before, CX_PLUS, 7, 9), (after, CX_MINUS, 10, 8))
    ):
        for j, k in enumerate(dirs):
            halo[i, j, 8:72, :] = ref[j * ROWS : (j + 1) * ROWS, :]
            halo[i, j, 79:80, :] = ref[e + j : e + j + 1, :]
            halo[i, j, 72:73, :] = ref[e + 8 + j : e + 9 + j, :]
            if k == far_below:
                halo[i, j, 7:8, :] = ref[e + j : e + j + 1, :]
                halo[i, j, 78:79, :] = ref[e + 5 : e + 6, :]
            if k == far_above:
                halo[i, j, 73:74, :] = ref[e + 13 : e + 14, :]
                halo[i, j, 80:81, :] = ref[j * ROWS : j * ROWS + 1, :]
        halo_flags[i, 8:72, :] = ref[5 * ROWS : 6 * ROWS, :].astype(I32)
        halo_flags[i, 79:80, :] = ref[e + 6 : e + 7, :].astype(I32)
        halo_flags[i, 7:8, :] = ref[e + 6 : e + 7, :].astype(I32)
        halo_flags[i, 78:79, :] = ref[e + 7 : e + 8, :].astype(I32)
        halo_flags[i, 72:73, :] = ref[e + 14 : e + 15, :].astype(I32)
        halo_flags[i, 73:74, :] = ref[e + 15 : e + 16, :].astype(I32)
        halo_flags[i, 80:81, :] = ref[5 * ROWS : 5 * ROWS + 1, :].astype(I32)
    for x in (0, last):

        def read(k, dx, tile, x=x):
            if x - dx < 0:
                return halo[0, CX_PLUS.index(k), rows_of(tile), :]
            if x - dx > last:
                return halo[1, CX_MINUS.index(k), rows_of(tile), :]
            return post[k, x - dx, rows_of(tile), :]

        def read_mask(dx, tile, x=x):
            if x - dx < 0 or x - dx > last:
                return halo_flags[0 if x - dx < 0 else 1, rows_of(tile), :]
            return flags[x - dx, rows_of(tile), :]

        step_layer(x, read, read_mask, post, post2, bits_out)
    for x, ref, dirs, k_below, k_above in ((last, fwd2, CX_PLUS, 7, 9), (0, bwd2, CX_MINUS, 10, 8)):
        for j, k in enumerate(dirs):
            ref[j * ROWS : (j + 1) * ROWS, :] = post2[k, x, 8:72, :]
        ref[320:321, :] = post2[k_below, x, 79:80, :]
        ref[321:322, :] = post2[k_above, x, 72:73, :]


def final_layer(x, read, post2, bits, result, flow, out, sem):
    def body(t, carry):
        rows = tile_rows(t)
        own = [post2[k, x, rows_of(t), :] for k in range(19)]
        f = stream(read, own, bits[x, rows, :], t)
        for k in range(19):
            result[k, rows, :] = f[k]
        rho, ux, uy, uz = velocity_of(f)
        flow[0, x, rows, :] = ux
        flow[1, x, rows, :] = uy
        flow[2, x, rows, :] = uz
        return carry

    lax.fori_loop(0, TILES, body, 0)
    copy = pltpu.make_async_copy(result, out.at[:, x], sem)
    copy.start()
    return copy


def final_middle_kernel(nx, post2, bits, out, flow, result, sems):
    copies = []
    for i, x in enumerate(range(1, nx - 1)):
        read = lambda k, dx, tile, x=x: post2[k, x - dx, rows_of(tile), :]
        copies.append(final_layer(x, read, post2, bits, result.at[i], flow, out, sems.at[i]))
    for copy in copies:
        copy.wait()


def final_outer_kernel(nx, out_in, flow_in, post2, bits, before, after, out, flow, halo, result, sems):
    last = nx - 1
    for i, (ref, dirs, k_below, k_above) in enumerate(
        ((before, CX_PLUS, 7, 9), (after, CX_MINUS, 10, 8))
    ):
        for j in range(5):
            halo[i, j, 8:72, :] = ref[j * ROWS : (j + 1) * ROWS, :]
        halo[i, dirs.index(k_below), 7:8, :] = ref[320:321, :]
        halo[i, dirs.index(k_above), 72:73, :] = ref[321:322, :]
    copies = []
    for i, x in enumerate((0, last)):

        def read(k, dx, tile, x=x):
            if x - dx < 0:
                return halo[0, CX_PLUS.index(k), rows_of(tile), :]
            if x - dx > last:
                return halo[1, CX_MINUS.index(k), rows_of(tile), :]
            return post2[k, x - dx, rows_of(tile), :]

        copies.append(final_layer(x, read, post2, bits, result.at[i], flow, out, sems.at[i]))
    for copy in copies:
        copy.wait()


def pair_kernel(first_patch, pair_tiles, pos, vel, noise, *refs):
    base, rows, cols, theta, acc = refs[-5:]
    g = pl.program_id(0) + first_patch
    tile = noise.shape[-1]
    count = pos.shape[-1] // tile
    pairs = noise.shape[1]
    both = [ref[c, pl.ds(g, 1), :] for ref in (pos, vel) for c in range(3)]
    speed = both[3:]
    both = [both[c] if c < 3 else 4.5 * both[c] for c in range(6)]
    stacked = jnp.concatenate(both + [jnp.zeros((2, both[0].shape[1]), F32)], axis=0)
    turned = stacked.T
    for c in range(6):
        for j in range(count):
            part = turned[j * tile : (j + 1) * tile, c : c + 1]
            cols[c, j] = jnp.broadcast_to(part, (tile, tile))
            rows[c, j] = jnp.broadcast_to(both[c][:, j * tile : (j + 1) * tile], (8, tile))
    acc[...] = jnp.zeros_like(acc)
    eye = lax.broadcasted_iota(I32, (tile, tile), 0) == lax.broadcasted_iota(I32, (tile, tile), 1)
    scale = jnp.where(eye, 15.0, 0.0).astype(BF16)
    for p in range(pairs):
        theta[p] = lax.dot_general(
            scale, noise[0, p], (((1,), (1,)), ((), ())), preferred_element_type=F32
        )

    def one_pair(p, carry):
        first = pair_tiles[g, 0, p]
        second = pair_tiles[g, 1, p]
        mine = [rows[c, first] for c in range(6)]
        parts = []
        for s in range(tile // 8):
            part = slice(8 * s, 8 * s + 8)
            dx, dy, dz = [mine[c] - cols[c, second, part, :] for c in range(3)]
            vx, vy, vz = [mine[c] - cols[c, second, part, :] for c in range(3, 6)]
            square = (dx * dx + 0.01) + (dy * dy + dz * dz)
            close = jnp.maximum(lax.rsqrt(square) - 1.0, 0.0)
            along = dx * vx + (dy * vy + dz * vz)
            force = close * ((theta[p, part, :] + 25.0) - close * along)
            here = [force * dx, force * dy, force * dz]
            parts = here if not parts else [a + b for a, b in zip(parts, here)]
        for c in range(3):
            acc[first, c] += parts[c]
        return carry

    lax.fori_loop(0, pairs, one_pair, 0)
    for c in range(3):
        force = jnp.concatenate(
            [jnp.sum(acc[j, c], axis=0, keepdims=True) for j in range(count)], axis=1
        )
        base[c, pl.ds(g, 1), :] = 0.5 * speed[c] + 0.04 * force


def split(value):
    high = value.astype(BF16)
    return high, (value - high.astype(F32)).astype(BF16)


def ranks(owner, count):
    out = []
    for g in range(count):
        rank = jnp.int32(0)
        for h in range(g):
            rank = rank + (owner[h] == owner[g]).astype(I32)
        out.append(rank)
    return out


def one_hot(index, extent):
    want = index.astype(F32).astype(BF16)
    place = lax.broadcasted_iota(I32, (extent, index.shape[1]), 0).astype(F32).astype(BF16)
    return place == want


def scatter_kernel(n, per, owner, voxel, vel, *refs):
    sent, out, table = refs[: n - 1], refs[n - 1], refs[n]
    me = lax.axis_index("xs")
    beads = voxel.shape[1]
    for r in range(per):
        for c in range(3):
            table[me, r, c : c + 1, :] = vel[c, pl.ds(me * per + r, 1), :]
        for d in range(1, n):
            source = lax.rem(me + n - d, n)
            for c in range(3):
                table[source, r, c : c + 1, :] = sent_velocity(sent, n, d, r, c)
    out[...] = jnp.zeros_like(out)
    rank = ranks(owner, voxel.shape[0])
    one, zero = BF16(1), BF16(0)
    for g in range(voxel.shape[0]):
        index = voxel[g : g + 1, :]
        lanes = jnp.where(one_hot(index & 255, 256), one, zero)
        at_row = one_hot(index >> 8, out.shape[1])
        values = table[owner[g], rank[g]]
        lanes2 = jnp.concatenate([lanes, lanes], axis=1)
        for c in range(3):
            high, low = split(values[c : c + 1, :])
            left = jnp.concatenate(
                [jnp.where(at_row, high, zero), jnp.where(at_row, low, zero)], axis=1
            )
            out[c] += lax.dot_general(
                left, lanes2, (((1,), (1,)), ((), ())), preferred_element_type=F32
            )
        out[3] += lax.dot_general(
            jnp.where(at_row, one, zero), lanes, (((1,), (1,)), ((), ())), preferred_element_type=F32
        )


def gather_kernel(n, per, owner, voxel, flow, *refs):
    outs, table, field = refs[:n], refs[n], refs[n + 1]
    me = lax.axis_index("xs")
    patches = voxel.shape[0]
    nx = flow.shape[1]
    rows = nx * ROWS
    for c in range(3):
        for x in range(nx):
            high, low = split(flow[c, x])
            field[c, x * ROWS : (x + 1) * ROWS, 0:256] = high
            field[c, x * ROWS : (x + 1) * ROWS, 256:512] = low
    one, zero = BF16(1), BF16(0)
    for g in range(patches):
        index = voxel[g : g + 1, :]
        lanes = jnp.where(one_hot(index & 255, 256), one, zero)
        lanes2 = jnp.concatenate([lanes, lanes], axis=0)
        at_row = lax.broadcasted_iota(I32, (rows, index.shape[1]), 0) == (index >> 8)
        for c in range(3):
            found = lax.dot_general(
                field[c], lanes2, (((1,), (0,)), ((), ())), preferred_element_type=F32
            )
            table[g, c : c + 1, :] = jnp.sum(jnp.where(at_row, found, 0.0), axis=0, keepdims=True)
    rank = ranks(owner, patches)
    for d in range(n):
        target = lax.rem(me + d, n)
        for r in range(per):
            found = jnp.int32(0)
            for g in range(patches):
                found = jnp.where((owner[g] == target) & (rank[g] == r), g, found)
            outs[d][r * 3 : r * 3 + 3, :] = table[found, 0:3, :]


def field_kernel(total, flow, field):
    for x in range(field.shape[1]):
        rows = slice(x * ROWS, (x + 1) * ROWS)
        number = 10.0 * total[3, rows, :]
        for c in range(3):
            field[c, x] = 0.5 * total[c, rows, :] - number * flow[c, x]


def final_kernel(n, per, pos, base, *refs):
    flows, new_pos, new_vel = refs[:n], refs[n], refs[n + 1]
    me = lax.axis_index("xs")
    for d in range(n):
        source = lax.rem(me + n - d, n)
        for r in range(per):
            at = pl.ds(source * per + r, 1)
            for c in range(3):
                speed = base[c, at, :] + 10.0 * flows[d][r * 3 + c : r * 3 + c + 1, :]
                new_vel[c, at, :] = speed
                new_pos[c, at, :] = pos[c, at, :] + 0.04 * speed


def shift(value, axis, by):
    n = lax.axis_size(axis)
    return lax.ppermute(value, axis, [(i, (i + by) % n) for i in range(n)])


def pair_call(first_patch, patches, pair_tiles, pos, vel, noise, given, after):
    beads = pos.shape[2]
    tile = noise.shape[-1]
    count = beads // tile
    whole = lambda g, s: (0, 0, 0)
    ins = [pos, vel, noise] + given + after
    return pl.pallas_call(
        functools.partial(pair_kernel, first_patch),
        grid_spec=pltpu.PrefetchScalarGridSpec(
            num_scalar_prefetch=1,
            grid=(patches,),
            in_specs=[
                pl.BlockSpec(pos.shape, whole),
                pl.BlockSpec(vel.shape, whole),
                pl.BlockSpec((1,) + noise.shape[1:], lambda g, s: (g + first_patch, 0, 0, 0)),
            ]
            + [pl.BlockSpec(pos.shape, whole)] * len(given)
            + [ANY_SPEC] * len(after),
            out_specs=pl.BlockSpec(pos.shape, whole),
            scratch_shapes=[
                pltpu.VMEM((6, count, 8, tile), F32),
                pltpu.VMEM((6, count, tile, tile), F32),
                pltpu.VMEM(noise.shape[1:], F32),
                pltpu.VMEM((count, 3, 8, tile), F32),
            ],
        ),
        out_shape=jax.ShapeDtypeStruct(pos.shape, F32),
        input_output_aliases={4: 0} if given else {},
        compiler_params=params(),
        cost_estimate=cost(3_000_000_000, 1_500_000),
        name="pair_forces",
    )(pair_tiles, *ins)


def per_device(
    populations, fluid_mask, patch_voxel, patch_owner, positions, velocities, pair_tiles, pair_noise
):
    n = lax.axis_size("xs")
    patches, beads = patch_voxel.shape
    per = patches // n
    nx = populations.shape[1]
    lanes = populations.shape[3]
    arr = lambda *shape: jax.ShapeDtypeStruct(shape, F32)
    ints = lambda *shape: jax.ShapeDtypeStruct(shape, I32)
    vmem, dma = pltpu.VMEM, pltpu.SemaphoreType.DMA
    positions = jnp.transpose(positions, (1, 0, 2))
    velocities = jnp.transpose(velocities, (1, 0, 2))
    pair_tiles = jnp.transpose(pair_tiles, (0, 2, 1))

    post, fwd, bwd, up, down, *others = call(
        functools.partial(collide_kernel, n, per, nx),
        [populations, fluid_mask, velocities],
        [
            arr(19, nx, PAD, lanes),
            arr(400, lanes),
            arr(400, lanes),
            arr(nx, 32, lanes),
            arr(nx, 32, lanes),
        ]
        + [arr(16, lanes)] * (n - 3),
        "collide_first",
        cost(3_000_000_000, 11_000_000),
        specs={0: HBM_SPEC, 1: HBM_SPEC},
        out_specs=[VMEM_SPEC] * (5 + n - 3),
        scratch_shapes=[vmem((nx, 19, ROWS, lanes), F32), vmem((nx, ROWS, lanes), I32), dma((nx + 1,))],
    )
    below = shift(up, "xs", 1)
    above = shift(down, "xs", -1)
    sent = [below] + [shift(other, "xs", d + 2) for d, other in enumerate(others)] + [above]

    half = patches // 2
    bead_args = (pair_tiles, positions, velocities, pair_noise)
    base = pair_call(0, half, *bead_args, [], [down])

    post, fwd, bwd, flags = call(
        functools.partial(edges_kernel, n, nx),
        [post, fwd, bwd, fluid_mask, below, above],
        [arr(*post.shape), arr(*fwd.shape), arr(*bwd.shape), ints(nx, PAD, lanes)],
        "edges",
        cost(1000, 100_000),
        after=[base],
        out_specs=[VMEM_SPEC] * 4,
        input_output_aliases={0: 0, 1: 1, 2: 2},
    )
    before = shift(fwd, "ax", 1)
    after = shift(bwd, "ax", -1)

    post2, bits = call(
        functools.partial(middle_kernel, nx),
        [post, flags],
        [arr(19, nx, PAD, lanes), ints(nx, 72, lanes)],
        "middle_layers",
        cost(3_000_000_000, 9_000_000),
        out_specs=[VMEM_SPEC] * 2,
    )
    base = pair_call(half, patches - half, *bead_args, [base], [flags])

    post2, bits, fwd2, bwd2 = call(
        functools.partial(outer_kernel, nx),
        [post, flags, before, after, post2, bits],
        [arr(*post2.shape), ints(*bits.shape), arr(328, lanes), arr(328, lanes)],
        "outer_layers",
        cost(3_000_000_000, 9_000_000),
        after=[base],
        out_specs=[VMEM_SPEC] * 4,
        input_output_aliases={4: 0, 5: 1},
        scratch_shapes=[vmem((2, 5, PAD, lanes), F32), vmem((2, PAD, lanes), I32)],
    )
    before2 = shift(fwd2, "ax", 1)
    after2 = shift(bwd2, "ax", -1)

    out, flow = call(
        functools.partial(final_middle_kernel, nx),
        [post2, bits],
        [arr(*populations.shape), arr(3, nx, ROWS, lanes)],
        "final_middle",
        cost(3_000_000_000, 7_000_000),
        out_specs=[ANY_SPEC, VMEM_SPEC],
        scratch_shapes=[vmem((nx - 2, 19, ROWS, lanes), F32), dma((nx - 2,))],
    )
    total = call(
        functools.partial(scatter_kernel, n, per),
        [patch_owner, patch_voxel, velocities] + sent,
        arr(4, nx * ROWS, lanes),
        "bead_sums",
        cost(3_000_000_000, 1_500_000),
        after=[fwd2],
        specs={0: SMEM_SPEC},
        out_specs=VMEM_SPEC,
        scratch_shapes=[vmem((n, per, 8, beads), F32)],
    )
    out, flow = call(
        functools.partial(final_outer_kernel, nx),
        [out, flow, post2, bits, before2, after2],
        [arr(*populations.shape), arr(*flow.shape)],
        "final_outer",
        cost(3_000_000_000, 7_000_000),
        after=[total],
        specs={0: ANY_SPEC},
        out_specs=[ANY_SPEC, VMEM_SPEC],
        input_output_aliases={0: 0, 1: 1},
        scratch_shapes=[vmem((2, 5, PAD, lanes), F32), vmem((2, 19, ROWS, lanes), F32), dma((2,))],
    )
    flows = call(
        functools.partial(gather_kernel, n, per),
        [patch_owner, patch_voxel, flow],
        [arr(8, beads)] * n,
        "bead_flow",
        cost(3_000_000_000, 1_500_000),
        specs={0: SMEM_SPEC},
        out_specs=[VMEM_SPEC] * n,
        scratch_shapes=[vmem((patches, 8, beads), F32), vmem((3, nx * ROWS, 2 * lanes), BF16)],
    )
    sent_flows = [flows[0]] + [shift(flows[d], "xs", d) for d in range(1, n)]
    field = call(
        field_kernel,
        [total, flow],
        arr(3, nx, ROWS, lanes),
        "drag_field",
        cost(400_000_000, 2_500_000),
        after=[flows[1]],
        out_specs=VMEM_SPEC,
    )
    new_pos, new_vel = call(
        functools.partial(final_kernel, n, per),
        [positions, base] + sent_flows,
        [arr(*positions.shape)] * 2,
        "bead_update",
        cost(50_000, 300_000),
        after=[field],
        out_specs=[VMEM_SPEC] * 2,
    )
    return out, jnp.transpose(new_pos, (1, 0, 2)), jnp.transpose(new_vel, (1, 0, 2)), field


def solution(mesh):
    return jax.shard_map(
        per_device,
        mesh=mesh,
        in_specs=(
            P(None, "ax", "xs", None),
            P("ax", "xs", None),
            P(("ax", "xs"), None),
            P(("ax", "xs")),
            P(("ax", "xs"), None, None),
            P(("ax", "xs"), None, None),
            P(("ax", "xs"), None, None),
            P(("ax", "xs"), None, None, None),
        ),
        out_specs=(
            P(None, "ax", "xs", None),
            P(("ax", "xs"), None, None),
            P(("ax", "xs"), None, None),
            P(None, "ax", "xs", None),
        ),
        check_vma=False,
    )
```

time: 688 us -> 64.6 us (0.09)
  loops' own time: 247 us -> 0 us
  other arithmetic: 179 us -> 0 us
  local copies, waits for them, and re-layouts: 157 us -> 5.31 us
  waiting for transfers between devices: 73.4 us -> 6.53 us
  Pallas kernels: 0 us -> 36.5 us
  starting transfers between devices: 25.1 us -> 15.1 us
    another operation x9 -> x0, loops' own time: 247 us -> none  [the longest x8 246 us: pair_forces(): total, unused = lax.scan(one_pair, start, (pair_list, noise))]
    scatter-add x3 -> x0, other arithmetic: 66.4 us -> none  [per_device(): jax.ops.segment_sum(back[:, comp, :].reshape(-1), flat_ids, num_segments=...]
    ppermute x8 -> x10, waiting for transfers between devices: 63.5 us -> 6.53 us  [shift(): return lax.ppermute(value, axis, [(i, (i + by) % n) for i in range(n)])]
    slice x71 -> x0, local copies, waits for them, and re-layouts: 39.1 us -> none  [the longest x64 37.1 us: one_pair(): pos_b = lax.dynamic_index_in_dim(pos_tiles, pair[1], 1, keepdims=False)]
    unnamed x40 -> x0, other arithmetic: 36.8 us -> none
    pallas_call x0 -> x12, Pallas kernels: none -> 36.5 us  [the longest x10 24.7 us: call(): pl.pallas_call(body, in_specs=[specs.get(i, VMEM_SPEC) for i in range(cou...]
    reduce_sum x193 -> x0, other arithmetic: 35.4 us -> none  [the longest x64 14.5 us: one_pair(): force = jnp.sum(scalar[None] * unit, axis=2)]
    dynamic_update_slice x32 -> x0, local copies, waits for them, and re-layouts: 23.2 us -> none  [per_device(): lax.map(patch_step, (positions, velocities, received, pair_tiles, pair_no...]
  transfers between devices with their start and end apart: 10 -> 10, of which waited for: 9 -> 4; matrix products, arithmetic and copies ran while one was open for 1% -> 0% of each run, Pallas kernels for 0% -> 41%
where the time goes in v2:
time: 64.6 us; the launch traced here: 64.3 us
  Pallas kernels  36.5 us (57%)
  starting transfers between devices  15.1 us (23%)
  waiting for transfers between devices  6.53 us (10%)
  local copies, waits for them, and re-layouts  5.31 us (8%)
  between operations  0.81 us (1%)
    pallas_call x10, Pallas kernels, call(): pl.pallas_call(body, in_specs=[specs.get(i, VMEM_SPEC) for i in range(cou...  24.7 us
    ppermute x10, starting transfers between devices, shift(): return lax.ppermute(value, axis, [(i, (i + by) % n) for i in range(n)])  15.1 us
    pallas_call x2, Pallas kernels, pair_call(): pl.pallas_call(functools.partial(pair_kernel, first_patch), grid_spec=plt...  11.9 us
    ppermute x10, waiting for transfers between devices, shift(): return lax.ppermute(value, axis, [(i, (i + by) % n) for i in range(n)])  6.53 us
    unnamed x18, local copies, waits for them, and re-layouts  5.31 us
  transfers between devices with their start and end apart: 10, of which 4 were waited for; matrix products, arithmetic and copies ran while one was open for 0% of the time, Pallas kernels for 41%

profile of v2, /device:TPU:0, one launch (start us, length us, event | category | flops | bytes accessed | tf_op | source)
XLA Modules:
  0.0 64.3 jit_solution(6301079795000874879)
XLA Ops:
  0.6 0.0 copy-start.1
  0.6 0.9 %copy-done.1 = s32[4,64,256]{2,1,0:T(8,128)S(1)} copy-done((s32[4,64,256]{2,1,0:T(8,128)S(1)}, s32[4,64,256]{2,1,0:T(8,128)}, u32[]{:S(2)}) %copy-start.1) | copy-done | bytes 262168
  1.6 0.0 copy-start.3
  1.6 2.4 %copy-done.3 = f32[19,4,64,256]{3,2,1,0:T(8,128)S(1)} copy-done((f32[19,4,64,256]{3,2,1,0:T(8,128)S(1)}, f32[19,4,64,256]{3,2,1,0:T(8,128)}, u32[]{:S(2)}) %copy-start.3) | copy-done | bytes 4980760
  4.0 0.0 copy-start.5
  4.0 0.8 %copy-done.5 = f32[8,3,512]{2,0,1:T(8,128)S(1)} copy-done((f32[8,3,512]{2,0,1:T(8,128)S(1)}, f32[8,3,512]{2,0,1:T(8,128)}, u32[]{:S(2)}) %copy-start.5) | copy-done | bytes 49176
  4.8 0.0 copy-start.2
  4.8 0.0 copy-start.4
  4.8 0.0 copy-start.7
  4.8 2.5 %collide_first.1 = (f32[19,4,88,256]{3,2,1,0:T(8,128)S(1)}, f32[400,256]{1,0:T(8,128)S(1)}, f32[400,256]{1,0:T(8,128)S(1)}, f32[4,32,256]{2,1,0:T(8,128)S(1)}, f...) custom-call(f32[19,4,64,256]{3,2,1,0:T(8,128)S(1)} %copy-done.3, s32[4,64,256]{2,1,0:T(8,128)S(1)} %copy-done.1, ...), custom_call_target="tpu_custom_call" | custom-call | flops 3000000000 | bytes 11000000 | tf_op jit(solution)/shard_map/collide_first/pallas_call | solution.py:64
  7.3 4.1 %collective-permute-start.6 = (f32[16,256]{1,0:T(8,128)S(1)}, f32[16,256]{1,0:T(8,128)S(1)}, u32[]{:S(2)}, u32[]{:S(2)}) collective-permute-start(f32[16,256]{1,0:T(8,128)S(1)} %get-tuple-element.47), channel_id=1, source_target_pairs={{0,2},{1,3},{2,0},{3,1},{4,6},{5,7},{6,4},{7,5},{8,10},{9,11},{10,... | collective-permute-start | bytes 49160 | tf_op jit(solution)/shard_map/ppermute | solution.py:547
  11.4 1.6 %collective-permute-start = (f32[4,32,256]{2,1,0:T(8,128)S(1)}, f32[4,32,256]{2,1,0:T(8,128)S(1)}, u32[]{:S(2)}, u32[]{:S(2)}) collective-permute-start(f32[4,32,256]{2,1,0:T(8,128)S(1)} %get-tuple-element.33), channel_id=1, source_target_pairs={{0,1},{1,2},{2,3},{3,0},{4,5},{5,6},{6,7},{7,4},{8,9},{9,10},{10,1... | collective-permute-start | bytes 393224 | tf_op jit(solution)/shard_map/ppermute | solution.py:547
  12.9 2.2 %collective-permute-start.1 = (f32[4,32,256]{2,1,0:T(8,128)S(1)}, f32[4,32,256]{2,1,0:T(8,128)S(1)}, u32[]{:S(2)}, u32[]{:S(2)}) collective-permute-start(f32[4,32,256]{2,1,0:T(8,128)S(1)} %get-tuple-element.34.refs_0_), channel_id=1, source_target_pairs={{0,3},{1,0},{2,1},{3,2},{4,7},{5,4},{6,5},{7,6},{8,11},{9,8},{10,9... | collective-permute-start | bytes 393224 | tf_op jit(solution)/shard_map/ppermute | solution.py:547
  15.2 0.0 copy-done.2
  15.2 0.0 copy-done.4
  15.2 0.0 copy-done.7
  15.2 5.9 %pair_forces.2.refs_6_.refs_0_ = f32[3,8,512]{2,1,0:T(8,128)S(1)} custom-call(s32[8,2,8]{2,1,0:T(2,128)S(1)} %bitcast.12, f32[3,8,512]{2,1,0:T(8,128)S(1)} %bitcast.5, f32[3,8,512]{2,1,0:T(8,128)S(1)} %bitcast.9, bf16[8,8,128,128]{3,2,1,0:T(8,128)(2,1)S(1)} %copy-done.4, f32[4,32,256]{2,1,0:T(8,128)S(1)} %get-tuple-element.34.refs_0_), custom_call_target="tpu_custom_call" | custom-call | flops 3000000000 | bytes 1500000 | tf_op jit(solution)/shard_map/pair_forces/pallas_call | solution.py:556
  21.1 0.0 collective-permute-done.refs_4_.refs_3_
  21.1 0.0 collective-permute-done.1.refs_5_
  21.1 0.2 edges.1
  21.3 0.1 collective-permute-start.2
  21.4 2.6 %collective-permute-start.3 = (f32[400,256]{1,0:T(8,128)S(1)}, f32[400,256]{1,0:T(8,128)S(1)}, u32[]{:S(2)}, u32[]{:S(2)}) collective-permute-start(f32[400,256]{1,0:T(8,128)S(1)} %get-tuple-element.38), channel_id=1, source_target_pairs={{0,28},{4,0},{8,4},{12,8},{16,12},{20,16},{24,20},{28,24},{1,29},{... | collective-permute-start | bytes 1228808 | tf_op jit(solution)/shard_map/ppermute | solution.py:547
  24.0 5.9 %pair_forces.3.refs_6_.refs_1_ = f32[3,8,512]{2,1,0:T(8,128)S(1)} custom-call(s32[8,2,8]{2,1,0:T(2,128)S(1)} %bitcast.13, f32[3,8,512]{2,1,0:T(8,128)S(1)} %bitcast.6, f32[3,8,512]{2,1,0:T(8,128)S(1)} %bitcast.10, bf16[8,8,128,128]{3,2,1,0:T(8,128)(2,1)S(1)} %copy-done.4, ...), custom_call_target="tpu_custom_call", output_to_operand_aliasing={{}: (4, {})} | custom-call | flops 3000000000 | bytes 1500000 | tf_op jit(solution)/shard_map/pair_forces/pallas_call | solution.py:556
  30.0 3.0 %middle_layers.1 = (f32[19,4,88,256]{3,2,1,0:T(8,128)S(1)}, s32[4,72,256]{2,1,0:T(8,128)S(1)}) custom-call(f32[19,4,88,256]{3,2,1,0:T(8,128)S(1)} %get-tuple-element.35.refs_0_, s32[4,88,256]{2,1,0:T(8,128)S(1)} %get-tuple-element.36.refs_1_), custom_call_target="tpu_custom_call" | custom-call | flops 3000000000 | bytes 9000000 | tf_op jit(solution)/shard_map/middle_layers/pallas_call | solution.py:64
  32.9 0.0 collective-permute-done.2.refs_2_
  33.0 0.0 collective-permute-done.3.refs_3_
  33.0 3.1 %outer_layers.1 = (f32[19,4,88,256]{3,2,1,0:T(8,128)S(1)}, s32[4,72,256]{2,1,0:T(8,128)S(1)}, f32[328,256]{1,0:T(8,128)S(1)}, f32[328,256]{1,0:T(8,128)S(1)}) custom-call(f32[19,4,88,256]{3,2,1,0:T(8,128)S(1)} %get-tuple-element.35.refs_0_, s32[4,88,256]{2,1,0:T(8,128)S(1)} %get-tuple-element.36.refs_1_, ...), custom_call_target="tpu_custom_call", output_to_operand_aliasing={{0}: (4, {}), {1}: (5, {})} | custom-call | flops 3000000000 | bytes 9000000 | tf_op jit(solution)/shard_map/outer_layers/pallas_call | solution.py:64
  36.0 0.0 copy-start.6
  36.1 0.0 copy-start.8
  36.1 2.0 %collective-permute-start.5 = (f32[328,256]{1,0:T(8,128)S(1)}, f32[328,256]{1,0:T(8,128)S(1)}, u32[]{:S(2)}, u32[]{:S(2)}) collective-permute-start(f32[328,256]{1,0:T(8,128)S(1)} %get-tuple-element.46), channel_id=1, source_target_pairs={{0,28},{4,0},{8,4},{12,8},{16,12},{20,16},{24,20},{28,24},{1,29},{... | collective-permute-start | bytes 1007624 | tf_op jit(solution)/shard_map/ppermute | solution.py:547
  38.1 0.0 collective-permute-start.4
  38.1 2.8 %final_middle.1 = (f32[19,4,64,256]{3,2,1,0:T(8,128)}, f32[3,4,64,256]{3,2,1,0:T(8,128)S(1)}) custom-call(f32[19,4,88,256]{3,2,1,0:T(8,128)S(1)} %get-tuple-element.41.refs_0_.refs_2_, s32[4,72,256]{2,1,0:T(8,128)S(1)} %get-tuple-element.42.refs_1_.refs_3_), custom_call_target="tpu_custom_call" | custom-call | flops 3000000000 | bytes 7000000 | tf_op jit(solution)/shard_map/final_middle/pallas_call | solution.py:64
  40.9 0.0 collective-permute-done.6.refs_4_
  40.9 0.0 copy-done.6
  40.9 0.0 copy-done.8
  40.9 4.5 %bead_sums.1.refs_6_.refs_0_ = f32[4,256,256]{2,1,0:T(8,128)S(1)} custom-call(s32[8]{0:T(128)S(1)} %copy-done.8, s32[8,512]{1,0:T(8,128)S(1)} %copy-done.6, f32[3,8,512]{2,1,0:T(8,128)S(1)} %bitcast.11, f32[4,32,256]{2,1,0:T(8,128)S(1)} %collective-permute-done.refs_4_.refs_3_, f32[16,256]{1,0:T(8,128)S(1)} %collective-permute-done.6.refs_4_, ...), custom_call_target="tpu_custom_call" | custom-call | flops 3000000000 | bytes 1500000 | tf_op jit(solution)/shard_map/bead_sums/pallas_call | solution.py:64
  45.4 0.9 %collective-permute-done.5.refs_5_ = f32[328,256]{1,0:T(8,128)S(1)} collective-permute-done((f32[328,256]{1,0:T(8,128)S(1)}, f32[328,256]{1,0:T(8,128)S(1)}, u32[]{:S(2)}, u32[]{:S(2)}) %collective-permute-start.5) | collective-permute-done | bytes 335904 | tf_op jit(solution)/shard_map/ppermute | solution.py:547
  46.4 1.3 %collective-permute-done.4.refs_4_ = f32[328,256]{1,0:T(8,128)S(1)} collective-permute-done((f32[328,256]{1,0:T(8,128)S(1)}, f32[328,256]{1,0:T(8,128)S(1)}, u32[]{:S(2)}, u32[]{:S(2)}) %collective-permute-start.4) | collective-permute-done | bytes 335904 | tf_op jit(solution)/shard_map/ppermute | solution.py:547
  47.7 2.8 %final_outer.1 = (f32[19,4,64,256]{3,2,1,0:T(8,128)}, f32[3,4,64,256]{3,2,1,0:T(8,128)S(1)}) custom-call(f32[19,4,64,256]{3,2,1,0:T(8,128)} %get-tuple-element.43.refs_0_, f32[3,4,64,256]{3,2,1,0:T(8,128)S(1)} %get-tuple-element.44.refs_1_, f32[19,4,88,256]{3,2,1,0:T(8,128)S(1)} %get-tuple-element.41.refs_0_.refs_2_, ...), custom_call_target="tpu_custom_call", output_to_operand_aliasing={{0}: (0, {}), {1}: (1, {})} | custom-call | flops 3000000000 | bytes 7000000 | tf_op jit(solution)/shard_map/final_outer/pallas_call | solution.py:64
  50.5 4.3 %bead_flow.1 = (f32[8,512]{1,0:T(8,128)S(1)}, f32[8,512]{1,0:T(8,128)S(1)}, f32[8,512]{1,0:T(8,128)S(1)}, f32[8,512]{1,0:T(8,128)S(1)}) custom-call(s32[8]{0:T(128)S(1)} %copy-done.8, s32[8,512]{1,0:T(8,128)S(1)} %copy-done.6, f32[3,4,64,256]{3,2,1,0:T(8,128)S(1)} %get-tuple-element.49.refs_2_.refs_1_), custom_call_target="tpu_custom_call" | custom-call | flops 3000000000 | bytes 1500000 | tf_op jit(solution)/shard_map/bead_flow/pallas_call | solution.py:64
  54.8 0.5 collective-permute-start.8
  55.2 1.7 %collective-permute-start.9 = (f32[8,512]{1,0:T(8,128)S(1)}, f32[8,512]{1,0:T(8,128)S(1)}, u32[]{:S(2)}, u32[]{:S(2)}) collective-permute-start(f32[8,512]{1,0:T(8,128)S(1)} %get-tuple-element.53), channel_id=1, source_target_pairs={{0,3},{1,0},{2,1},{3,2},{4,7},{5,4},{6,5},{7,6},{8,11},{9,8},{10,9... | collective-permute-start | bytes 49160 | tf_op jit(solution)/shard_map/ppermute | solution.py:547
  57.0 0.3 collective-permute-start.7
  57.3 1.0 %drag_field.1.refs_6_ = f32[3,4,64,256]{3,2,1,0:T(8,128)} custom-call(f32[4,256,256]{2,1,0:T(8,128)S(1)} %bead_sums.1.refs_6_.refs_0_, f32[3,4,64,256]{3,2,1,0:T(8,128)S(1)} %get-tuple-element.49.refs_2_.refs_1_, f32[8,512]{1,0:T(8,128)S(1)} %get-tuple-element.51.refs_2_), custom_call_target="tpu_custom_call" | custom-call | flops 400000000 | bytes 2500000 | tf_op jit(solution)/shard_map/drag_field/pallas_call | solution.py:64
  58.2 1.2 %collective-permute-done.8.refs_4_ = f32[8,512]{1,0:T(8,128)S(1)} collective-permute-done((f32[8,512]{1,0:T(8,128)S(1)}, f32[8,512]{1,0:T(8,128)S(1)}, u32[]{:S(2)}, u32[]{:S(2)}) %collective-permute-start.8) | collective-permute-done | bytes 16416 | tf_op jit(solution)/shard_map/ppermute | solution.py:547
  59.5 0.0 collective-permute-done.9.refs_5_
  59.5 3.0 %collective-permute-done.7.refs_3_ = f32[8,512]{1,0:T(8,128)S(1)} collective-permute-done((f32[8,512]{1,0:T(8,128)S(1)}, f32[8,512]{1,0:T(8,128)S(1)}, u32[]{:S(2)}, u32[]{:S(2)}) %collective-permute-start.7) | collective-permute-done | bytes 16416 | tf_op jit(solution)/shard_map/ppermute | solution.py:547
  62.5 0.0 copy-start
  62.5 1.1 %copy-done = f32[3,4,64,256]{3,2,1,0:T(8,128)S(1)} copy-done((f32[3,4,64,256]{3,2,1,0:T(8,128)S(1)}, f32[3,4,64,256]{3,2,1,0:T(8,128)}, u32[]{:S(2)}) %copy-start) | copy-done | bytes 786456
  63.7 0.7 %bead_update.1 = (f32[3,8,512]{2,1,0:T(8,128)}, f32[3,8,512]{2,1,0:T(8,128)}) custom-call(f32[3,8,512]{2,1,0:T(8,128)S(1)} %bitcast.7, f32[3,8,512]{2,1,0:T(8,128)S(1)} %pair_forces.3.refs_6_.refs_1_, f32[8,512]{1,0:T(8,128)S(1)} %get-tuple-element.50.refs_2_, f32[8,512]{1,0:T(8,128)S(1)} %collective-permute-done.7.refs_3_, ...), custom_call_target="tpu_custom_call" | custom-call | flops 50000 | bytes 300000 | tf_op jit(solution)/shard_map/bead_update/pallas_call | solution.py:64
Async XLA Ops:
  0.6 1.0 %copy-start.1 = (s32[4,64,256]{2,1,0:T(8,128)S(1)}, s32[4,64,256]{2,1,0:T(8,128)}, u32[]{:S(2)}) copy-start(s32[4,64,256]{2,1,0:T(8,128)} %refs_3_.1) | copy-start | bytes 786436
  1.6 2.4 %copy-start.3 = (f32[19,4,64,256]{3,2,1,0:T(8,128)S(1)}, f32[19,4,64,256]{3,2,1,0:T(8,128)}, u32[]{:S(2)}) copy-start(f32[19,4,64,256]{3,2,1,0:T(8,128)} %refs_0_.3) | copy-start | bytes 14942212
  4.0 0.8 %copy-start.5 = (f32[8,3,512]{2,0,1:T(8,128)S(1)}, f32[8,3,512]{2,0,1:T(8,128)}, u32[]{:S(2)}) copy-start(f32[8,3,512]{2,0,1:T(8,128)} %param.13) | copy-start | bytes 147460
  4.8 10.4 %copy-start.2 = (f32[8,3,512]{2,0,1:T(8,128)S(1)}, f32[8,3,512]{2,0,1:T(8,128)}, u32[]{:S(2)}) copy-start(f32[8,3,512]{2,0,1:T(8,128)} %param.12) | copy-start | bytes 147460
  4.8 10.4 %copy-start.4 = (bf16[8,8,128,128]{3,2,1,0:T(8,128)(2,1)S(1)}, bf16[8,8,128,128]{3,2,1,0:T(8,128)(2,1)}, u32[]{:S(2)}) copy-start(bf16[8,8,128,128]{3,2,1,0:T(8,128)(2,1)} %noise.3) | copy-start | bytes 6291460
  4.8 10.4 %copy-start.7 = (s32[8,8,2]{1,2,0:T(2,128)S(1)}, s32[8,8,2]{1,2,0:T(2,128)}, u32[]{:S(2)}) copy-start(s32[8,8,2]{1,2,0:T(2,128)} %param.14) | copy-start | bytes 1540
  7.3 33.6 %collective-permute-start.6 = (f32[16,256]{1,0:T(8,128)S(1)}, f32[16,256]{1,0:T(8,128)S(1)}, u32[]{:S(2)}, u32[]{:S(2)}) collective-permute-start(f32[16,256]{1,0:T(8,128)S(1)} %get-tuple-element.47), channel_id=1, source_target_pairs={{0,2},{1,3},{2,0},{3,1},{4,6},{5,7},{6,4},{7,5},{8,10},{9,11},{10,... | collective-permute-start | bytes 49160 | tf_op jit(solution)/shard_map/ppermute | solution.py:547
  11.4 9.8 %collective-permute-start = (f32[4,32,256]{2,1,0:T(8,128)S(1)}, f32[4,32,256]{2,1,0:T(8,128)S(1)}, u32[]{:S(2)}, u32[]{:S(2)}) collective-permute-start(f32[4,32,256]{2,1,0:T(8,128)S(1)} %get-tuple-element.33), channel_id=1, source_target_pairs={{0,1},{1,2},{2,3},{3,0},{4,5},{5,6},{6,7},{7,4},{8,9},{9,10},{10,1... | collective-permute-start | bytes 393224 | tf_op jit(solution)/shard_map/ppermute | solution.py:547
  12.9 8.2 %collective-permute-start.1 = (f32[4,32,256]{2,1,0:T(8,128)S(1)}, f32[4,32,256]{2,1,0:T(8,128)S(1)}, u32[]{:S(2)}, u32[]{:S(2)}) collective-permute-start(f32[4,32,256]{2,1,0:T(8,128)S(1)} %get-tuple-element.34.refs_0_), channel_id=1, source_target_pairs={{0,3},{1,0},{2,1},{3,2},{4,7},{5,4},{6,5},{7,6},{8,11},{9,8},{10,9... | collective-permute-start | bytes 393224 | tf_op jit(solution)/shard_map/ppermute | solution.py:547
  21.3 11.6 %collective-permute-start.2 = (f32[400,256]{1,0:T(8,128)S(1)}, f32[400,256]{1,0:T(8,128)S(1)}, u32[]{:S(2)}, u32[]{:S(2)}) collective-permute-start(f32[400,256]{1,0:T(8,128)S(1)} %get-tuple-element.37), channel_id=1, source_target_pairs={{0,4},{4,8},{8,12},{12,16},{16,20},{20,24},{24,28},{28,0},{1,5},{5... | collective-permute-start | bytes 1228808 | tf_op jit(solution)/shard_map/ppermute | solution.py:547
  21.4 11.6 %collective-permute-start.3 = (f32[400,256]{1,0:T(8,128)S(1)}, f32[400,256]{1,0:T(8,128)S(1)}, u32[]{:S(2)}, u32[]{:S(2)}) collective-permute-start(f32[400,256]{1,0:T(8,128)S(1)} %get-tuple-element.38), channel_id=1, source_target_pairs={{0,28},{4,0},{8,4},{12,8},{16,12},{20,16},{24,20},{28,24},{1,29},{... | collective-permute-start | bytes 1228808 | tf_op jit(solution)/shard_map/ppermute | solution.py:547
  36.0 4.8 %copy-start.6 = (s32[8,512]{1,0:T(8,128)S(1)}, s32[8,512]{1,0:T(8,128)}, u32[]{:S(2)}) copy-start(s32[8,512]{1,0:T(8,128)} %refs_1_.5) | copy-start | bytes 49156
  36.1 4.8 %copy-start.8 = (s32[8]{0:T(128)S(1)}, s32[8]{0:T(128)}, u32[]{:S(2)}) copy-start(s32[8]{0:T(128)} %refs_0_.5) | copy-start | bytes 100
  36.1 10.3 %collective-permute-start.5 = (f32[328,256]{1,0:T(8,128)S(1)}, f32[328,256]{1,0:T(8,128)S(1)}, u32[]{:S(2)}, u32[]{:S(2)}) collective-permute-start(f32[328,256]{1,0:T(8,128)S(1)} %get-tuple-element.46), channel_id=1, source_target_pairs={{0,28},{4,0},{8,4},{12,8},{16,12},{20,16},{24,20},{28,24},{1,29},{... | collective-permute-start | bytes 1007624 | tf_op jit(solution)/shard_map/ppermute | solution.py:547
  38.1 9.6 %collective-permute-start.4 = (f32[328,256]{1,0:T(8,128)S(1)}, f32[328,256]{1,0:T(8,128)S(1)}, u32[]{:S(2)}, u32[]{:S(2)}) collective-permute-start(f32[328,256]{1,0:T(8,128)S(1)} %get-tuple-element.45.refs_6_), channel_id=1, source_target_pairs={{0,4},{4,8},{8,12},{12,16},{16,20},{20,24},{24,28},{28,0},{1,5},{5... | collective-permute-start | bytes 1007624 | tf_op jit(solution)/shard_map/ppermute | solution.py:547
  54.8 4.7 %collective-permute-start.8 = (f32[8,512]{1,0:T(8,128)S(1)}, f32[8,512]{1,0:T(8,128)S(1)}, u32[]{:S(2)}, u32[]{:S(2)}) collective-permute-start(f32[8,512]{1,0:T(8,128)S(1)} %get-tuple-element.52), channel_id=1, source_target_pairs={{0,2},{1,3},{2,0},{3,1},{4,6},{5,7},{6,4},{7,5},{8,10},{9,11},{10,... | collective-permute-start | bytes 49160 | tf_op jit(solution)/shard_map/ppermute | solution.py:547
  55.2 4.2 %collective-permute-start.9 = (f32[8,512]{1,0:T(8,128)S(1)}, f32[8,512]{1,0:T(8,128)S(1)}, u32[]{:S(2)}, u32[]{:S(2)}) collective-permute-start(f32[8,512]{1,0:T(8,128)S(1)} %get-tuple-element.53), channel_id=1, source_target_pairs={{0,3},{1,0},{2,1},{3,2},{4,7},{5,4},{6,5},{7,6},{8,11},{9,8},{10,9... | collective-permute-start | bytes 49160 | tf_op jit(solution)/shard_map/ppermute | solution.py:547
  57.0 5.5 %collective-permute-start.7 = (f32[8,512]{1,0:T(8,128)S(1)}, f32[8,512]{1,0:T(8,128)S(1)}, u32[]{:S(2)}, u32[]{:S(2)}) collective-permute-start(f32[8,512]{1,0:T(8,128)S(1)} %get-tuple-element.51.refs_2_), channel_id=1, source_target_pairs={{0,1},{1,2},{2,3},{3,0},{4,5},{5,6},{6,7},{7,4},{8,9},{9,10},{10,1... | collective-permute-start | bytes 49160 | tf_op jit(solution)/shard_map/ppermute | solution.py:547
  62.5 1.1 %copy-start = (f32[3,4,64,256]{3,2,1,0:T(8,128)S(1)}, f32[3,4,64,256]{3,2,1,0:T(8,128)}, u32[]{:S(2)}) copy-start(f32[3,4,64,256]{3,2,1,0:T(8,128)} %drag_field.1.refs_6_) | copy-start | bytes 2359300

commit v3 on v2

--- a/solution.py
+++ b/solution.py
@@ -39,7 +39,6 @@
 VMEM_SPEC = pl.BlockSpec(memory_space=pltpu.VMEM)
 SMEM_SPEC = pl.BlockSpec(memory_space=pltpu.SMEM)
 ANY_SPEC = pl.BlockSpec(memory_space=pl.ANY)
-HBM_SPEC = pl.BlockSpec(memory_space=pltpu.HBM)
 
 ROWS = 64
 PAD = 88
@@ -69,6 +68,10 @@
         name=name,
         **{"compiler_params": params(), **kwargs},
     )(*ins, *after)
+
+
+def in_hbm(value):
+    return pltpu.with_memory_space_constraint(value, pltpu.HBM)
 
 
 def tree(values):
@@ -166,17 +169,19 @@
 
 
 def collide_kernel(n, per, nx, pop, mask, vel, post, fwd, bwd, up, down, *rest):
-    others, (here, flags, sems) = rest[: n - 3], rest[n - 3 :]
+    others, (here, flags, speeds, sems) = rest[: n - 3], rest[n - 3 :]
     copies = [pltpu.make_async_copy(pop.at[:, x], here.at[x], sems.at[x]) for x in range(nx)]
-    copies.append(pltpu.make_async_copy(mask, flags, sems.at[nx]))
-    for copy in copies:
+    copies.append(pltpu.make_async_copy(vel, speeds, sems.at[nx]))
+    copies.append(pltpu.make_async_copy(mask, flags, sems.at[nx + 1]))
+    for copy in copies[nx:] + copies[:nx]:
         copy.start()
     me = lax.axis_index("xs")
+    copies[nx].wait()
     for d in range(1, n):
         target = lax.rem(me + d, n)
         for r in range(per):
             for c in range(3):
-                row = vel[c, pl.ds(target * per + r, 1), :]
+                row = speeds[c, pl.ds(target * per + r, 1), :]
                 for half in range(2):
                     i = (r * 3 + c) * 2 + half
                     piece = row[:, half * 256 : (half + 1) * 256]
@@ -185,7 +190,7 @@
                         ref[i // 3, 26 + i % 3 : 27 + i % 3, :] = piece
                     else:
                         others[d - 2][i : i + 1, :] = piece
-    copies[nx].wait()
+    copies[nx + 1].wait()
     for x in range(nx):
         copies[x].wait()
 
@@ -285,51 +290,44 @@
         )
 
 
-def outer_kernel(
-    nx, post, flags, before, after, post2_in, bits_in, post2, bits_out, fwd2, bwd2, halo, halo_flags
-):
-    last = nx - 1
+def outer_kernel(nx, first, post, flags, face, post2_in, bits_in, post2, bits_out, send, halo, halo_flags):
+    x, near = (0, -1) if first else (nx - 1, nx)
+    dirs, k_below, k_above = (CX_PLUS, 7, 9) if first else (CX_MINUS, 10, 8)
     e = 6 * ROWS
-    for i, (ref, dirs, far_below, far_above) in enumerate(
-        ((before, CX_PLUS, 7, 9), (after, CX_MINUS, 10, 8))
-    ):
-        for j, k in enumerate(dirs):
-            halo[i, j, 8:72, :] = ref[j * ROWS : (j + 1) * ROWS, :]
-            halo[i, j, 79:80, :] = ref[e + j : e + j + 1, :]
-            halo[i, j, 72:73, :] = ref[e + 8 + j : e + 9 + j, :]
-            if k == far_below:
-                halo[i, j, 7:8, :] = ref[e + j : e + j + 1, :]
-                halo[i, j, 78:79, :] = ref[e + 5 : e + 6, :]
-            if k == far_above:
-                halo[i, j, 73:74, :] = ref[e + 13 : e + 14, :]
-                halo[i, j, 80:81, :] = ref[j * ROWS : j * ROWS + 1, :]
-        halo_flags[i, 8:72, :] = ref[5 * ROWS : 6 * ROWS, :].astype(I32)
-        halo_flags[i, 79:80, :] = ref[e + 6 : e + 7, :].astype(I32)
-        halo_flags[i, 7:8, :] = ref[e + 6 : e + 7, :].astype(I32)
-        halo_flags[i, 78:79, :] = ref[e + 7 : e + 8, :].astype(I32)
-        halo_flags[i, 72:73, :] = ref[e + 14 : e + 15, :].astype(I32)
-        halo_flags[i, 73:74, :] = ref[e + 15 : e + 16, :].astype(I32)
-        halo_flags[i, 80:81, :] = ref[5 * ROWS : 5 * ROWS + 1, :].astype(I32)
-    for x in (0, last):
-
-        def read(k, dx, tile, x=x):
-            if x - dx < 0:
-                return halo[0, CX_PLUS.index(k), rows_of(tile), :]
-            if x - dx > last:
-                return halo[1, CX_MINUS.index(k), rows_of(tile), :]
-            return post[k, x - dx, rows_of(tile), :]
-
-        def read_mask(dx, tile, x=x):
-            if x - dx < 0 or x - dx > last:
-                return halo_flags[0 if x - dx < 0 else 1, rows_of(tile), :]
-            return flags[x - dx, rows_of(tile), :]
-
-        step_layer(x, read, read_mask, post, post2, bits_out)
-    for x, ref, dirs, k_below, k_above in ((last, fwd2, CX_PLUS, 7, 9), (0, bwd2, CX_MINUS, 10, 8)):
-        for j, k in enumerate(dirs):
-            ref[j * ROWS : (j + 1) * ROWS, :] = post2[k, x, 8:72, :]
-        ref[320:321, :] = post2[k_below, x, 79:80, :]
-        ref[321:322, :] = post2[k_above, x, 72:73, :]
+    for j, k in enumerate(dirs):
+        halo[j, 8:72, :] = face[j * ROWS : (j + 1) * ROWS, :]
+        halo[j, 79:80, :] = face[e + j : e + j + 1, :]
+        halo[j, 72:73, :] = face[e + 8 + j : e + 9 + j, :]
+        if k == k_below:
+            halo[j, 7:8, :] = face[e + j : e + j + 1, :]
+            halo[j, 78:79, :] = face[e + 5 : e + 6, :]
+        if k == k_above:
+            halo[j, 73:74, :] = face[e + 13 : e + 14, :]
+            halo[j, 80:81, :] = face[j * ROWS : j * ROWS + 1, :]
+    halo_flags[8:72, :] = face[5 * ROWS : 6 * ROWS, :].astype(I32)
+    halo_flags[79:80, :] = face[e + 6 : e + 7, :].astype(I32)
+    halo_flags[7:8, :] = face[e + 6 : e + 7, :].astype(I32)
+    halo_flags[78:79, :] = face[e + 7 : e + 8, :].astype(I32)
+    halo_flags[72:73, :] = face[e + 14 : e + 15, :].astype(I32)
+    halo_flags[73:74, :] = face[e + 15 : e + 16, :].astype(I32)
+    halo_flags[80:81, :] = face[5 * ROWS : 5 * ROWS + 1, :].astype(I32)
+
+    def read(k, dx, tile):
+        if x - dx == near:
+            return halo[dirs.index(k), rows_of(tile), :]
+        return post[k, x - dx, rows_of(tile), :]
+
+    def read_mask(dx, tile):
+        if x - dx == near:
+            return halo_flags[rows_of(tile), :]
+        return flags[x - dx, rows_of(tile), :]
+
+    step_layer(x, read, read_mask, post, post2, bits_out)
+    dirs, k_below, k_above = (CX_MINUS, 10, 8) if first else (CX_PLUS, 7, 9)
+    for j, k in enumerate(dirs):
+        send[j * ROWS : (j + 1) * ROWS, :] = post2[k, x, 8:72, :]
+    send[320:321, :] = post2[k_below, x, 79:80, :]
+    send[321:322, :] = post2[k_above, x, 72:73, :]
 
 
 def final_layer(x, read, post2, bits, result, flow, out, sem):
@@ -360,28 +358,20 @@
         copy.wait()
 
 
-def final_outer_kernel(nx, out_in, flow_in, post2, bits, before, after, out, flow, halo, result, sems):
-    last = nx - 1
-    for i, (ref, dirs, k_below, k_above) in enumerate(
-        ((before, CX_PLUS, 7, 9), (after, CX_MINUS, 10, 8))
-    ):
-        for j in range(5):
-            halo[i, j, 8:72, :] = ref[j * ROWS : (j + 1) * ROWS, :]
-        halo[i, dirs.index(k_below), 7:8, :] = ref[320:321, :]
-        halo[i, dirs.index(k_above), 72:73, :] = ref[321:322, :]
-    copies = []
-    for i, x in enumerate((0, last)):
-
-        def read(k, dx, tile, x=x):
-            if x - dx < 0:
-                return halo[0, CX_PLUS.index(k), rows_of(tile), :]
-            if x - dx > last:
-                return halo[1, CX_MINUS.index(k), rows_of(tile), :]
-            return post2[k, x - dx, rows_of(tile), :]
-
-        copies.append(final_layer(x, read, post2, bits, result.at[i], flow, out, sems.at[i]))
-    for copy in copies:
-        copy.wait()
+def final_outer_kernel(nx, first, out_in, flow_in, post2, bits, face, out, flow, halo, result, sems):
+    x, near = (0, -1) if first else (nx - 1, nx)
+    dirs, k_below, k_above = (CX_PLUS, 7, 9) if first else (CX_MINUS, 10, 8)
+    for j in range(5):
+        halo[j, 8:72, :] = face[j * ROWS : (j + 1) * ROWS, :]
+    halo[dirs.index(k_below), 7:8, :] = face[320:321, :]
+    halo[dirs.index(k_above), 72:73, :] = face[321:322, :]
+
+    def read(k, dx, tile):
+        if x - dx == near:
+            return halo[dirs.index(k), rows_of(tile), :]
+        return post2[k, x - dx, rows_of(tile), :]
+
+    final_layer(x, read, post2, bits, result, flow, out, sems.at[0]).wait()
 
 
 def pair_kernel(first_patch, pair_tiles, pos, vel, noise, *refs):
@@ -489,31 +479,49 @@
         )
 
 
-def gather_kernel(n, per, owner, voxel, flow, *refs):
-    outs, table, field = refs[:n], refs[n], refs[n + 1]
-    me = lax.axis_index("xs")
-    patches = voxel.shape[0]
-    nx = flow.shape[1]
-    rows = nx * ROWS
+def found_flow(voxel, flow, layers, field, store):
+    patches, beads = voxel.shape
+    rows = len(layers) * ROWS
     for c in range(3):
-        for x in range(nx):
+        for i, x in enumerate(layers):
             high, low = split(flow[c, x])
-            field[c, x * ROWS : (x + 1) * ROWS, 0:256] = high
-            field[c, x * ROWS : (x + 1) * ROWS, 256:512] = low
+            field[c, i * ROWS : (i + 1) * ROWS, 0:256] = high
+            field[c, i * ROWS : (i + 1) * ROWS, 256:512] = low
+    place = lax.broadcasted_iota(I32, (rows, beads), 0)
+    step = (layers[1] - layers[0] - 1) * ROWS
+    place = place + layers[0] * ROWS + jnp.where(place >= ROWS, step, 0)
     one, zero = BF16(1), BF16(0)
     for g in range(patches):
         index = voxel[g : g + 1, :]
         lanes = jnp.where(one_hot(index & 255, 256), one, zero)
         lanes2 = jnp.concatenate([lanes, lanes], axis=0)
-        at_row = lax.broadcasted_iota(I32, (rows, index.shape[1]), 0) == (index >> 8)
+        at_row = place == (index >> 8)
         for c in range(3):
             found = lax.dot_general(
                 field[c], lanes2, (((1,), (0,)), ((), ())), preferred_element_type=F32
             )
-            table[g, c : c + 1, :] = jnp.sum(jnp.where(at_row, found, 0.0), axis=0, keepdims=True)
+            store(g, c, jnp.sum(jnp.where(at_row, found, 0.0), axis=0, keepdims=True))
+
+
+def gather_middle_kernel(layers, voxel, flow, table, field):
+    def store(g, c, row):
+        table[g, c : c + 1, :] = row
+
+    found_flow(voxel, flow, layers, field, store)
+
+
+def gather_outer_kernel(n, per, layers, owner, voxel, flow, part, *refs):
+    outs, table, field = refs[:n], refs[n], refs[n + 1]
+    patches = voxel.shape[0]
+
+    def store(g, c, row):
+        table[g, c : c + 1, :] = part[g, c : c + 1, :] + row
+
+    found_flow(voxel, flow, layers, field, store)
+    me = lax.axis_index("xs")
     rank = ranks(owner, patches)
     for d in range(n):
-        target = lax.rem(me + d, n)
+        target = me ^ d
         for r in range(per):
             found = jnp.int32(0)
             for g in range(patches):
@@ -533,7 +541,7 @@
     flows, new_pos, new_vel = refs[:n], refs[n], refs[n + 1]
     me = lax.axis_index("xs")
     for d in range(n):
-        source = lax.rem(me + n - d, n)
+        source = me ^ d
         for r in range(per):
             at = pl.ds(source * per + r, 1)
             for c in range(3):
@@ -545,6 +553,11 @@
 def shift(value, axis, by):
     n = lax.axis_size(axis)
     return lax.ppermute(value, axis, [(i, (i + by) % n) for i in range(n)])
+
+
+def swap(value, axis, by):
+    n = lax.axis_size(axis)
+    return lax.ppermute(value, axis, [(i, i ^ by) for i in range(n)])
 
 
 def pair_call(first_patch, patches, pair_tiles, pos, vel, noise, given, after):
@@ -598,7 +611,7 @@
 
     post, fwd, bwd, up, down, *others = call(
         functools.partial(collide_kernel, n, per, nx),
-        [populations, fluid_mask, velocities],
+        [in_hbm(populations), in_hbm(fluid_mask), in_hbm(velocities)],
         [
             arr(19, nx, PAD, lanes),
             arr(400, lanes),
@@ -609,9 +622,9 @@
         + [arr(16, lanes)] * (n - 3),
         "collide_first",
         cost(3_000_000_000, 11_000_000),
-        specs={0: HBM_SPEC, 1: HBM_SPEC},
+        specs={0: ANY_SPEC, 1: ANY_SPEC, 2: ANY_SPEC},
         out_specs=[VMEM_SPEC] * (5 + n - 3),
-        scratch_shapes=[vmem((nx, 19, ROWS, lanes), F32), vmem((nx, ROWS, lanes), I32), dma((nx + 1,))],
+        scratch_shapes=[vmem((nx, 19, ROWS, lanes), F32), vmem((nx, ROWS, lanes), I32), vmem(velocities.shape, F32), dma((nx + 2,))],
     )
     below = shift(up, "xs", 1)
     above = shift(down, "xs", -1)
@@ -644,19 +657,23 @@
     )
     base = pair_call(half, patches - half, *bead_args, [base], [flags])
 
-    post2, bits, fwd2, bwd2 = call(
-        functools.partial(outer_kernel, nx),
-        [post, flags, before, after, post2, bits],
-        [arr(*post2.shape), ints(*bits.shape), arr(328, lanes), arr(328, lanes)],
-        "outer_layers",
-        cost(3_000_000_000, 9_000_000),
-        after=[base],
-        out_specs=[VMEM_SPEC] * 4,
-        input_output_aliases={4: 0, 5: 1},
-        scratch_shapes=[vmem((2, 5, PAD, lanes), F32), vmem((2, PAD, lanes), I32)],
-    )
+    def outer(first, face, post2, bits, after):
+        return call(
+            functools.partial(outer_kernel, nx, first),
+            [post, flags, face, post2, bits],
+            [arr(*post2.shape), ints(*bits.shape), arr(328, lanes)],
+            "first_layer" if first else "last_layer",
+            cost(1_500_000_000, 5_000_000),
+            after=after,
+            out_specs=[VMEM_SPEC] * 3,
+            input_output_aliases={3: 0, 4: 1},
+            scratch_shapes=[vmem((5, PAD, lanes), F32), vmem((PAD, lanes), I32)],
+        )
+
+    post2, bits, bwd2 = outer(True, before, post2, bits, [base])
+    after2 = shift(bwd2, "ax", -1)
+    post2, bits, fwd2 = outer(False, after, post2, bits, [])
     before2 = shift(fwd2, "ax", 1)
-    after2 = shift(bwd2, "ax", -1)
 
     out, flow = call(
         functools.partial(final_middle_kernel, nx),
@@ -678,29 +695,43 @@
         out_specs=VMEM_SPEC,
         scratch_shapes=[vmem((n, per, 8, beads), F32)],
     )
-    out, flow = call(
-        functools.partial(final_outer_kernel, nx),
-        [out, flow, post2, bits, before2, after2],
-        [arr(*populations.shape), arr(*flow.shape)],
-        "final_outer",
-        cost(3_000_000_000, 7_000_000),
-        after=[total],
-        specs={0: ANY_SPEC},
-        out_specs=[ANY_SPEC, VMEM_SPEC],
-        input_output_aliases={0: 0, 1: 1},
-        scratch_shapes=[vmem((2, 5, PAD, lanes), F32), vmem((2, 19, ROWS, lanes), F32), dma((2,))],
-    )
+    part = call(
+        functools.partial(gather_middle_kernel, list(range(1, nx - 1))),
+        [patch_voxel, flow],
+        arr(patches, 8, beads),
+        "flow_middle",
+        cost(3_000_000_000, 1_500_000),
+        out_specs=VMEM_SPEC,
+        scratch_shapes=[vmem((3, (nx - 2) * ROWS, 2 * lanes), BF16)],
+    )
+
+    def final_outer(first, face, out, flow, after):
+        return call(
+            functools.partial(final_outer_kernel, nx, first),
+            [out, flow, post2, bits, face],
+            [arr(*populations.shape), arr(*flow.shape)],
+            "final_first" if first else "final_last",
+            cost(1_500_000_000, 4_000_000),
+            after=after,
+            specs={0: ANY_SPEC},
+            out_specs=[ANY_SPEC, VMEM_SPEC],
+            input_output_aliases={0: 0, 1: 1},
+            scratch_shapes=[vmem((5, PAD, lanes), F32), vmem((19, ROWS, lanes), F32), dma((1,))],
+        )
+
+    out, flow = final_outer(False, after2, out, flow, [total, part])
+    out, flow = final_outer(True, before2, out, flow, [])
     flows = call(
-        functools.partial(gather_kernel, n, per),
-        [patch_owner, patch_voxel, flow],
+        functools.partial(gather_outer_kernel, n, per, [0, nx - 1]),
+        [patch_owner, patch_voxel, flow, part],
         [arr(8, beads)] * n,
-        "bead_flow",
+        "flow_outer",
         cost(3_000_000_000, 1_500_000),
         specs={0: SMEM_SPEC},
         out_specs=[VMEM_SPEC] * n,
-        scratch_shapes=[vmem((patches, 8, beads), F32), vmem((3, nx * ROWS, 2 * lanes), BF16)],
-    )
-    sent_flows = [flows[0]] + [shift(flows[d], "xs", d) for d in range(1, n)]
+        scratch_shapes=[vmem((patches, 8, beads), F32), vmem((3, 2 * ROWS, 2 * lanes), BF16)],
+    )
+    sent_flows = [flows[0]] + [swap(flows[d], "xs", d) for d in range(1, n)]
     field = call(
         field_kernel,
         [total, flow],
@@ -716,7 +747,6 @@
         [arr(*positions.shape)] * 2,
         "bead_update",
         cost(50_000, 300_000),
-        after=[field],
         out_specs=[VMEM_SPEC] * 2,
     )
     return out, jnp.transpose(new_pos, (1, 0, 2)), jnp.transpose(new_vel, (1, 0, 2)), field

time: 64.6 us -> 59.5 us (0.921)
  local copies, waits for them, and re-layouts: 5.31 us -> 0.04 us
  waiting for transfers between devices: 6.53 us -> 2.53 us
  Pallas kernels: 36.5 us -> 38.8 us
  starting transfers between devices: 15.1 us -> 17.1 us
    ppermute x10 -> x7, waiting for transfers between devices: 6.53 us -> 0.94 us  [shift(): return lax.ppermute(value, axis, [(i, (i + by) % n) for i in range(n)])]
    unnamed x18 -> x14, local copies, waits for them, and re-layouts: 5.31 us -> 0.04 us
    ppermute x0 -> x3, starting transfers between devices: none -> 3.55 us  [swap(): return lax.ppermute(value, axis, [(i, i ^ by) for i in range(n)])]
    pallas_call x10 -> x13, Pallas kernels: 24.7 us -> 26.9 us  [call(): pl.pallas_call(body, in_specs=[specs.get(i, VMEM_SPEC) for i in range(cou...]
    ppermute x0 -> x3, waiting for transfers between devices: none -> 1.6 us  [swap(): return lax.ppermute(value, axis, [(i, i ^ by) for i in range(n)])]
    ppermute x10 -> x7, starting transfers between devices: 15.1 us -> 13.6 us  [shift(): return lax.ppermute(value, axis, [(i, (i + by) % n) for i in range(n)])]
  transfers between devices with their start and end apart: 10 -> 10, of which waited for: 4 -> 3; matrix products, arithmetic and copies ran while one was open for 0% -> 0% of each run, Pallas kernels for 41% -> 51%
where the time goes in v3:
time: 59.5 us; the launch traced here: 59.4 us
  Pallas kernels  38.8 us (65%)
  starting transfers between devices  17.1 us (29%)
  waiting for transfers between devices  2.53 us (4%)
  between operations  0.88 us (1%)
    pallas_call x13, Pallas kernels, call(): pl.pallas_call(body, in_specs=[specs.get(i, VMEM_SPEC) for i in range(cou...  26.9 us
    ppermute x7, starting transfers between devices, shift(): return lax.ppermute(value, axis, [(i, (i + by) % n) for i in range(n)])  13.6 us
    pallas_call x2, Pallas kernels, pair_call(): pl.pallas_call(functools.partial(pair_kernel, first_patch), grid_spec=plt...  11.9 us
    ppermute x3, starting transfers between devices, swap(): return lax.ppermute(value, axis, [(i, i ^ by) for i in range(n)])  3.55 us
    ppermute x3, waiting for transfers between devices, swap(): return lax.ppermute(value, axis, [(i, i ^ by) for i in range(n)])  1.6 us
  transfers between devices with their start and end apart: 10, of which 3 were waited for; matrix products, arithmetic and copies ran while one was open for 0% of the time, Pallas kernels for 51%

profile of v3, /device:TPU:0, one launch (start us, length us, event | category | flops | bytes accessed | tf_op | source)
XLA Modules:
  0.0 59.4 jit_solution(5839372007553451103)
XLA Ops:
  0.6 0.0 copy-start.3
  0.6 0.0 copy-start.2
  0.7 0.0 copy-start.5
  0.7 0.0 copy-start.1
  0.7 3.6 %collide_first.1 = (f32[19,4,88,256]{3,2,1,0:T(8,128)S(1)}, f32[400,256]{1,0:T(8,128)S(1)}, f32[400,256]{1,0:T(8,128)S(1)}, f32[4,32,256]{2,1,0:T(8,128)S(1)}, f...) custom-call(f32[19,4,64,256]{3,2,1,0:T(8,128)} %refs_0_.4, s32[4,64,256]{2,1,0:T(8,128)} %refs_3_.1, f32[3,8,512]{2,1,0:T(8,128)} %bitcast.8), custom_call_target="tpu_custom_call" | custom-call | flops 3000000000 | bytes 11000000 | tf_op jit(solution)/shard_map/collide_first/pallas_call | solution.py:63
  4.3 0.0 copy-start
  4.3 4.1 %collective-permute-start.5 = (f32[16,256]{1,0:T(8,128)S(1)}, f32[16,256]{1,0:T(8,128)S(1)}, u32[]{:S(2)}, u32[]{:S(2)}) collective-permute-start(f32[16,256]{1,0:T(8,128)S(1)} %get-tuple-element.52), channel_id=1, source_target_pairs={{0,2},{1,3},{2,0},{3,1},{4,6},{5,7},{6,4},{7,5},{8,10},{9,11},{10,... | collective-permute-start | bytes 49160 | tf_op jit(solution)/shard_map/ppermute | solution.py:555
  8.4 1.6 %collective-permute-start = (f32[4,32,256]{2,1,0:T(8,128)S(1)}, f32[4,32,256]{2,1,0:T(8,128)S(1)}, u32[]{:S(2)}, u32[]{:S(2)}) collective-permute-start(f32[4,32,256]{2,1,0:T(8,128)S(1)} %get-tuple-element.37), channel_id=1, source_target_pairs={{0,1},{1,2},{2,3},{3,0},{4,5},{5,6},{6,7},{7,4},{8,9},{9,10},{10,1... | collective-permute-start | bytes 393224 | tf_op jit(solution)/shard_map/ppermute | solution.py:555
  10.0 2.2 %collective-permute-start.1 = (f32[4,32,256]{2,1,0:T(8,128)S(1)}, f32[4,32,256]{2,1,0:T(8,128)S(1)}, u32[]{:S(2)}, u32[]{:S(2)}) collective-permute-start(f32[4,32,256]{2,1,0:T(8,128)S(1)} %get-tuple-element.38.refs_0_), channel_id=1, source_target_pairs={{0,3},{1,0},{2,1},{3,2},{4,7},{5,4},{6,5},{7,6},{8,11},{9,8},{10,9... | collective-permute-start | bytes 393224 | tf_op jit(solution)/shard_map/ppermute | solution.py:555
  12.2 0.0 copy-done.3
  12.2 0.0 copy-done.2
  12.2 0.0 copy-done.5
  12.2 0.0 copy-done.1
  12.3 5.9 %pair_forces.2.refs_6_.refs_0_ = f32[3,8,512]{2,1,0:T(8,128)S(1)} custom-call(s32[8,2,8]{2,1,0:T(2,128)S(1)} %bitcast.12, f32[3,8,512]{2,1,0:T(8,128)S(1)} %bitcast.5, f32[3,8,512]{2,1,0:T(8,128)S(1)} %bitcast.9, bf16[8,8,128,128]{3,2,1,0:T(8,128)(2,1)S(1)} %copy-done.2, f32[4,32,256]{2,1,0:T(8,128)S(1)} %get-tuple-element.38.refs_0_), custom_call_target="tpu_custom_call" | custom-call | flops 3000000000 | bytes 1500000 | tf_op jit(solution)/shard_map/pair_forces/pallas_call | solution.py:569
  18.2 0.0 collective-permute-done.refs_4_.refs_3_
  18.2 0.0 collective-permute-done.1.refs_5_
  18.2 0.0 copy-done
  18.2 0.2 edges.1
  18.4 0.1 collective-permute-start.3
  18.5 6.0 %pair_forces.3.refs_5_.refs_1_ = f32[3,8,512]{2,1,0:T(8,128)S(1)} custom-call(s32[8,2,8]{2,1,0:T(2,128)S(1)} %bitcast.13, f32[3,8,512]{2,1,0:T(8,128)S(1)} %bitcast.6, f32[3,8,512]{2,1,0:T(8,128)S(1)} %bitcast.10, bf16[8,8,128,128]{3,2,1,0:T(8,128)(2,1)S(1)} %copy-done.2, ...), custom_call_target="tpu_custom_call", output_to_operand_aliasing={{}: (4, {})} | custom-call | flops 3000000000 | bytes 1500000 | tf_op jit(solution)/shard_map/pair_forces/pallas_call | solution.py:569
  24.4 2.7 %collective-permute-start.2 = (f32[400,256]{1,0:T(8,128)S(1)}, f32[400,256]{1,0:T(8,128)S(1)}, u32[]{:S(2)}, u32[]{:S(2)}) collective-permute-start(f32[400,256]{1,0:T(8,128)S(1)} %get-tuple-element.41), channel_id=1, source_target_pairs={{0,28},{4,0},{8,4},{12,8},{16,12},{20,16},{24,20},{28,24},{1,29},{... | collective-permute-start | bytes 1228808 | tf_op jit(solution)/shard_map/ppermute | solution.py:555
  27.1 3.0 %middle_layers.1 = (f32[19,4,88,256]{3,2,1,0:T(8,128)S(1)}, s32[4,72,256]{2,1,0:T(8,128)S(1)}) custom-call(f32[19,4,88,256]{3,2,1,0:T(8,128)S(1)} %get-tuple-element.39.refs_0_, s32[4,88,256]{2,1,0:T(8,128)S(1)} %get-tuple-element.40.refs_1_), custom_call_target="tpu_custom_call" | custom-call | flops 3000000000 | bytes 9000000 | tf_op jit(solution)/shard_map/middle_layers/pallas_call | solution.py:63
  30.1 0.0 collective-permute-done.3.refs_2_
  30.1 1.6 %first_layer.1 = (f32[19,4,88,256]{3,2,1,0:T(8,128)S(1)}, s32[4,72,256]{2,1,0:T(8,128)S(1)}, f32[328,256]{1,0:T(8,128)S(1)}) custom-call(f32[19,4,88,256]{3,2,1,0:T(8,128)S(1)} %get-tuple-element.39.refs_0_, s32[4,88,256]{2,1,0:T(8,128)S(1)} %get-tuple-element.40.refs_1_, ...), custom_call_target="tpu_custom_call", output_to_operand_aliasing={{0}: (3, {}), {1}: (4, {})} | custom-call | flops 1500000000 | bytes 5000000 | tf_op jit(solution)/shard_map/first_layer/pallas_call | solution.py:63
  31.6 0.9 %collective-permute-done.2.refs_2_ = f32[400,256]{1,0:T(8,128)S(1)} collective-permute-done((f32[400,256]{1,0:T(8,128)S(1)}, f32[400,256]{1,0:T(8,128)S(1)}, u32[]{:S(2)}, u32[]{:S(2)}) %collective-permute-start.2) | collective-permute-done | bytes 409632 | tf_op jit(solution)/shard_map/ppermute | solution.py:555
  32.6 1.5 %last_layer.1 = (f32[19,4,88,256]{3,2,1,0:T(8,128)S(1)}, s32[4,72,256]{2,1,0:T(8,128)S(1)}, f32[328,256]{1,0:T(8,128)S(1)}) custom-call(f32[19,4,88,256]{3,2,1,0:T(8,128)S(1)} %get-tuple-element.39.refs_0_, s32[4,88,256]{2,1,0:T(8,128)S(1)} %get-tuple-element.40.refs_1_, ...), custom_call_target="tpu_custom_call", output_to_operand_aliasing={{0}: (3, {}), {1}: (4, {})} | custom-call | flops 1500000000 | bytes 5000000 | tf_op jit(solution)/shard_map/last_layer/pallas_call | solution.py:63
  34.1 0.0 copy-start.4
  34.1 0.9 %collective-permute-start.6 = (f32[328,256]{1,0:T(8,128)S(1)}, f32[328,256]{1,0:T(8,128)S(1)}, u32[]{:S(2)}, u32[]{:S(2)}) collective-permute-start(f32[328,256]{1,0:T(8,128)S(1)} %get-tuple-element.53.refs_6_), channel_id=1, source_target_pairs={{0,4},{4,8},{8,12},{12,16},{16,20},{20,24},{24,28},{28,0},{1,5},{5... | collective-permute-start | bytes 1007624 | tf_op jit(solution)/shard_map/ppermute | solution.py:555
  35.1 2.0 %collective-permute-start.4 = (f32[328,256]{1,0:T(8,128)S(1)}, f32[328,256]{1,0:T(8,128)S(1)}, u32[]{:S(2)}, u32[]{:S(2)}) collective-permute-start(f32[328,256]{1,0:T(8,128)S(1)} %get-tuple-element.51), channel_id=1, source_target_pairs={{0,28},{4,0},{8,4},{12,8},{16,12},{20,16},{24,20},{28,24},{1,29},{... | collective-permute-start | bytes 1007624 | tf_op jit(solution)/shard_map/ppermute | solution.py:555
  37.0 2.8 %final_middle.1 = (f32[19,4,64,256]{3,2,1,0:T(8,128)}, f32[3,4,64,256]{3,2,1,0:T(8,128)S(1)}) custom-call(f32[19,4,88,256]{3,2,1,0:T(8,128)S(1)} %get-tuple-element.47.refs_0_.refs_2_, s32[4,72,256]{2,1,0:T(8,128)S(1)} %get-tuple-element.48.refs_1_.refs_3_), custom_call_target="tpu_custom_call" | custom-call | flops 3000000000 | bytes 7000000 | tf_op jit(solution)/shard_map/final_middle/pallas_call | solution.py:63
  39.8 0.0 copy-start.6
  39.8 0.0 copy-done.4
  39.8 1.8 %flow_middle.1.refs_6_.refs_3_ = f32[8,8,512]{2,1,0:T(8,128)S(1)} custom-call(s32[8,512]{1,0:T(8,128)S(1)} %copy-done.4, f32[3,4,64,256]{3,2,1,0:T(8,128)S(1)} %get-tuple-element.50.refs_1_), custom_call_target="tpu_custom_call" | custom-call | flops 3000000000 | bytes 1500000 | tf_op jit(solution)/shard_map/flow_middle/pallas_call | solution.py:63
  41.7 0.0 collective-permute-done.5.refs_4_
  41.7 0.0 copy-done.6
  41.7 4.5 %bead_sums.1.refs_5_.refs_0_ = f32[4,256,256]{2,1,0:T(8,128)S(1)} custom-call(s32[8]{0:T(128)S(1)} %copy-done.6, s32[8,512]{1,0:T(8,128)S(1)} %copy-done.4, f32[3,8,512]{2,1,0:T(8,128)S(1)} %bitcast.11, f32[4,32,256]{2,1,0:T(8,128)S(1)} %collective-permute-done.refs_4_.refs_3_, f32[16,256]{1,0:T(8,128)S(1)} %collective-permute-done.5.refs_4_, ...), custom_call_target="tpu_custom_call" | custom-call | flops 3000000000 | bytes 1500000 | tf_op jit(solution)/shard_map/bead_sums/pallas_call | solution.py:63
  46.2 0.0 collective-permute-done.4.refs_4_
  46.3 1.9 %final_last.1 = (f32[19,4,64,256]{3,2,1,0:T(8,128)}, f32[3,4,64,256]{3,2,1,0:T(8,128)S(1)}) custom-call(f32[19,4,64,256]{3,2,1,0:T(8,128)} %get-tuple-element.49.refs_0_, f32[3,4,64,256]{3,2,1,0:T(8,128)S(1)} %get-tuple-element.50.refs_1_, f32[19,4,88,256]{3,2,1,0:T(8,128)S(1)} %get-tuple-element.47.refs_0_.refs_2_, ...), custom_call_target="tpu_custom_call", output_to_operand_aliasing={{0}: (0, {}), {1}: (1, {})} | custom-call | flops 1500000000 | bytes 4000000 | tf_op jit(solution)/shard_map/final_last/pallas_call | solution.py:63
  48.2 0.0 collective-permute-done.6.refs_4_
  48.2 1.9 %final_first.1 = (f32[19,4,64,256]{3,2,1,0:T(8,128)}, f32[3,4,64,256]{3,2,1,0:T(8,128)S(1)}) custom-call(f32[19,4,64,256]{3,2,1,0:T(8,128)} %get-tuple-element.54.refs_0_, f32[3,4,64,256]{3,2,1,0:T(8,128)S(1)} %get-tuple-element.55.refs_1_, f32[19,4,88,256]{3,2,1,0:T(8,128)S(1)} %get-tuple-element.47.refs_0_.refs_2_, ...), custom_call_target="tpu_custom_call", output_to_operand_aliasing={{0}: (0, {}), {1}: (1, {})} | custom-call | flops 1500000000 | bytes 4000000 | tf_op jit(solution)/shard_map/final_first/pallas_call | solution.py:63
  50.1 2.5 %flow_outer.1 = (f32[8,512]{1,0:T(8,128)S(1)}, f32[8,512]{1,0:T(8,128)S(1)}, f32[8,512]{1,0:T(8,128)S(1)}, f32[8,512]{1,0:T(8,128)S(1)}) custom-call(s32[8]{0:T(128)S(1)} %copy-done.6, s32[8,512]{1,0:T(8,128)S(1)} %copy-done.4, f32[3,4,64,256]{3,2,1,0:T(8,128)S(1)} %get-tuple-element.57.refs_2_.refs_1_, f32[8,8,512]{2,1,0:T(8,128)S(1)} %flow_middle.1.refs_6_.refs_3_), custom_call_target="tpu_custom_call" | custom-call | flops 3000000000 | bytes 1500000 | tf_op jit(solution)/shard_map/flow_outer/pallas_call | solution.py:63
  52.6 0.4 collective-permute-start.8
  53.0 1.8 %collective-permute-start.9 = (f32[8,512]{1,0:T(8,128)S(1)}, f32[8,512]{1,0:T(8,128)S(1)}, u32[]{:S(2)}, u32[]{:S(2)}) collective-permute-start(f32[8,512]{1,0:T(8,128)S(1)} %get-tuple-element.61), channel_id=1, source_target_pairs={{0,3},{1,2},{2,1},{3,0},{4,7},{5,6},{6,5},{7,4},{8,11},{9,10},{10,... | collective-permute-start | bytes 49160 | tf_op jit(solution)/shard_map/ppermute | solution.py:560
  54.8 1.3 %collective-permute-start.7 = (f32[8,512]{1,0:T(8,128)S(1)}, f32[8,512]{1,0:T(8,128)S(1)}, u32[]{:S(2)}, u32[]{:S(2)}) collective-permute-start(f32[8,512]{1,0:T(8,128)S(1)} %get-tuple-element.59.refs_2_), channel_id=1, source_target_pairs={{0,1},{1,0},{2,3},{3,2},{4,5},{5,4},{6,7},{7,6},{8,9},{9,8},{10,11... | collective-permute-start | bytes 49160 | tf_op jit(solution)/shard_map/ppermute | solution.py:560
  56.1 1.0 %drag_field.1 = f32[3,4,64,256]{3,2,1,0:T(8,128)} custom-call(f32[4,256,256]{2,1,0:T(8,128)S(1)} %bead_sums.1.refs_5_.refs_0_, f32[3,4,64,256]{3,2,1,0:T(8,128)S(1)} %get-tuple-element.57.refs_2_.refs_1_, f32[8,512]{1,0:T(8,128)S(1)} %get-tuple-element.59.refs_2_), custom_call_target="tpu_custom_call" | custom-call | flops 400000000 | bytes 2500000 | tf_op jit(solution)/shard_map/drag_field/pallas_call | solution.py:63
  57.1 0.2 collective-permute-done.8.refs_4_
  57.3 1.4 %collective-permute-done.9.refs_5_ = f32[8,512]{1,0:T(8,128)S(1)} collective-permute-done((f32[8,512]{1,0:T(8,128)S(1)}, f32[8,512]{1,0:T(8,128)S(1)}, u32[]{:S(2)}, u32[]{:S(2)}) %collective-permute-start.9) | collective-permute-done | bytes 16416 | tf_op jit(solution)/shard_map/ppermute | solution.py:560
  58.7 0.0 collective-permute-done.7.refs_3_
  58.7 0.7 %bead_update.1 = (f32[3,8,512]{2,1,0:T(8,128)}, f32[3,8,512]{2,1,0:T(8,128)}) custom-call(f32[3,8,512]{2,1,0:T(8,128)S(1)} %bitcast.7, f32[3,8,512]{2,1,0:T(8,128)S(1)} %pair_forces.3.refs_5_.refs_1_, f32[8,512]{1,0:T(8,128)S(1)} %get-tuple-element.58.refs_2_, f32[8,512]{1,0:T(8,128)S(1)} %collective-permute-done.7.refs_3_, ...), custom_call_target="tpu_custom_call" | custom-call | flops 50000 | bytes 300000 | tf_op jit(solution)/shard_map/bead_update/pallas_call | solution.py:63
Async XLA Ops:
  0.6 11.6 %copy-start.3 = (f32[8,3,512]{2,0,1:T(8,128)S(1)}, f32[8,3,512]{2,0,1:T(8,128)}, u32[]{:S(2)}) copy-start(f32[8,3,512]{2,0,1:T(8,128)} %param.13) | copy-start | bytes 147460
  0.6 11.6 %copy-start.2 = (bf16[8,8,128,128]{3,2,1,0:T(8,128)(2,1)S(1)}, bf16[8,8,128,128]{3,2,1,0:T(8,128)(2,1)}, u32[]{:S(2)}) copy-start(bf16[8,8,128,128]{3,2,1,0:T(8,128)(2,1)} %noise.3) | copy-start | bytes 6291460
  0.7 11.6 %copy-start.5 = (s32[8,8,2]{1,2,0:T(2,128)S(1)}, s32[8,8,2]{1,2,0:T(2,128)}, u32[]{:S(2)}) copy-start(s32[8,8,2]{1,2,0:T(2,128)} %param.14) | copy-start | bytes 1540
  0.7 11.6 %copy-start.1 = (f32[8,3,512]{2,0,1:T(8,128)S(1)}, f32[8,3,512]{2,0,1:T(8,128)}, u32[]{:S(2)}) copy-start(f32[8,3,512]{2,0,1:T(8,128)} %param.12) | copy-start | bytes 147460
  4.3 13.9 %copy-start = (s32[4,64,256]{2,1,0:T(8,128)S(1)}, s32[4,64,256]{2,1,0:T(8,128)}, u32[]{:S(2)}) copy-start(s32[4,64,256]{2,1,0:T(8,128)} %refs_3_.1) | copy-start | bytes 786436
  4.3 37.4 %collective-permute-start.5 = (f32[16,256]{1,0:T(8,128)S(1)}, f32[16,256]{1,0:T(8,128)S(1)}, u32[]{:S(2)}, u32[]{:S(2)}) collective-permute-start(f32[16,256]{1,0:T(8,128)S(1)} %get-tuple-element.52), channel_id=1, source_target_pairs={{0,2},{1,3},{2,0},{3,1},{4,6},{5,7},{6,4},{7,5},{8,10},{9,11},{10,... | collective-permute-start | bytes 49160 | tf_op jit(solution)/shard_map/ppermute | solution.py:555
  8.4 9.8 %collective-permute-start = (f32[4,32,256]{2,1,0:T(8,128)S(1)}, f32[4,32,256]{2,1,0:T(8,128)S(1)}, u32[]{:S(2)}, u32[]{:S(2)}) collective-permute-start(f32[4,32,256]{2,1,0:T(8,128)S(1)} %get-tuple-element.37), channel_id=1, source_target_pairs={{0,1},{1,2},{2,3},{3,0},{4,5},{5,6},{6,7},{7,4},{8,9},{9,10},{10,1... | collective-permute-start | bytes 393224 | tf_op jit(solution)/shard_map/ppermute | solution.py:555
  10.0 8.2 %collective-permute-start.1 = (f32[4,32,256]{2,1,0:T(8,128)S(1)}, f32[4,32,256]{2,1,0:T(8,128)S(1)}, u32[]{:S(2)}, u32[]{:S(2)}) collective-permute-start(f32[4,32,256]{2,1,0:T(8,128)S(1)} %get-tuple-element.38.refs_0_), channel_id=1, source_target_pairs={{0,3},{1,0},{2,1},{3,2},{4,7},{5,4},{6,5},{7,6},{8,11},{9,8},{10,9... | collective-permute-start | bytes 393224 | tf_op jit(solution)/shard_map/ppermute | solution.py:555
  18.4 11.7 %collective-permute-start.3 = (f32[400,256]{1,0:T(8,128)S(1)}, f32[400,256]{1,0:T(8,128)S(1)}, u32[]{:S(2)}, u32[]{:S(2)}) collective-permute-start(f32[400,256]{1,0:T(8,128)S(1)} %get-tuple-element.42), channel_id=1, source_target_pairs={{0,4},{4,8},{8,12},{12,16},{16,20},{20,24},{24,28},{28,0},{1,5},{5... | collective-permute-start | bytes 1228808 | tf_op jit(solution)/shard_map/ppermute | solution.py:555
  24.4 8.1 %collective-permute-start.2 = (f32[400,256]{1,0:T(8,128)S(1)}, f32[400,256]{1,0:T(8,128)S(1)}, u32[]{:S(2)}, u32[]{:S(2)}) collective-permute-start(f32[400,256]{1,0:T(8,128)S(1)} %get-tuple-element.41), channel_id=1, source_target_pairs={{0,28},{4,0},{8,4},{12,8},{16,12},{20,16},{24,20},{28,24},{1,29},{... | collective-permute-start | bytes 1228808 | tf_op jit(solution)/shard_map/ppermute | solution.py:555
  34.1 5.7 %copy-start.4 = (s32[8,512]{1,0:T(8,128)S(1)}, s32[8,512]{1,0:T(8,128)}, u32[]{:S(2)}) copy-start(s32[8,512]{1,0:T(8,128)} %refs_1_.5) | copy-start | bytes 49156
  34.1 14.1 %collective-permute-start.6 = (f32[328,256]{1,0:T(8,128)S(1)}, f32[328,256]{1,0:T(8,128)S(1)}, u32[]{:S(2)}, u32[]{:S(2)}) collective-permute-start(f32[328,256]{1,0:T(8,128)S(1)} %get-tuple-element.53.refs_6_), channel_id=1, source_target_pairs={{0,4},{4,8},{8,12},{12,16},{16,20},{20,24},{24,28},{28,0},{1,5},{5... | collective-permute-start | bytes 1007624 | tf_op jit(solution)/shard_map/ppermute | solution.py:555
  35.1 11.2 %collective-permute-start.4 = (f32[328,256]{1,0:T(8,128)S(1)}, f32[328,256]{1,0:T(8,128)S(1)}, u32[]{:S(2)}, u32[]{:S(2)}) collective-permute-start(f32[328,256]{1,0:T(8,128)S(1)} %get-tuple-element.51), channel_id=1, source_target_pairs={{0,28},{4,0},{8,4},{12,8},{16,12},{20,16},{24,20},{28,24},{1,29},{... | collective-permute-start | bytes 1007624 | tf_op jit(solution)/shard_map/ppermute | solution.py:555
  39.8 1.9 %copy-start.6 = (s32[8]{0:T(128)S(1)}, s32[8]{0:T(128)}, u32[]{:S(2)}) copy-start(s32[8]{0:T(128)} %refs_0_.7) | copy-start | bytes 100
  52.6 4.7 %collective-permute-start.8 = (f32[8,512]{1,0:T(8,128)S(1)}, f32[8,512]{1,0:T(8,128)S(1)}, u32[]{:S(2)}, u32[]{:S(2)}) collective-permute-start(f32[8,512]{1,0:T(8,128)S(1)} %get-tuple-element.60), channel_id=1, source_target_pairs={{0,2},{1,3},{2,0},{3,1},{4,6},{5,7},{6,4},{7,5},{8,10},{9,11},{10,... | collective-permute-start | bytes 49160 | tf_op jit(solution)/shard_map/ppermute | solution.py:560
  53.0 5.6 %collective-permute-start.9 = (f32[8,512]{1,0:T(8,128)S(1)}, f32[8,512]{1,0:T(8,128)S(1)}, u32[]{:S(2)}, u32[]{:S(2)}) collective-permute-start(f32[8,512]{1,0:T(8,128)S(1)} %get-tuple-element.61), channel_id=1, source_target_pairs={{0,3},{1,2},{2,1},{3,0},{4,7},{5,6},{6,5},{7,4},{8,11},{9,10},{10,... | collective-permute-start | bytes 49160 | tf_op jit(solution)/shard_map/ppermute | solution.py:560
  54.8 3.9 %collective-permute-start.7 = (f32[8,512]{1,0:T(8,128)S(1)}, f32[8,512]{1,0:T(8,128)S(1)}, u32[]{:S(2)}, u32[]{:S(2)}) collective-permute-start(f32[8,512]{1,0:T(8,128)S(1)} %get-tuple-element.59.refs_2_), channel_id=1, source_target_pairs={{0,1},{1,0},{2,3},{3,2},{4,5},{5,4},{6,7},{7,6},{8,9},{9,8},{10,11... | collective-permute-start | bytes 49160 | tf_op jit(solution)/shard_map/ppermute | solution.py:560

commit v4 on v3

--- a/solution.py
+++ b/solution.py
@@ -169,14 +169,24 @@
 
 
 def collide_kernel(n, per, nx, pop, mask, vel, post, fwd, bwd, up, down, *rest):
-    others, (here, flags, speeds, sems) = rest[: n - 3], rest[n - 3 :]
-    copies = [pltpu.make_async_copy(pop.at[:, x], here.at[x], sems.at[x]) for x in range(nx)]
-    copies.append(pltpu.make_async_copy(vel, speeds, sems.at[nx]))
-    copies.append(pltpu.make_async_copy(mask, flags, sems.at[nx + 1]))
-    for copy in copies[nx:] + copies[:nx]:
+    others, (here, flags, speeds, sems, small) = rest[: n - 3], rest[n - 3 :]
+    order = [(x, h) for x in [0, nx - 1] + list(range(1, nx - 1)) for h in range(1)]
+    span = ROWS // 1
+    copies = [
+        pltpu.make_async_copy(
+            pop.at[:, x, pl.ds(h * span, span)], here.at[x, :, pl.ds(h * span, span)], sems.at[i]
+        )
+        for i, (x, h) in enumerate(order)
+    ]
+    extra = [
+        pltpu.make_async_copy(vel, speeds, small.at[0]),
+        pltpu.make_async_copy(mask, flags, small.at[1]),
+    ]
+    ahead = 3
+    for copy in copies[:ahead] + extra:
         copy.start()
     me = lax.axis_index("xs")
-    copies[nx].wait()
+    extra[0].wait()
     for d in range(1, n):
         target = lax.rem(me + d, n)
         for r in range(per):
@@ -190,19 +200,21 @@
                         ref[i // 3, 26 + i % 3 : 27 + i % 3, :] = piece
                     else:
                         others[d - 2][i : i + 1, :] = piece
-    copies[nx + 1].wait()
-    for x in range(nx):
-        copies[x].wait()
-
-        def body(t, carry, x=x):
-            rows = tile_rows(t)
-            out = collide([here[x, k, rows, :] for k in range(19)])
+    extra[1].wait()
+    for i, (x, h) in enumerate(order):
+        copies[i].wait()
+        if i + ahead < len(copies):
+            copies[i + ahead].start()
+
+        def body(t, carry, x=x, h=h):
+            t = t + h * (TILES // 1)
+            out = collide([here[x, k, tile_rows(t), :] for k in range(19)])
             for k in range(19):
                 post[k, x, rows_of(t), :] = out[k]
             return carry
 
-        lax.fori_loop(0, TILES, body, 0)
-        for ref, near, beyond, dirs in ((up, ROWS - 1, ROWS - 2, CY_PLUS), (down, 0, 1, CY_MINUS)):
+        lax.fori_loop(0, TILES // 1, body, 0, unroll=TILES // 1)
+        for ref, near, beyond, dirs in ((down, 0, 1, CY_MINUS), (up, ROWS - 1, ROWS - 2, CY_PLUS)):
             for k in range(19):
                 ref[x, k : k + 1, :] = post[k, x, 8 + near : 9 + near, :]
             for j, k in enumerate(dirs):
@@ -226,7 +238,7 @@
     return jnp.concatenate(out, axis=1)
 
 
-def edges_kernel(n, nx, post_in, fwd_in, bwd_in, mask, below, above, post, fwd, bwd, flags):
+def edges_kernel(n, nx, post_in, mask, below, above, post, fwd, bwd, flags):
     me = lax.axis_index("xs")
     has_below, has_above = (me > 0).astype(F32), (me < n - 1).astype(F32)
     for x in range(nx):
@@ -251,16 +263,15 @@
         (fwd, nx - 1, CX_PLUS, 7, 9),
         (bwd, 0, CX_MINUS, 10, 8),
     ):
-        e = 6 * ROWS
         for j, k in enumerate(dirs):
-            rows[e + j : e + j + 1, :] = below[x, k : k + 1, :]
-            rows[e + 8 + j : e + 9 + j, :] = above[x, k : k + 1, :]
+            rows[j : j + 1, :] = below[x, k : k + 1, :]
+            rows[8 + j : 9 + j, :] = above[x, k : k + 1, :]
         j = 19 + CY_PLUS.index(far_below)
-        rows[e + 5 : e + 6, :] = below[x, j : j + 1, :]
+        rows[5:6, :] = below[x, j : j + 1, :]
         j = 19 + CY_MINUS.index(far_above)
-        rows[e + 13 : e + 14, :] = above[x, j : j + 1, :]
-        rows[e + 6 : e + 8, :] = below[x, 24:26, :] * has_below
-        rows[e + 14 : e + 16, :] = above[x, 24:26, :] * has_above
+        rows[13:14, :] = above[x, j : j + 1, :]
+        rows[6:8, :] = below[x, 24:26, :] * has_below
+        rows[14:16, :] = above[x, 24:26, :] * has_above
 
 
 def step_layer(x, read, read_mask, post, post2, bits_out):
@@ -273,7 +284,7 @@
         bits_out[x, tile_rows(t), :] = bits
         return carry
 
-    lax.fori_loop(0, TILES + 1, body, 0)
+    lax.fori_loop(0, TILES + 1, body, 0, unroll=TILES + 1)
     for k in CY_PLUS:
         post2[k, x, 7:8, :] = post2[k, x, 79:80, :]
 
@@ -290,26 +301,27 @@
         )
 
 
-def outer_kernel(nx, first, post, flags, face, post2_in, bits_in, post2, bits_out, send, halo, halo_flags):
+def outer_kernel(
+    nx, first, post, flags, face, edge, post2_in, bits_in, post2, bits_out, send, halo, halo_flags
+):
     x, near = (0, -1) if first else (nx - 1, nx)
     dirs, k_below, k_above = (CX_PLUS, 7, 9) if first else (CX_MINUS, 10, 8)
-    e = 6 * ROWS
     for j, k in enumerate(dirs):
         halo[j, 8:72, :] = face[j * ROWS : (j + 1) * ROWS, :]
-        halo[j, 79:80, :] = face[e + j : e + j + 1, :]
-        halo[j, 72:73, :] = face[e + 8 + j : e + 9 + j, :]
+        halo[j, 79:80, :] = edge[j : j + 1, :]
+        halo[j, 72:73, :] = edge[8 + j : 9 + j, :]
         if k == k_below:
-            halo[j, 7:8, :] = face[e + j : e + j + 1, :]
-            halo[j, 78:79, :] = face[e + 5 : e + 6, :]
+            halo[j, 7:8, :] = edge[j : j + 1, :]
+            halo[j, 78:79, :] = edge[5:6, :]
         if k == k_above:
-            halo[j, 73:74, :] = face[e + 13 : e + 14, :]
+            halo[j, 73:74, :] = edge[13:14, :]
             halo[j, 80:81, :] = face[j * ROWS : j * ROWS + 1, :]
     halo_flags[8:72, :] = face[5 * ROWS : 6 * ROWS, :].astype(I32)
-    halo_flags[79:80, :] = face[e + 6 : e + 7, :].astype(I32)
-    halo_flags[7:8, :] = face[e + 6 : e + 7, :].astype(I32)
-    halo_flags[78:79, :] = face[e + 7 : e + 8, :].astype(I32)
-    halo_flags[72:73, :] = face[e + 14 : e + 15, :].astype(I32)
-    halo_flags[73:74, :] = face[e + 15 : e + 16, :].astype(I32)
+    halo_flags[79:80, :] = edge[6:7, :].astype(I32)
+    halo_flags[7:8, :] = edge[6:7, :].astype(I32)
+    halo_flags[78:79, :] = edge[7:8, :].astype(I32)
+    halo_flags[72:73, :] = edge[14:15, :].astype(I32)
+    halo_flags[73:74, :] = edge[15:16, :].astype(I32)
     halo_flags[80:81, :] = face[5 * ROWS : 5 * ROWS + 1, :].astype(I32)
 
     def read(k, dx, tile):
@@ -343,86 +355,131 @@
         flow[2, x, rows, :] = uz
         return carry
 
-    lax.fori_loop(0, TILES, body, 0)
+    lax.fori_loop(0, TILES, body, 0, unroll=TILES)
     copy = pltpu.make_async_copy(result, out.at[:, x], sem)
     copy.start()
     return copy
 
 
-def final_middle_kernel(nx, post2, bits, out, flow, result, sems):
+def final_middle_kernel(nx, post2, bits, voxel, out, flow, table, result, field, sems):
     copies = []
     for i, x in enumerate(range(1, nx - 1)):
         read = lambda k, dx, tile, x=x: post2[k, x - dx, rows_of(tile), :]
         copies.append(final_layer(x, read, post2, bits, result.at[i], flow, out, sems.at[i]))
+
+    def store(g, c, row):
+        table[g, c : c + 1, :] = row
+
+    found_flow(voxel, flow, list(range(1, nx - 1)), field, store)
     for copy in copies:
         copy.wait()
 
 
-def final_outer_kernel(nx, first, out_in, flow_in, post2, bits, face, out, flow, halo, result, sems):
-    x, near = (0, -1) if first else (nx - 1, nx)
-    dirs, k_below, k_above = (CX_PLUS, 7, 9) if first else (CX_MINUS, 10, 8)
-    for j in range(5):
-        halo[j, 8:72, :] = face[j * ROWS : (j + 1) * ROWS, :]
-    halo[dirs.index(k_below), 7:8, :] = face[320:321, :]
-    halo[dirs.index(k_above), 72:73, :] = face[321:322, :]
-
-    def read(k, dx, tile):
-        if x - dx == near:
-            return halo[dirs.index(k), rows_of(tile), :]
-        return post2[k, x - dx, rows_of(tile), :]
-
-    final_layer(x, read, post2, bits, result, flow, out, sems.at[0]).wait()
-
-
-def pair_kernel(first_patch, pair_tiles, pos, vel, noise, *refs):
+def final_outer_kernel(
+    n, per, nx, out_in, flow_in, post2, bits, after, before, voxel, owner, part, out, flow, *refs
+):
+    outs, (halo, result, table, field, sems) = refs[:n], refs[n:]
+    copies = []
+    for i, (face, first) in enumerate(((after, False), (before, True))):
+        x, near = (0, -1) if first else (nx - 1, nx)
+        dirs, k_below, k_above = (CX_PLUS, 7, 9) if first else (CX_MINUS, 10, 8)
+        for j in range(5):
+            halo[i, j, 8:72, :] = face[j * ROWS : (j + 1) * ROWS, :]
+        halo[i, dirs.index(k_below), 7:8, :] = face[320:321, :]
+        halo[i, dirs.index(k_above), 72:73, :] = face[321:322, :]
+
+        def read(k, dx, tile, i=i, x=x, near=near, dirs=dirs):
+            if x - dx == near:
+                return halo[i, dirs.index(k), rows_of(tile), :]
+            return post2[k, x - dx, rows_of(tile), :]
+
+        copies.append(final_layer(x, read, post2, bits, result.at[i], flow, out, sems.at[i]))
+
+    def store(g, c, row):
+        table[g, c : c + 1, :] = part[g, c : c + 1, :] + row
+
+    found_flow(voxel, flow, [0, nx - 1], field, store)
+    patches = voxel.shape[0]
+    me = lax.axis_index("xs")
+    rank = ranks(owner, patches)
+    for d in range(n):
+        target = me ^ d
+        for r in range(per):
+            found = jnp.int32(0)
+            for g in range(patches):
+                found = jnp.where((owner[g] == target) & (rank[g] == r), g, found)
+            outs[d][r * 3 : r * 3 + 3, :] = table[found, 0:3, :]
+    for copy in copies:
+        copy.wait()
+
+
+def pair_kernel(begin, end, pair_tiles, pos, vel, noise, *refs):
     base, rows, cols, theta, acc = refs[-5:]
-    g = pl.program_id(0) + first_patch
     tile = noise.shape[-1]
     count = pos.shape[-1] // tile
     pairs = noise.shape[1]
-    both = [ref[c, pl.ds(g, 1), :] for ref in (pos, vel) for c in range(3)]
-    speed = both[3:]
-    both = [both[c] if c < 3 else 4.5 * both[c] for c in range(6)]
-    stacked = jnp.concatenate(both + [jnp.zeros((2, both[0].shape[1]), F32)], axis=0)
-    turned = stacked.T
-    for c in range(6):
-        for j in range(count):
-            part = turned[j * tile : (j + 1) * tile, c : c + 1]
-            cols[c, j] = jnp.broadcast_to(part, (tile, tile))
-            rows[c, j] = jnp.broadcast_to(both[c][:, j * tile : (j + 1) * tile], (8, tile))
-    acc[...] = jnp.zeros_like(acc)
+    patches = end - begin
+    spread = (lax.broadcasted_iota(I32, (24, 6 * tile), 0) & 7) == (
+        lax.broadcasted_iota(I32, (24, 6 * tile), 1) // tile
+    )
+    spread = jnp.where(spread, 1.0, 0.0).astype(BF16)
     eye = lax.broadcasted_iota(I32, (tile, tile), 0) == lax.broadcasted_iota(I32, (tile, tile), 1)
     scale = jnp.where(eye, 15.0, 0.0).astype(BF16)
-    for p in range(pairs):
-        theta[p] = lax.dot_general(
-            scale, noise[0, p], (((1,), (1,)), ((), ())), preferred_element_type=F32
-        )
-
-    def one_pair(p, carry):
-        first = pair_tiles[g, 0, p]
-        second = pair_tiles[g, 1, p]
-        mine = [rows[c, first] for c in range(6)]
-        parts = []
+    empty = jnp.zeros((2, pos.shape[-1]), F32)
+    parts, speeds = [], []
+    for g in range(patches):
+        both = [ref[c, begin + g : begin + g + 1, :] for ref in (pos, vel) for c in range(3)]
+        speeds.append(both[3:])
+        both = [both[c] if c < 3 else 4.5 * both[c] for c in range(6)]
+        for c in range(6):
+            for j in range(count):
+                rows[g, c, j] = jnp.broadcast_to(both[c][:, j * tile : (j + 1) * tile], (8, tile))
+        stacked = jnp.concatenate(both + [empty], axis=0)
+        high, rest = stacked.astype(BF16), stacked - stacked.astype(BF16).astype(F32)
+        mid, low = rest.astype(BF16), rest - rest.astype(BF16).astype(F32)
+        parts += [high.astype(F32), mid.astype(F32), low]
+    used = 24 * patches
+    parts.append(jnp.zeros((-used % 128, pos.shape[-1]), F32))
+    parts = jnp.concatenate(parts, axis=0).T.astype(BF16)
+    acc[...] = jnp.zeros_like(acc)
+    for g in range(patches):
+        for j in range(count):
+            left = parts[j * tile : (j + 1) * tile, 24 * g : 24 * (g + 1)]
+            wide = jnp.dot(left, spread, preferred_element_type=F32)
+            for c in range(6):
+                cols[g, c, j] = wide[:, c * tile : (c + 1) * tile]
+        for p in range(pairs):
+            theta[g * pairs + p] = lax.dot_general(
+                scale, noise[begin + g, p], (((1,), (1,)), ((), ())), preferred_element_type=F32
+            )
+
+    def one_pair(i, carry):
+        g, p = i // pairs, i % pairs
+        first = pair_tiles[begin + g, 0, p]
+        second = pair_tiles[begin + g, 1, p]
+        mine = [rows[g, c, first] for c in range(6)]
+        total = []
         for s in range(tile // 8):
             part = slice(8 * s, 8 * s + 8)
-            dx, dy, dz = [mine[c] - cols[c, second, part, :] for c in range(3)]
-            vx, vy, vz = [mine[c] - cols[c, second, part, :] for c in range(3, 6)]
+            dx, dy, dz = [mine[c] - cols[g, c, second, part, :] for c in range(3)]
+            vx, vy, vz = [mine[c] - cols[g, c, second, part, :] for c in range(3, 6)]
             square = (dx * dx + 0.01) + (dy * dy + dz * dz)
             close = jnp.maximum(lax.rsqrt(square) - 1.0, 0.0)
             along = dx * vx + (dy * vy + dz * vz)
-            force = close * ((theta[p, part, :] + 25.0) - close * along)
+            force = close * ((theta[i, part, :] + 25.0) - close * along)
             here = [force * dx, force * dy, force * dz]
-            parts = here if not parts else [a + b for a, b in zip(parts, here)]
+            total = here if not total else [a + b for a, b in zip(total, here)]
         for c in range(3):
-            acc[first, c] += parts[c]
+            acc[g, first, c] += total[c]
         return carry
 
-    lax.fori_loop(0, pairs, one_pair, 0)
-    for c in range(3):
-        force = jnp.concatenate(
-            [jnp.sum(acc[j, c], axis=0, keepdims=True) for j in range(count)], axis=1
-        )
-        base[c, pl.ds(g, 1), :] = 0.5 * speed[c] + 0.04 * force
+    lax.fori_loop(0, patches * pairs, one_pair, 0, unroll=4)
+    for g in range(patches):
+        for c in range(3):
+            force = jnp.concatenate(
+                [jnp.sum(acc[g, j, c], axis=0, keepdims=True) for j in range(count)], axis=1
+            )
+            base[c, begin + g : begin + g + 1, :] = 0.5 * speeds[g][c] + 0.04 * force
 
 
 def split(value):
@@ -503,32 +560,6 @@
             store(g, c, jnp.sum(jnp.where(at_row, found, 0.0), axis=0, keepdims=True))
 
 
-def gather_middle_kernel(layers, voxel, flow, table, field):
-    def store(g, c, row):
-        table[g, c : c + 1, :] = row
-
-    found_flow(voxel, flow, layers, field, store)
-
-
-def gather_outer_kernel(n, per, layers, owner, voxel, flow, part, *refs):
-    outs, table, field = refs[:n], refs[n], refs[n + 1]
-    patches = voxel.shape[0]
-
-    def store(g, c, row):
-        table[g, c : c + 1, :] = part[g, c : c + 1, :] + row
-
-    found_flow(voxel, flow, layers, field, store)
-    me = lax.axis_index("xs")
-    rank = ranks(owner, patches)
-    for d in range(n):
-        target = me ^ d
-        for r in range(per):
-            found = jnp.int32(0)
-            for g in range(patches):
-                found = jnp.where((owner[g] == target) & (rank[g] == r), g, found)
-            outs[d][r * 3 : r * 3 + 3, :] = table[found, 0:3, :]
-
-
 def field_kernel(total, flow, field):
     for x in range(field.shape[1]):
         rows = slice(x * ROWS, (x + 1) * ROWS)
@@ -560,38 +591,26 @@
     return lax.ppermute(value, axis, [(i, i ^ by) for i in range(n)])
 
 
-def pair_call(first_patch, patches, pair_tiles, pos, vel, noise, given, after):
-    beads = pos.shape[2]
+def pair_call(begin, end, pair_tiles, pos, vel, noise, given, after):
     tile = noise.shape[-1]
-    count = beads // tile
-    whole = lambda g, s: (0, 0, 0)
-    ins = [pos, vel, noise] + given + after
-    return pl.pallas_call(
-        functools.partial(pair_kernel, first_patch),
-        grid_spec=pltpu.PrefetchScalarGridSpec(
-            num_scalar_prefetch=1,
-            grid=(patches,),
-            in_specs=[
-                pl.BlockSpec(pos.shape, whole),
-                pl.BlockSpec(vel.shape, whole),
-                pl.BlockSpec((1,) + noise.shape[1:], lambda g, s: (g + first_patch, 0, 0, 0)),
-            ]
-            + [pl.BlockSpec(pos.shape, whole)] * len(given)
-            + [ANY_SPEC] * len(after),
-            out_specs=pl.BlockSpec(pos.shape, whole),
-            scratch_shapes=[
-                pltpu.VMEM((6, count, 8, tile), F32),
-                pltpu.VMEM((6, count, tile, tile), F32),
-                pltpu.VMEM(noise.shape[1:], F32),
-                pltpu.VMEM((count, 3, 8, tile), F32),
-            ],
-        ),
-        out_shape=jax.ShapeDtypeStruct(pos.shape, F32),
+    count = pos.shape[2] // tile
+    return call(
+        functools.partial(pair_kernel, begin, end),
+        [pair_tiles, pos, vel, noise] + given,
+        jax.ShapeDtypeStruct(pos.shape, F32),
+        "pair_forces",
+        cost(1000, 1000),
+        after=after,
+        specs={0: SMEM_SPEC},
+        out_specs=VMEM_SPEC,
         input_output_aliases={4: 0} if given else {},
-        compiler_params=params(),
-        cost_estimate=cost(3_000_000_000, 1_500_000),
-        name="pair_forces",
-    )(pair_tiles, *ins)
+        scratch_shapes=[
+            pltpu.VMEM((end - begin, 6, count, 8, tile), F32),
+            pltpu.VMEM((end - begin, 6, count, tile, tile), F32),
+            pltpu.VMEM(((end - begin) * noise.shape[1], tile, tile), F32),
+            pltpu.VMEM((end - begin, count, 3, 8, tile), F32),
+        ],
+    )
 
 
 def per_device(
@@ -612,20 +631,23 @@
     post, fwd, bwd, up, down, *others = call(
         functools.partial(collide_kernel, n, per, nx),
         [in_hbm(populations), in_hbm(fluid_mask), in_hbm(velocities)],
-        [
-            arr(19, nx, PAD, lanes),
-            arr(400, lanes),
-            arr(400, lanes),
-            arr(nx, 32, lanes),
-            arr(nx, 32, lanes),
-        ]
+        [arr(19, nx, PAD, lanes), arr(384, lanes), arr(384, lanes)]
+        + [arr(nx, 32, lanes)] * 2
         + [arr(16, lanes)] * (n - 3),
         "collide_first",
         cost(3_000_000_000, 11_000_000),
         specs={0: ANY_SPEC, 1: ANY_SPEC, 2: ANY_SPEC},
-        out_specs=[VMEM_SPEC] * (5 + n - 3),
-        scratch_shapes=[vmem((nx, 19, ROWS, lanes), F32), vmem((nx, ROWS, lanes), I32), vmem(velocities.shape, F32), dma((nx + 2,))],
-    )
+        out_specs=[VMEM_SPEC] * (n + 2),
+        scratch_shapes=[
+            vmem((nx, 19, ROWS, lanes), F32),
+            vmem((nx, ROWS, lanes), I32),
+            vmem(velocities.shape, F32),
+            dma((2 * nx,)),
+            dma((2,)),
+        ],
+    )
+    before = shift(fwd, "ax", 1)
+    after = shift(bwd, "ax", -1)
     below = shift(up, "xs", 1)
     above = shift(down, "xs", -1)
     sent = [below] + [shift(other, "xs", d + 2) for d, other in enumerate(others)] + [above]
@@ -634,102 +656,89 @@
     bead_args = (pair_tiles, positions, velocities, pair_noise)
     base = pair_call(0, half, *bead_args, [], [down])
 
-    post, fwd, bwd, flags = call(
+    post, edge_fwd, edge_bwd, flags = call(
         functools.partial(edges_kernel, n, nx),
-        [post, fwd, bwd, fluid_mask, below, above],
-        [arr(*post.shape), arr(*fwd.shape), arr(*bwd.shape), ints(nx, PAD, lanes)],
+        [post, fluid_mask, below, above],
+        [arr(*post.shape), arr(16, lanes), arr(16, lanes), ints(nx, PAD, lanes)],
         "edges",
-        cost(1000, 100_000),
-        after=[base],
+        cost(1000, 1000),
+        after=[base] + sent[1:-1],
         out_specs=[VMEM_SPEC] * 4,
-        input_output_aliases={0: 0, 1: 1, 2: 2},
-    )
-    before = shift(fwd, "ax", 1)
-    after = shift(bwd, "ax", -1)
+        input_output_aliases={0: 0},
+    )
+    edge_before = shift(edge_fwd, "ax", 1)
+    edge_after = shift(edge_bwd, "ax", -1)
 
     post2, bits = call(
         functools.partial(middle_kernel, nx),
         [post, flags],
         [arr(19, nx, PAD, lanes), ints(nx, 72, lanes)],
         "middle_layers",
-        cost(3_000_000_000, 9_000_000),
+        cost(1000, 1000),
         out_specs=[VMEM_SPEC] * 2,
     )
-    base = pair_call(half, patches - half, *bead_args, [base], [flags])
-
-    def outer(first, face, post2, bits, after):
+    base = pair_call(half, patches, *bead_args, [base], [flags])
+
+    def outer(first, face, edge, post2, bits, after):
         return call(
             functools.partial(outer_kernel, nx, first),
-            [post, flags, face, post2, bits],
+            [post, flags, face, edge, post2, bits],
             [arr(*post2.shape), ints(*bits.shape), arr(328, lanes)],
             "first_layer" if first else "last_layer",
-            cost(1_500_000_000, 5_000_000),
+            cost(1000, 1000),
             after=after,
             out_specs=[VMEM_SPEC] * 3,
-            input_output_aliases={3: 0, 4: 1},
+            input_output_aliases={4: 0, 5: 1},
             scratch_shapes=[vmem((5, PAD, lanes), F32), vmem((PAD, lanes), I32)],
         )
 
-    post2, bits, bwd2 = outer(True, before, post2, bits, [base])
+    post2, bits, bwd2 = outer(True, before, edge_before, post2, bits, [base, after, edge_after])
     after2 = shift(bwd2, "ax", -1)
-    post2, bits, fwd2 = outer(False, after, post2, bits, [])
+    post2, bits, fwd2 = outer(False, after, edge_after, post2, bits, [])
     before2 = shift(fwd2, "ax", 1)
 
-    out, flow = call(
+    out, flow, part = call(
         functools.partial(final_middle_kernel, nx),
-        [post2, bits],
-        [arr(*populations.shape), arr(3, nx, ROWS, lanes)],
+        [post2, bits, patch_voxel],
+        [arr(*populations.shape), arr(3, nx, ROWS, lanes), arr(patches, 8, beads)],
         "final_middle",
-        cost(3_000_000_000, 7_000_000),
-        out_specs=[ANY_SPEC, VMEM_SPEC],
-        scratch_shapes=[vmem((nx - 2, 19, ROWS, lanes), F32), dma((nx - 2,))],
+        cost(1000, 1000),
+        after=[fwd2],
+        out_specs=[ANY_SPEC, VMEM_SPEC, VMEM_SPEC],
+        scratch_shapes=[
+            vmem((nx - 2, 19, ROWS, lanes), F32),
+            vmem((3, (nx - 2) * ROWS, 2 * lanes), BF16),
+            dma((nx - 2,)),
+        ],
     )
     total = call(
         functools.partial(scatter_kernel, n, per),
         [patch_owner, patch_voxel, velocities] + sent,
         arr(4, nx * ROWS, lanes),
         "bead_sums",
-        cost(3_000_000_000, 1_500_000),
+        cost(1000, 1000),
         after=[fwd2],
         specs={0: SMEM_SPEC},
         out_specs=VMEM_SPEC,
         scratch_shapes=[vmem((n, per, 8, beads), F32)],
     )
-    part = call(
-        functools.partial(gather_middle_kernel, list(range(1, nx - 1))),
-        [patch_voxel, flow],
-        arr(patches, 8, beads),
-        "flow_middle",
-        cost(3_000_000_000, 1_500_000),
-        out_specs=VMEM_SPEC,
-        scratch_shapes=[vmem((3, (nx - 2) * ROWS, 2 * lanes), BF16)],
-    )
-
-    def final_outer(first, face, out, flow, after):
-        return call(
-            functools.partial(final_outer_kernel, nx, first),
-            [out, flow, post2, bits, face],
-            [arr(*populations.shape), arr(*flow.shape)],
-            "final_first" if first else "final_last",
-            cost(1_500_000_000, 4_000_000),
-            after=after,
-            specs={0: ANY_SPEC},
-            out_specs=[ANY_SPEC, VMEM_SPEC],
-            input_output_aliases={0: 0, 1: 1},
-            scratch_shapes=[vmem((5, PAD, lanes), F32), vmem((19, ROWS, lanes), F32), dma((1,))],
-        )
-
-    out, flow = final_outer(False, after2, out, flow, [total, part])
-    out, flow = final_outer(True, before2, out, flow, [])
-    flows = call(
-        functools.partial(gather_outer_kernel, n, per, [0, nx - 1]),
-        [patch_owner, patch_voxel, flow, part],
-        [arr(8, beads)] * n,
-        "flow_outer",
-        cost(3_000_000_000, 1_500_000),
-        specs={0: SMEM_SPEC},
-        out_specs=[VMEM_SPEC] * n,
-        scratch_shapes=[vmem((patches, 8, beads), F32), vmem((3, 2 * ROWS, 2 * lanes), BF16)],
+    out, flow, *flows = call(
+        functools.partial(final_outer_kernel, n, per, nx),
+        [out, flow, post2, bits, after2, before2, patch_voxel, patch_owner, part],
+        [arr(*populations.shape), arr(*flow.shape)] + [arr(8, beads)] * n,
+        "final_outer",
+        cost(1000, 1000),
+        after=[total],
+        specs={0: ANY_SPEC, 7: SMEM_SPEC},
+        out_specs=[ANY_SPEC] + [VMEM_SPEC] * (n + 1),
+        input_output_aliases={0: 0, 1: 1},
+        scratch_shapes=[
+            vmem((2, 5, PAD, lanes), F32),
+            vmem((2, 19, ROWS, lanes), F32),
+            vmem((patches, 8, beads), F32),
+            vmem((3, 2 * ROWS, 2 * lanes), BF16),
+            dma((2,)),
+        ],
     )
     sent_flows = [flows[0]] + [swap(flows[d], "xs", d) for d in range(1, n)]
     field = call(
@@ -737,7 +746,7 @@
         [total, flow],
         arr(3, nx, ROWS, lanes),
         "drag_field",
-        cost(400_000_000, 2_500_000),
+        cost(1000, 1000),
         after=[flows[1]],
         out_specs=VMEM_SPEC,
     )
@@ -746,7 +755,7 @@
         [positions, base] + sent_flows,
         [arr(*positions.shape)] * 2,
         "bead_update",
-        cost(50_000, 300_000),
+        cost(1000, 1000),
         out_specs=[VMEM_SPEC] * 2,
     )
     return out, jnp.transpose(new_pos, (1, 0, 2)), jnp.transpose(new_vel, (1, 0, 2)), field

time: 59.5 us -> 51.1 us (0.86)
  Pallas kernels: 38.8 us -> 29.9 us
  waiting for transfers between devices: 2.53 us -> 3.91 us
  starting transfers between devices: 17.1 us -> 16.4 us
    pallas_call x2 -> x0, Pallas kernels: 11.9 us -> none  [pair_call(): pl.pallas_call(functools.partial(pair_kernel, first_patch), grid_spec=plt...]
    pallas_call x13 -> x12, Pallas kernels: 26.9 us -> 29.9 us  [call(): pl.pallas_call(body, in_specs=[specs.get(i, VMEM_SPEC) for i in range(cou...]
    ppermute x7 -> x9, waiting for transfers between devices: 0.94 us -> 1.83 us  [shift(): return lax.ppermute(value, axis, [(i, (i + by) % n) for i in range(n)])]
    ppermute x7 -> x9, starting transfers between devices: 13.6 us -> 12.8 us  [shift(): return lax.ppermute(value, axis, [(i, (i + by) % n) for i in range(n)])]
  transfers between devices with their start and end apart: 10 -> 12, of which waited for: 3 -> 4; matrix products, arithmetic and copies ran while one was open for 0% -> 0% of each run, Pallas kernels for 51% -> 37%
where the time goes in v4:
time: 51.1 us; the launch traced here: 51 us
  Pallas kernels  29.9 us (59%)
  starting transfers between devices  16.4 us (32%)
  waiting for transfers between devices  3.91 us (8%)
  between operations  0.81 us (2%)
    pallas_call x12, Pallas kernels, call(): pl.pallas_call(body, in_specs=[specs.get(i, VMEM_SPEC) for i in range(cou...  29.9 us
    ppermute x9, starting transfers between devices, shift(): return lax.ppermute(value, axis, [(i, (i + by) % n) for i in range(n)])  12.8 us
    ppermute x3, starting transfers between devices, swap(): return lax.ppermute(value, axis, [(i, i ^ by) for i in range(n)])  3.55 us
    ppermute x3, waiting for transfers between devices, swap(): return lax.ppermute(value, axis, [(i, i ^ by) for i in range(n)])  2.08 us
    ppermute x9, waiting for transfers between devices, shift(): return lax.ppermute(value, axis, [(i, (i + by) % n) for i in range(n)])  1.83 us
  transfers between devices with their start and end apart: 12, of which 4 were waited for; matrix products, arithmetic and copies ran while one was open for 0% of the time, Pallas kernels for 37%

profile of v4, /device:TPU:0, one launch (start us, length us, event | category | flops | bytes accessed | tf_op | source)
XLA Modules:
  0.0 51.0 jit_solution(9552405429901775836)
XLA Ops:
  0.6 0.0 copy-start.3
  0.6 0.0 copy-start.1
  0.7 0.0 copy-start
  0.7 0.0 copy-start.5
  0.7 0.0 copy-start.2
  0.7 4.1 %collide_first.1 = (f32[19,4,88,256]{3,2,1,0:T(8,128)S(1)}, f32[384,256]{1,0:T(8,128)S(1)}, f32[384,256]{1,0:T(8,128)S(1)}, f32[4,32,256]{2,1,0:T(8,128)S(1)}, f...) custom-call(f32[19,4,64,256]{3,2,1,0:T(8,128)} %refs_0_.2, s32[4,64,256]{2,1,0:T(8,128)} %refs_1_.4, f32[3,8,512]{2,1,0:T(8,128)} %bitcast.5), custom_call_target="tpu_custom_call" | custom-call | flops 3000000000 | bytes 11000000 | tf_op jit(solution)/shard_map/collide_first/pallas_call | solution.py:63
  4.8 3.4 %collective-permute-start.3 = (f32[384,256]{1,0:T(8,128)S(1)}, f32[384,256]{1,0:T(8,128)S(1)}, u32[]{:S(2)}, u32[]{:S(2)}) collective-permute-start(f32[384,256]{1,0:T(8,128)S(1)} %get-tuple-element.39), channel_id=1, source_target_pairs={{0,28},{4,0},{8,4},{12,8},{16,12},{20,16},{24,20},{28,24},{1,29},{... | collective-permute-start | bytes 1179656 | tf_op jit(solution)/shard_map/ppermute | solution.py:586
  8.2 0.0 collective-permute-start.5
  8.2 1.6 %collective-permute-start = (f32[4,32,256]{2,1,0:T(8,128)S(1)}, f32[4,32,256]{2,1,0:T(8,128)S(1)}, u32[]{:S(2)}, u32[]{:S(2)}) collective-permute-start(f32[4,32,256]{2,1,0:T(8,128)S(1)} %get-tuple-element.34), channel_id=1, source_target_pairs={{0,1},{1,2},{2,3},{3,0},{4,5},{5,6},{6,7},{7,4},{8,9},{9,10},{10,1... | collective-permute-start | bytes 393224 | tf_op jit(solution)/shard_map/ppermute | solution.py:586
  9.8 2.2 %collective-permute-start.1 = (f32[4,32,256]{2,1,0:T(8,128)S(1)}, f32[4,32,256]{2,1,0:T(8,128)S(1)}, u32[]{:S(2)}, u32[]{:S(2)}) collective-permute-start(f32[4,32,256]{2,1,0:T(8,128)S(1)} %get-tuple-element.35.refs_4_), channel_id=1, source_target_pairs={{0,3},{1,0},{2,1},{3,2},{4,7},{5,4},{6,5},{7,6},{8,11},{9,8},{10,9... | collective-permute-start | bytes 393224 | tf_op jit(solution)/shard_map/ppermute | solution.py:586
  12.0 0.8 %collective-permute-start.2 = (f32[16,256]{1,0:T(8,128)S(1)}, f32[16,256]{1,0:T(8,128)S(1)}, u32[]{:S(2)}, u32[]{:S(2)}) collective-permute-start(f32[16,256]{1,0:T(8,128)S(1)} %get-tuple-element.36), channel_id=1, source_target_pairs={{0,2},{1,3},{2,0},{3,1},{4,6},{5,7},{6,4},{7,5},{8,10},{9,11},{10,... | collective-permute-start | bytes 49160 | tf_op jit(solution)/shard_map/ppermute | solution.py:586
  12.8 0.0 copy-done.1
  12.8 0.0 copy-done
  12.8 0.0 copy-done.5
  12.8 0.0 copy-done.2
  12.8 4.6 %pair_forces.2.refs_4_ = f32[3,8,512]{2,1,0:T(8,128)S(1)} custom-call(s32[8,2,8]{2,1,0:T(2,128)S(1)} %bitcast.12, f32[3,8,512]{2,1,0:T(8,128)S(1)} %bitcast.9, f32[3,8,512]{2,1,0:T(8,128)S(1)} %bitcast.6, bf16[8,8,128,128]{3,2,1,0:T(8,128)(2,1)S(1)} %copy-done, f32[4,32,256]{2,1,0:T(8,128)S(1)} %get-tuple-element.35.refs_4_), custom_call_target="tpu_custom_call" | custom-call | flops 1000 | bytes 1000 | tf_op jit(solution)/shard_map/pair_forces/pallas_call | solution.py:63
  17.4 1.3 %collective-permute-done.2.refs_5_.refs_4_ = f32[16,256]{1,0:T(8,128)S(1)} collective-permute-done((f32[16,256]{1,0:T(8,128)S(1)}, f32[16,256]{1,0:T(8,128)S(1)}, u32[]{:S(2)}, u32[]{:S(2)}) %collective-permute-start.2) | collective-permute-done | bytes 16416 | tf_op jit(solution)/shard_map/ppermute | solution.py:586
  18.7 0.0 collective-permute-done.refs_2_.refs_3_
  18.7 0.0 collective-permute-done.1.refs_3_.refs_5_
  18.7 0.0 copy-done.3
  18.7 0.2 edges.1
  18.9 1.9 %collective-permute-start.4 = (f32[16,256]{1,0:T(8,128)S(1)}, f32[16,256]{1,0:T(8,128)S(1)}, u32[]{:S(2)}, u32[]{:S(2)}) collective-permute-start(f32[16,256]{1,0:T(8,128)S(1)} %get-tuple-element.40), channel_id=1, source_target_pairs={{0,28},{4,0},{8,4},{12,8},{16,12},{20,16},{24,20},{28,24},{1,29},{... | collective-permute-start | bytes 49160 | tf_op jit(solution)/shard_map/ppermute | solution.py:586
  20.8 0.0 collective-permute-start.6
  20.8 4.6 %pair_forces.3.refs_6_.refs_1_ = f32[3,8,512]{2,1,0:T(8,128)S(1)} custom-call(s32[8,2,8]{2,1,0:T(2,128)S(1)} %bitcast.13, f32[3,8,512]{2,1,0:T(8,128)S(1)} %bitcast.10, f32[3,8,512]{2,1,0:T(8,128)S(1)} %bitcast.7, bf16[8,8,128,128]{3,2,1,0:T(8,128)(2,1)S(1)} %copy-done, f32[3,8,512]{2,1,0:T(8,128)S(1)} %pair_forces.2.refs_4_, ...), custom_call_target="tpu_custom_call", output_to_operand_aliasing={{}: (4, {})} | custom-call | flops 1000 | bytes 1000 | tf_op jit(solution)/shard_map/pair_forces/pallas_call | solution.py:63
  25.4 1.6 %middle_layers.1 = (f32[19,4,88,256]{3,2,1,0:T(8,128)S(1)}, s32[4,72,256]{2,1,0:T(8,128)S(1)}) custom-call(f32[19,4,88,256]{3,2,1,0:T(8,128)S(1)} %get-tuple-element.37.refs_0_, s32[4,88,256]{2,1,0:T(8,128)S(1)} %get-tuple-element.38.refs_1_.refs_5_), custom_call_target="tpu_custom_call" | custom-call | flops 1000 | bytes 1000 | tf_op jit(solution)/shard_map/middle_layers/pallas_call | solution.py:63
  27.0 0.0 collective-permute-done.4.refs_8_.refs_3_
  27.0 0.0 collective-permute-done.6.refs_3_
  27.1 0.0 collective-permute-done.3.refs_7_.refs_2_
  27.1 0.0 collective-permute-done.5.refs_2_
  27.1 0.9 %first_layer.1 = (f32[19,4,88,256]{3,2,1,0:T(8,128)S(1)}, s32[4,72,256]{2,1,0:T(8,128)S(1)}, f32[328,256]{1,0:T(8,128)S(1)}) custom-call(f32[19,4,88,256]{3,2,1,0:T(8,128)S(1)} %get-tuple-element.37.refs_0_, s32[4,88,256]{2,1,0:T(8,128)S(1)} %get-tuple-element.38.refs_1_.refs_5_, ...), custom_call_target="tpu_custom_call", output_to_operand_aliasing={{0}: (4, {}), {1}: (5, {})} | custom-call | flops 1000 | bytes 1000 | tf_op jit(solution)/shard_map/first_layer/pallas_call | solution.py:63
  28.0 0.0 copy-start.4
  28.0 0.9 %last_layer.1 = (f32[19,4,88,256]{3,2,1,0:T(8,128)S(1)}, s32[4,72,256]{2,1,0:T(8,128)S(1)}, f32[328,256]{1,0:T(8,128)S(1)}) custom-call(f32[19,4,88,256]{3,2,1,0:T(8,128)S(1)} %get-tuple-element.37.refs_0_, s32[4,88,256]{2,1,0:T(8,128)S(1)} %get-tuple-element.38.refs_1_.refs_5_, ...), custom_call_target="tpu_custom_call", output_to_operand_aliasing={{0}: (4, {}), {1}: (5, {})} | custom-call | flops 1000 | bytes 1000 | tf_op jit(solution)/shard_map/last_layer/pallas_call | solution.py:63
  28.9 0.0 copy-start.6
  28.9 0.1 collective-permute-start.8
  28.9 2.9 %collective-permute-start.7 = (f32[328,256]{1,0:T(8,128)S(1)}, f32[328,256]{1,0:T(8,128)S(1)}, u32[]{:S(2)}, u32[]{:S(2)}) collective-permute-start(f32[328,256]{1,0:T(8,128)S(1)} %get-tuple-element.52), channel_id=1, source_target_pairs={{0,28},{4,0},{8,4},{12,8},{16,12},{20,16},{24,20},{28,24},{1,29},{... | collective-permute-start | bytes 1007624 | tf_op jit(solution)/shard_map/ppermute | solution.py:586
  31.8 0.0 copy-done.4
  31.8 2.5 %final_middle.1 = (f32[19,4,64,256]{3,2,1,0:T(8,128)}, f32[3,4,64,256]{3,2,1,0:T(8,128)S(1)}, f32[8,8,512]{2,1,0:T(8,128)S(1)}) custom-call(f32[19,4,88,256]{3,2,1,0:T(8,128)S(1)} %get-tuple-element.47.refs_0_.refs_2_, s32[4,72,256]{2,1,0:T(8,128)S(1)} %get-tuple-element.48.refs_1_.refs_3_, s32[8,512]{1,0:T(8,128)S(1)} %copy-done.4, ...), custom_call_target="tpu_custom_call" | custom-call | flops 1000 | bytes 1000 | tf_op jit(solution)/shard_map/final_middle/pallas_call | solution.py:63
  34.3 0.0 copy-done.6
  34.3 4.5 %bead_sums.1.refs_9_.refs_0_ = f32[4,256,256]{2,1,0:T(8,128)S(1)} custom-call(s32[8]{0:T(128)S(1)} %copy-done.6, s32[8,512]{1,0:T(8,128)S(1)} %copy-done.4, f32[3,8,512]{2,1,0:T(8,128)S(1)} %bitcast.8, f32[4,32,256]{2,1,0:T(8,128)S(1)} %collective-permute-done.refs_2_.refs_3_, f32[16,256]{1,0:T(8,128)S(1)} %collective-permute-done.2.refs_5_.refs_4_, ...), custom_call_target="tpu_custom_call" | custom-call | flops 1000 | bytes 1000 | tf_op jit(solution)/shard_map/bead_sums/pallas_call | solution.py:63
  38.9 0.5 %collective-permute-done.8.refs_5_ = f32[328,256]{1,0:T(8,128)S(1)} collective-permute-done((f32[328,256]{1,0:T(8,128)S(1)}, f32[328,256]{1,0:T(8,128)S(1)}, u32[]{:S(2)}, u32[]{:S(2)}) %collective-permute-start.8) | collective-permute-done | bytes 335904 | tf_op jit(solution)/shard_map/ppermute | solution.py:586
  39.4 0.0 collective-permute-done.7.refs_4_
  39.4 4.3 %final_outer.1 = (f32[19,4,64,256]{3,2,1,0:T(8,128)}, f32[3,4,64,256]{3,2,1,0:T(8,128)S(1)}, f32[8,512]{1,0:T(8,128)S(1)}, f32[8,512]{1,0:T(8,128)S(1)}, f32[8,512]{1,0:T(8,128)S(1)}, /*index=5*/f32[8,512]{1,0:T(8,128)S(1)}) custom-call(f32[19,4,64,256]{3,2,1,0:T(8,128)} %get-tuple-element.50.refs_0_, ...), custom_call_target="tpu_custom_call", output_to_operand_aliasing={{0}: (0, {}), {1}: (1, {})} | custom-call | flops 1000 | bytes 1000 | tf_op jit(solution)/shard_map/final_outer/pallas_call | solution.py:63
  43.7 1.0 %collective-permute-start.10 = (f32[8,512]{1,0:T(8,128)S(1)}, f32[8,512]{1,0:T(8,128)S(1)}, u32[]{:S(2)}, u32[]{:S(2)}) collective-permute-start(f32[8,512]{1,0:T(8,128)S(1)} %get-tuple-element.57), channel_id=1, source_target_pairs={{0,2},{1,3},{2,0},{3,1},{4,6},{5,7},{6,4},{7,5},{8,10},{9,11},{10,... | collective-permute-start | bytes 49160 | tf_op jit(solution)/shard_map/ppermute | solution.py:591
  44.6 1.8 %collective-permute-start.11 = (f32[8,512]{1,0:T(8,128)S(1)}, f32[8,512]{1,0:T(8,128)S(1)}, u32[]{:S(2)}, u32[]{:S(2)}) collective-permute-start(f32[8,512]{1,0:T(8,128)S(1)} %get-tuple-element.58), channel_id=1, source_target_pairs={{0,3},{1,2},{2,1},{3,0},{4,7},{5,6},{6,5},{7,4},{8,11},{9,10},{10,... | collective-permute-start | bytes 49160 | tf_op jit(solution)/shard_map/ppermute | solution.py:591
  46.4 0.8 %collective-permute-start.9 = (f32[8,512]{1,0:T(8,128)S(1)}, f32[8,512]{1,0:T(8,128)S(1)}, u32[]{:S(2)}, u32[]{:S(2)}) collective-permute-start(f32[8,512]{1,0:T(8,128)S(1)} %get-tuple-element.56.refs_2_), channel_id=1, source_target_pairs={{0,1},{1,0},{2,3},{3,2},{4,5},{5,4},{6,7},{7,6},{8,9},{9,8},{10,11... | collective-permute-start | bytes 49160 | tf_op jit(solution)/shard_map/ppermute | solution.py:591
  47.2 1.0 %drag_field.1 = f32[3,4,64,256]{3,2,1,0:T(8,128)} custom-call(f32[4,256,256]{2,1,0:T(8,128)S(1)} %bead_sums.1.refs_9_.refs_0_, f32[3,4,64,256]{3,2,1,0:T(8,128)S(1)} %get-tuple-element.61.refs_1_, f32[8,512]{1,0:T(8,128)S(1)} %get-tuple-element.56.refs_2_), custom_call_target="tpu_custom_call" | custom-call | flops 1000 | bytes 1000 | tf_op jit(solution)/shard_map/drag_field/pallas_call | solution.py:63
  48.2 0.1 collective-permute-done.10.refs_4_
  48.4 1.9 %collective-permute-done.11.refs_5_ = f32[8,512]{1,0:T(8,128)S(1)} collective-permute-done((f32[8,512]{1,0:T(8,128)S(1)}, f32[8,512]{1,0:T(8,128)S(1)}, u32[]{:S(2)}, u32[]{:S(2)}) %collective-permute-start.11) | collective-permute-done | bytes 16416 | tf_op jit(solution)/shard_map/ppermute | solution.py:591
  50.3 0.0 collective-permute-done.9.refs_3_
  50.3 0.7 %bead_update.1 = (f32[3,8,512]{2,1,0:T(8,128)}, f32[3,8,512]{2,1,0:T(8,128)}) custom-call(f32[3,8,512]{2,1,0:T(8,128)S(1)} %bitcast.11, f32[3,8,512]{2,1,0:T(8,128)S(1)} %pair_forces.3.refs_6_.refs_1_, f32[8,512]{1,0:T(8,128)S(1)} %get-tuple-element.55.refs_2_, f32[8,512]{1,0:T(8,128)S(1)} %collective-permute-done.9.refs_3_, ...), custom_call_target="tpu_custom_call" | custom-call | flops 1000 | bytes 1000 | tf_op jit(solution)/shard_map/bead_update/pallas_call | solution.py:63
Async XLA Ops:
  0.6 18.1 %copy-start.3 = (s32[4,64,256]{2,1,0:T(8,128)S(1)}, s32[4,64,256]{2,1,0:T(8,128)}, u32[]{:S(2)}) copy-start(s32[4,64,256]{2,1,0:T(8,128)} %refs_1_.4) | copy-start | bytes 786436
  0.6 12.2 %copy-start.1 = (f32[8,3,512]{2,0,1:T(8,128)S(1)}, f32[8,3,512]{2,0,1:T(8,128)}, u32[]{:S(2)}) copy-start(f32[8,3,512]{2,0,1:T(8,128)} %param.13) | copy-start | bytes 147460
  0.7 12.1 %copy-start = (bf16[8,8,128,128]{3,2,1,0:T(8,128)(2,1)S(1)}, bf16[8,8,128,128]{3,2,1,0:T(8,128)(2,1)}, u32[]{:S(2)}) copy-start(bf16[8,8,128,128]{3,2,1,0:T(8,128)(2,1)} %refs_3_.3) | copy-start | bytes 6291460
  0.7 12.1 %copy-start.5 = (s32[8,8,2]{1,2,0:T(2,128)S(1)}, s32[8,8,2]{1,2,0:T(2,128)}, u32[]{:S(2)}) copy-start(s32[8,8,2]{1,2,0:T(2,128)} %param.14) | copy-start | bytes 1540
  0.7 12.1 %copy-start.2 = (f32[8,3,512]{2,0,1:T(8,128)S(1)}, f32[8,3,512]{2,0,1:T(8,128)}, u32[]{:S(2)}) copy-start(f32[8,3,512]{2,0,1:T(8,128)} %param.12) | copy-start | bytes 147460
  4.8 22.3 %collective-permute-start.3 = (f32[384,256]{1,0:T(8,128)S(1)}, f32[384,256]{1,0:T(8,128)S(1)}, u32[]{:S(2)}, u32[]{:S(2)}) collective-permute-start(f32[384,256]{1,0:T(8,128)S(1)} %get-tuple-element.39), channel_id=1, source_target_pairs={{0,28},{4,0},{8,4},{12,8},{16,12},{20,16},{24,20},{28,24},{1,29},{... | collective-permute-start | bytes 1179656 | tf_op jit(solution)/shard_map/ppermute | solution.py:586
  8.2 18.9 %collective-permute-start.5 = (f32[384,256]{1,0:T(8,128)S(1)}, f32[384,256]{1,0:T(8,128)S(1)}, u32[]{:S(2)}, u32[]{:S(2)}) collective-permute-start(f32[384,256]{1,0:T(8,128)S(1)} %get-tuple-element.41), channel_id=1, source_target_pairs={{0,4},{4,8},{8,12},{12,16},{16,20},{20,24},{24,28},{28,0},{1,5},{5... | collective-permute-start | bytes 1179656 | tf_op jit(solution)/shard_map/ppermute | solution.py:586
  8.2 10.6 %collective-permute-start = (f32[4,32,256]{2,1,0:T(8,128)S(1)}, f32[4,32,256]{2,1,0:T(8,128)S(1)}, u32[]{:S(2)}, u32[]{:S(2)}) collective-permute-start(f32[4,32,256]{2,1,0:T(8,128)S(1)} %get-tuple-element.34), channel_id=1, source_target_pairs={{0,1},{1,2},{2,3},{3,0},{4,5},{5,6},{6,7},{7,4},{8,9},{9,10},{10,1... | collective-permute-start | bytes 393224 | tf_op jit(solution)/shard_map/ppermute | solution.py:586
  9.8 9.0 %collective-permute-start.1 = (f32[4,32,256]{2,1,0:T(8,128)S(1)}, f32[4,32,256]{2,1,0:T(8,128)S(1)}, u32[]{:S(2)}, u32[]{:S(2)}) collective-permute-start(f32[4,32,256]{2,1,0:T(8,128)S(1)} %get-tuple-element.35.refs_4_), channel_id=1, source_target_pairs={{0,3},{1,0},{2,1},{3,2},{4,7},{5,4},{6,5},{7,6},{8,11},{9,8},{10,9... | collective-permute-start | bytes 393224 | tf_op jit(solution)/shard_map/ppermute | solution.py:586
  12.0 6.7 %collective-permute-start.2 = (f32[16,256]{1,0:T(8,128)S(1)}, f32[16,256]{1,0:T(8,128)S(1)}, u32[]{:S(2)}, u32[]{:S(2)}) collective-permute-start(f32[16,256]{1,0:T(8,128)S(1)} %get-tuple-element.36), channel_id=1, source_target_pairs={{0,2},{1,3},{2,0},{3,1},{4,6},{5,7},{6,4},{7,5},{8,10},{9,11},{10,... | collective-permute-start | bytes 49160 | tf_op jit(solution)/shard_map/ppermute | solution.py:586
  18.9 8.1 %collective-permute-start.4 = (f32[16,256]{1,0:T(8,128)S(1)}, f32[16,256]{1,0:T(8,128)S(1)}, u32[]{:S(2)}, u32[]{:S(2)}) collective-permute-start(f32[16,256]{1,0:T(8,128)S(1)} %get-tuple-element.40), channel_id=1, source_target_pairs={{0,28},{4,0},{8,4},{12,8},{16,12},{20,16},{24,20},{28,24},{1,29},{... | collective-permute-start | bytes 49160 | tf_op jit(solution)/shard_map/ppermute | solution.py:586
  20.8 6.3 %collective-permute-start.6 = (f32[16,256]{1,0:T(8,128)S(1)}, f32[16,256]{1,0:T(8,128)S(1)}, u32[]{:S(2)}, u32[]{:S(2)}) collective-permute-start(f32[16,256]{1,0:T(8,128)S(1)} %get-tuple-element.42), channel_id=1, source_target_pairs={{0,4},{4,8},{8,12},{12,16},{16,20},{20,24},{24,28},{28,0},{1,5},{5... | collective-permute-start | bytes 49160 | tf_op jit(solution)/shard_map/ppermute | solution.py:586
  28.0 3.9 %copy-start.4 = (s32[8,512]{1,0:T(8,128)S(1)}, s32[8,512]{1,0:T(8,128)}, u32[]{:S(2)}) copy-start(s32[8,512]{1,0:T(8,128)} %refs_6_.1) | copy-start | bytes 49156
  28.9 5.4 %copy-start.6 = (s32[8]{0:T(128)S(1)}, s32[8]{0:T(128)}, u32[]{:S(2)}) copy-start(s32[8]{0:T(128)} %refs_7_.1) | copy-start | bytes 100
  28.9 10.5 %collective-permute-start.8 = (f32[328,256]{1,0:T(8,128)S(1)}, f32[328,256]{1,0:T(8,128)S(1)}, u32[]{:S(2)}, u32[]{:S(2)}) collective-permute-start(f32[328,256]{1,0:T(8,128)S(1)} %get-tuple-element.49.refs_3_.refs_6_), channel_id=1, source_target_pairs={{0,4},{4,8},{8,12},{12,16},{16,20},{20,24},{24,28},{28,0},{1,5},{5... | collective-permute-start | bytes 1007624 | tf_op jit(solution)/shard_map/ppermute | solution.py:586
  28.9 10.4 %collective-permute-start.7 = (f32[328,256]{1,0:T(8,128)S(1)}, f32[328,256]{1,0:T(8,128)S(1)}, u32[]{:S(2)}, u32[]{:S(2)}) collective-permute-start(f32[328,256]{1,0:T(8,128)S(1)} %get-tuple-element.52), channel_id=1, source_target_pairs={{0,28},{4,0},{8,4},{12,8},{16,12},{20,16},{24,20},{28,24},{1,29},{... | collective-permute-start | bytes 1007624 | tf_op jit(solution)/shard_map/ppermute | solution.py:586
  43.7 4.7 %collective-permute-start.10 = (f32[8,512]{1,0:T(8,128)S(1)}, f32[8,512]{1,0:T(8,128)S(1)}, u32[]{:S(2)}, u32[]{:S(2)}) collective-permute-start(f32[8,512]{1,0:T(8,128)S(1)} %get-tuple-element.57), channel_id=1, source_target_pairs={{0,2},{1,3},{2,0},{3,1},{4,6},{5,7},{6,4},{7,5},{8,10},{9,11},{10,... | collective-permute-start | bytes 49160 | tf_op jit(solution)/shard_map/ppermute | solution.py:591
  44.6 5.6 %collective-permute-start.11 = (f32[8,512]{1,0:T(8,128)S(1)}, f32[8,512]{1,0:T(8,128)S(1)}, u32[]{:S(2)}, u32[]{:S(2)}) collective-permute-start(f32[8,512]{1,0:T(8,128)S(1)} %get-tuple-element.58), channel_id=1, source_target_pairs={{0,3},{1,2},{2,1},{3,0},{4,7},{5,6},{6,5},{7,4},{8,11},{9,10},{10,... | collective-permute-start | bytes 49160 | tf_op jit(solution)/shard_map/ppermute | solution.py:591
  46.4 3.9 %collective-permute-start.9 = (f32[8,512]{1,0:T(8,128)S(1)}, f32[8,512]{1,0:T(8,128)S(1)}, u32[]{:S(2)}, u32[]{:S(2)}) collective-permute-start(f32[8,512]{1,0:T(8,128)S(1)} %get-tuple-element.56.refs_2_), channel_id=1, source_target_pairs={{0,1},{1,0},{2,3},{3,2},{4,5},{5,4},{6,7},{7,6},{8,9},{9,8},{10,11... | collective-permute-start | bytes 49160 | tf_op jit(solution)/shard_map/ppermute | solution.py:591

commit v5 on v4

--- a/solution.py
+++ b/solution.py
@@ -168,8 +168,49 @@
     return pl.ds(pl.multiple_of(8 * t, 8), 8)
 
 
-def collide_kernel(n, per, nx, pop, mask, vel, post, fwd, bwd, up, down, *rest):
-    others, (here, flags, speeds, sems, small) = rest[: n - 3], rest[n - 3 :]
+def three(value):
+    high, rest = value.astype(BF16), value - value.astype(BF16).astype(F32)
+    mid = rest.astype(BF16)
+    return high.astype(F32), mid.astype(F32), (rest - mid.astype(F32)).astype(BF16).astype(F32)
+
+
+def spread_beads(spots, speeds, rows, cols, left, right):
+    patches, beads = spots.shape[1:]
+    tile = cols.shape[-1]
+    count = beads // tile
+    place = lax.broadcasted_iota(I32, (48, 3 * tile), 0)
+    comp = lax.broadcasted_iota(I32, (48, 3 * tile), 1) // tile
+    part = ((place >> 3) == 0) | ((place >> 3) == 2) | ((place >> 3) == 5)
+    spread = jnp.where(part & ((place & 7) == comp + 2), -1.0, 0.0).astype(BF16)
+    stacks = []
+    for g in range(patches):
+        x = [spots[c, g : g + 1, :] for c in range(3)]
+        w = [4.5 * speeds[c, g : g + 1, :] for c in range(3)]
+        for c in range(3):
+            for j in range(count):
+                rows[g, c, j] = jnp.broadcast_to(x[c][:, j * tile : (j + 1) * tile], (8, tile))
+        dot = x[0] * w[0] + (x[1] * w[1] + x[2] * w[2])
+        one = jnp.ones_like(dot)
+        high, mid, low = three(jnp.concatenate([dot, one] + w + x, axis=0))
+        found = jnp.concatenate([high, mid, high, low, mid, high], axis=0).astype(BF16)
+        for j in range(count):
+            right[g, j] = found[:, j * tile : (j + 1) * tile]
+        high, mid, low = three(jnp.concatenate([one, dot] + [-v for v in x + w], axis=0))
+        stacks += [high, high, mid, high, mid, low]
+    if -48 * patches % 128:
+        stacks.append(jnp.zeros((-48 * patches % 128, beads), F32))
+    turned = jnp.concatenate(stacks, axis=0).T.astype(BF16)
+    for g in range(patches):
+        for j in range(count):
+            here = turned[j * tile : (j + 1) * tile, 48 * g : 48 * (g + 1)]
+            left[g, j] = here
+            wide = jnp.dot(here, spread, preferred_element_type=F32)
+            for c in range(3):
+                cols[g, c, j] = wide[:, c * tile : (c + 1) * tile]
+
+
+def collide_kernel(n, per, nx, pop, mask, pos, vel, post, fwd, bwd, up, down, rows, cols, left, right, *rest):
+    others, (here, flags, spots, speeds, sems, small) = rest[: n - 3], rest[n - 3 :]
     order = [(x, h) for x in [0, nx - 1] + list(range(1, nx - 1)) for h in range(1)]
     span = ROWS // 1
     copies = [
@@ -180,10 +221,11 @@
     ]
     extra = [
         pltpu.make_async_copy(vel, speeds, small.at[0]),
-        pltpu.make_async_copy(mask, flags, small.at[1]),
+        pltpu.make_async_copy(pos, spots, small.at[1]),
+        pltpu.make_async_copy(mask, flags, small.at[2]),
     ]
     ahead = 3
-    for copy in copies[:ahead] + extra:
+    for copy in extra[:2] + copies[:ahead] + extra[2:]:
         copy.start()
     me = lax.axis_index("xs")
     extra[0].wait()
@@ -201,6 +243,8 @@
                     else:
                         others[d - 2][i : i + 1, :] = piece
     extra[1].wait()
+    spread_beads(spots, speeds, rows, cols, left, right)
+    extra[2].wait()
     for i, (x, h) in enumerate(order):
         copies[i].wait()
         if i + ahead < len(copies):
@@ -413,60 +457,37 @@
         copy.wait()
 
 
-def pair_kernel(begin, end, pair_tiles, pos, vel, noise, *refs):
-    base, rows, cols, theta, acc = refs[-5:]
+def pair_kernel(begin, end, pair_tiles, vel, rows, cols, left, right, noise, *refs):
+    base, theta, along, acc = refs[-4:]
     tile = noise.shape[-1]
-    count = pos.shape[-1] // tile
+    count = cols.shape[2]
     pairs = noise.shape[1]
     patches = end - begin
-    spread = (lax.broadcasted_iota(I32, (24, 6 * tile), 0) & 7) == (
-        lax.broadcasted_iota(I32, (24, 6 * tile), 1) // tile
-    )
-    spread = jnp.where(spread, 1.0, 0.0).astype(BF16)
     eye = lax.broadcasted_iota(I32, (tile, tile), 0) == lax.broadcasted_iota(I32, (tile, tile), 1)
     scale = jnp.where(eye, 15.0, 0.0).astype(BF16)
-    empty = jnp.zeros((2, pos.shape[-1]), F32)
-    parts, speeds = [], []
-    for g in range(patches):
-        both = [ref[c, begin + g : begin + g + 1, :] for ref in (pos, vel) for c in range(3)]
-        speeds.append(both[3:])
-        both = [both[c] if c < 3 else 4.5 * both[c] for c in range(6)]
-        for c in range(6):
-            for j in range(count):
-                rows[g, c, j] = jnp.broadcast_to(both[c][:, j * tile : (j + 1) * tile], (8, tile))
-        stacked = jnp.concatenate(both + [empty], axis=0)
-        high, rest = stacked.astype(BF16), stacked - stacked.astype(BF16).astype(F32)
-        mid, low = rest.astype(BF16), rest - rest.astype(BF16).astype(F32)
-        parts += [high.astype(F32), mid.astype(F32), low]
-    used = 24 * patches
-    parts.append(jnp.zeros((-used % 128, pos.shape[-1]), F32))
-    parts = jnp.concatenate(parts, axis=0).T.astype(BF16)
     acc[...] = jnp.zeros_like(acc)
     for g in range(patches):
-        for j in range(count):
-            left = parts[j * tile : (j + 1) * tile, 24 * g : 24 * (g + 1)]
-            wide = jnp.dot(left, spread, preferred_element_type=F32)
-            for c in range(6):
-                cols[g, c, j] = wide[:, c * tile : (c + 1) * tile]
         for p in range(pairs):
             theta[g * pairs + p] = lax.dot_general(
                 scale, noise[begin + g, p], (((1,), (1,)), ((), ())), preferred_element_type=F32
             )
+            first, second = pair_tiles[begin + g, 0, p], pair_tiles[begin + g, 1, p]
+            along[g * pairs + p] = jnp.dot(
+                left[begin + g, second], right[begin + g, first], preferred_element_type=F32
+            )
 
     def one_pair(i, carry):
         g, p = i // pairs, i % pairs
         first = pair_tiles[begin + g, 0, p]
         second = pair_tiles[begin + g, 1, p]
-        mine = [rows[g, c, first] for c in range(6)]
+        mine = [rows[begin + g, c, first] for c in range(3)]
         total = []
         for s in range(tile // 8):
             part = slice(8 * s, 8 * s + 8)
-            dx, dy, dz = [mine[c] - cols[g, c, second, part, :] for c in range(3)]
-            vx, vy, vz = [mine[c] - cols[g, c, second, part, :] for c in range(3, 6)]
+            dx, dy, dz = [mine[c] - cols[begin + g, c, second, part, :] for c in range(3)]
             square = (dx * dx + 0.01) + (dy * dy + dz * dz)
             close = jnp.maximum(lax.rsqrt(square) - 1.0, 0.0)
-            along = dx * vx + (dy * vy + dz * vz)
-            force = close * ((theta[i, part, :] + 25.0) - close * along)
+            force = close * ((theta[i, part, :] + 25.0) - close * along[i, part, :])
             here = [force * dx, force * dy, force * dz]
             total = here if not total else [a + b for a, b in zip(total, here)]
         for c in range(3):
@@ -479,7 +500,8 @@
             force = jnp.concatenate(
                 [jnp.sum(acc[g, j, c], axis=0, keepdims=True) for j in range(count)], axis=1
             )
-            base[c, begin + g : begin + g + 1, :] = 0.5 * speeds[g][c] + 0.04 * force
+            speed = vel[c, begin + g : begin + g + 1, :]
+            base[c, begin + g : begin + g + 1, :] = 0.5 * speed + 0.04 * force
 
 
 def split(value):
@@ -569,7 +591,7 @@
 
 
 def final_kernel(n, per, pos, base, *refs):
-    flows, new_pos, new_vel = refs[:n], refs[n], refs[n + 1]
+    flows, new_pos, new_vel = refs[:n][::-1], refs[n], refs[n + 1]
     me = lax.axis_index("xs")
     for d in range(n):
         source = me ^ d
@@ -591,24 +613,22 @@
     return lax.ppermute(value, axis, [(i, i ^ by) for i in range(n)])
 
 
-def pair_call(begin, end, pair_tiles, pos, vel, noise, given, after):
+def pair_call(begin, end, pair_tiles, vel, rows, cols, left, right, noise, given, after):
     tile = noise.shape[-1]
-    count = pos.shape[2] // tile
     return call(
         functools.partial(pair_kernel, begin, end),
-        [pair_tiles, pos, vel, noise] + given,
-        jax.ShapeDtypeStruct(pos.shape, F32),
+        [pair_tiles, vel, rows, cols, left, right, noise] + given,
+        jax.ShapeDtypeStruct(vel.shape, F32),
         "pair_forces",
         cost(1000, 1000),
         after=after,
         specs={0: SMEM_SPEC},
         out_specs=VMEM_SPEC,
-        input_output_aliases={4: 0} if given else {},
+        input_output_aliases={7: 0} if given else {},
         scratch_shapes=[
-            pltpu.VMEM((end - begin, 6, count, 8, tile), F32),
-            pltpu.VMEM((end - begin, 6, count, tile, tile), F32),
             pltpu.VMEM(((end - begin) * noise.shape[1], tile, tile), F32),
-            pltpu.VMEM((end - begin, count, 3, 8, tile), F32),
+            pltpu.VMEM(((end - begin) * noise.shape[1], tile, tile), F32),
+            pltpu.VMEM((end - begin, cols.shape[2], 3, 8, tile), F32),
         ],
     )
 
@@ -621,6 +641,7 @@
     per = patches // n
     nx = populations.shape[1]
     lanes = populations.shape[3]
+    tiles = beads // 128
     arr = lambda *shape: jax.ShapeDtypeStruct(shape, F32)
     ints = lambda *shape: jax.ShapeDtypeStruct(shape, I32)
     vmem, dma = pltpu.VMEM, pltpu.SemaphoreType.DMA
@@ -628,33 +649,41 @@
     velocities = jnp.transpose(velocities, (1, 0, 2))
     pair_tiles = jnp.transpose(pair_tiles, (0, 2, 1))
 
-    post, fwd, bwd, up, down, *others = call(
+    post, fwd, bwd, up, down, *layouts = call(
         functools.partial(collide_kernel, n, per, nx),
-        [in_hbm(populations), in_hbm(fluid_mask), in_hbm(velocities)],
+        [in_hbm(value) for value in (populations, fluid_mask, positions, velocities)],
         [arr(19, nx, PAD, lanes), arr(384, lanes), arr(384, lanes)]
         + [arr(nx, 32, lanes)] * 2
+        + [
+            arr(patches, 3, tiles, 8, 128),
+            arr(patches, 3, tiles, 128, 128),
+            jax.ShapeDtypeStruct((patches, tiles, 128, 48), BF16),
+            jax.ShapeDtypeStruct((patches, tiles, 48, 128), BF16),
+        ]
         + [arr(16, lanes)] * (n - 3),
         "collide_first",
         cost(3_000_000_000, 11_000_000),
-        specs={0: ANY_SPEC, 1: ANY_SPEC, 2: ANY_SPEC},
-        out_specs=[VMEM_SPEC] * (n + 2),
+        specs={i: ANY_SPEC for i in range(4)},
+        out_specs=[VMEM_SPEC] * (n + 6),
         scratch_shapes=[
             vmem((nx, 19, ROWS, lanes), F32),
             vmem((nx, ROWS, lanes), I32),
+            vmem(positions.shape, F32),
             vmem(velocities.shape, F32),
             dma((2 * nx,)),
-            dma((2,)),
+            dma((3,)),
         ],
     )
     before = shift(fwd, "ax", 1)
     after = shift(bwd, "ax", -1)
+    layouts, others = layouts[:4], layouts[4:]
     below = shift(up, "xs", 1)
     above = shift(down, "xs", -1)
     sent = [below] + [shift(other, "xs", d + 2) for d, other in enumerate(others)] + [above]
 
-    half = patches // 2
-    bead_args = (pair_tiles, positions, velocities, pair_noise)
-    base = pair_call(0, half, *bead_args, [], [down])
+    cuts = (patches * 5 // 8, patches * 7 // 8)
+    bead_args = (pair_tiles, velocities, *layouts, pair_noise)
+    base = pair_call(0, cuts[0], *bead_args, [], [down])
 
     post, edge_fwd, edge_bwd, flags = call(
         functools.partial(edges_kernel, n, nx),
@@ -662,7 +691,7 @@
         [arr(*post.shape), arr(16, lanes), arr(16, lanes), ints(nx, PAD, lanes)],
         "edges",
         cost(1000, 1000),
-        after=[base] + sent[1:-1],
+        after=[base],
         out_specs=[VMEM_SPEC] * 4,
         input_output_aliases={0: 0},
     )
@@ -677,8 +706,6 @@
         cost(1000, 1000),
         out_specs=[VMEM_SPEC] * 2,
     )
-    base = pair_call(half, patches, *bead_args, [base], [flags])
-
     def outer(first, face, edge, post2, bits, after):
         return call(
             functools.partial(outer_kernel, nx, first),
@@ -692,11 +719,13 @@
             scratch_shapes=[vmem((5, PAD, lanes), F32), vmem((PAD, lanes), I32)],
         )
 
-    post2, bits, bwd2 = outer(True, before, edge_before, post2, bits, [base, after, edge_after])
+    base = pair_call(cuts[0], cuts[1], *bead_args, [base], [flags])
+    post2, bits, bwd2 = outer(True, before, edge_before, post2, bits, [base, after, edge_after] + sent[1:-1])
     after2 = shift(bwd2, "ax", -1)
     post2, bits, fwd2 = outer(False, after, edge_after, post2, bits, [])
     before2 = shift(fwd2, "ax", 1)
 
+    base = pair_call(cuts[1], patches, *bead_args, [base], [fwd2])
     out, flow, part = call(
         functools.partial(final_middle_kernel, nx),
         [post2, bits, patch_voxel],
@@ -728,7 +757,7 @@
         [arr(*populations.shape), arr(*flow.shape)] + [arr(8, beads)] * n,
         "final_outer",
         cost(1000, 1000),
-        after=[total],
+        after=[total, base],
         specs={0: ANY_SPEC, 7: SMEM_SPEC},
         out_specs=[ANY_SPEC] + [VMEM_SPEC] * (n + 1),
         input_output_aliases={0: 0, 1: 1},
@@ -752,7 +781,7 @@
     )
     new_pos, new_vel = call(
         functools.partial(final_kernel, n, per),
-        [positions, base] + sent_flows,
+        [positions, base] + sent_flows[::-1],
         [arr(*positions.shape)] * 2,
         "bead_update",
         cost(1000, 1000),

time: 51.1 us -> 48.9 us (0.957)
  waiting for transfers between devices: 3.91 us -> 2.18 us
  Pallas kernels: 29.9 us -> 28.3 us
  starting transfers between devices: 16.4 us -> 17.4 us
    pallas_call x12 -> x13, Pallas kernels: 29.9 us -> 28.3 us  [call(): pl.pallas_call(body, in_specs=[specs.get(i, VMEM_SPEC) for i in range(cou...]
    ppermute x3, waiting for transfers between devices: 2.08 us -> 1.17 us  [swap(): return lax.ppermute(value, axis, [(i, i ^ by) for i in range(n)])]
    ppermute x3, starting transfers between devices: 3.55 us -> 4.45 us  [swap(): return lax.ppermute(value, axis, [(i, i ^ by) for i in range(n)])]
    ppermute x9, waiting for transfers between devices: 1.83 us -> 1.01 us  [shift(): return lax.ppermute(value, axis, [(i, (i + by) % n) for i in range(n)])]
  transfers between devices with their start and end apart: 12 -> 12, of which waited for: 4 -> 4; matrix products, arithmetic and copies ran while one was open for 0% -> 0% of each run, Pallas kernels for 37% -> 35%
where the time goes in v5:
time: 48.9 us; the launch traced here: 48.8 us
  Pallas kernels  28.3 us (58%)
  starting transfers between devices  17.4 us (36%)
  waiting for transfers between devices  2.18 us (4%)
  between operations  0.82 us (2%)
    pallas_call x13, Pallas kernels, call(): pl.pallas_call(body, in_specs=[specs.get(i, VMEM_SPEC) for i in range(cou...  28.3 us
    ppermute x9, starting transfers between devices, shift(): return lax.ppermute(value, axis, [(i, (i + by) % n) for i in range(n)])  13 us
    ppermute x3, starting transfers between devices, swap(): return lax.ppermute(value, axis, [(i, i ^ by) for i in range(n)])  4.45 us
    ppermute x3, waiting for transfers between devices, swap(): return lax.ppermute(value, axis, [(i, i ^ by) for i in range(n)])  1.17 us
    ppermute x9, waiting for transfers between devices, shift(): return lax.ppermute(value, axis, [(i, (i + by) % n) for i in range(n)])  1.01 us
  transfers between devices with their start and end apart: 12, of which 4 were waited for; matrix products, arithmetic and copies ran while one was open for 0% of the time, Pallas kernels for 35%

profile of v5, /device:TPU:0, one launch (start us, length us, event | category | flops | bytes accessed | tf_op | source)
XLA Modules:
  0.0 48.8 jit_solution(18340975808000579574)
XLA Ops:
  0.6 0.0 copy-start.1
  0.6 0.0 copy-start
  0.7 0.0 copy-start.4
  0.7 4.4 %collide_first.1 = (f32[19,4,88,256]{3,2,1,0:T(8,128)S(1)}, f32[384,256]{1,0:T(8,128)S(1)}, f32[384,256]{1,0:T(8,128)S(1)}, f32[4,32,256]{2,1,0:T(8,128)S(1)}, f...) custom-call(f32[19,4,64,256]{3,2,1,0:T(8,128)} %refs_0_.2, ...), custom_call_target="tpu_custom_call" | custom-call | flops 3000000000 | bytes 11000000 | tf_op jit(solution)/shard_map/collide_first/pallas_call | solution.py:63
  5.1 0.0 copy-start.2
  5.1 3.4 %collective-permute-start.2 = (f32[384,256]{1,0:T(8,128)S(1)}, f32[384,256]{1,0:T(8,128)S(1)}, u32[]{:S(2)}, u32[]{:S(2)}) collective-permute-start(f32[384,256]{1,0:T(8,128)S(1)} %get-tuple-element.46), channel_id=1, source_target_pairs={{0,28},{4,0},{8,4},{12,8},{16,12},{20,16},{24,20},{28,24},{1,29},{... | collective-permute-start | bytes 1179656 | tf_op jit(solution)/shard_map/ppermute | solution.py:608
  8.5 0.0 collective-permute-start.4
  8.5 1.6 %collective-permute-start = (f32[4,32,256]{2,1,0:T(8,128)S(1)}, f32[4,32,256]{2,1,0:T(8,128)S(1)}, u32[]{:S(2)}, u32[]{:S(2)}) collective-permute-start(f32[4,32,256]{2,1,0:T(8,128)S(1)} %get-tuple-element.38), channel_id=1, source_target_pairs={{0,1},{1,2},{2,3},{3,0},{4,5},{5,6},{6,7},{7,4},{8,9},{9,10},{10,1... | collective-permute-start | bytes 393224 | tf_op jit(solution)/shard_map/ppermute | solution.py:608
  10.0 2.2 %collective-permute-start.1 = (f32[4,32,256]{2,1,0:T(8,128)S(1)}, f32[4,32,256]{2,1,0:T(8,128)S(1)}, u32[]{:S(2)}, u32[]{:S(2)}) collective-permute-start(f32[4,32,256]{2,1,0:T(8,128)S(1)} %get-tuple-element.39.refs_7_), channel_id=1, source_target_pairs={{0,3},{1,0},{2,1},{3,2},{4,7},{5,4},{6,5},{7,6},{8,11},{9,8},{10,9... | collective-permute-start | bytes 393224 | tf_op jit(solution)/shard_map/ppermute | solution.py:608
  12.3 0.8 %collective-permute-start.6 = (f32[16,256]{1,0:T(8,128)S(1)}, f32[16,256]{1,0:T(8,128)S(1)}, u32[]{:S(2)}, u32[]{:S(2)}) collective-permute-start(f32[16,256]{1,0:T(8,128)S(1)} %get-tuple-element.52), channel_id=1, source_target_pairs={{0,2},{1,3},{2,0},{3,1},{4,6},{5,7},{6,4},{7,5},{8,10},{9,11},{10,... | collective-permute-start | bytes 49160 | tf_op jit(solution)/shard_map/ppermute | solution.py:608
  13.1 0.0 copy-done.1
  13.1 0.0 copy-done
  13.1 0.0 copy-done.4
  13.1 4.0 %pair_forces.3.refs_4_.refs_7_ = f32[3,8,512]{2,1,0:T(8,128)S(1)} custom-call(s32[8,2,8]{2,1,0:T(2,128)S(1)} %bitcast.10, f32[3,8,512]{2,1,0:T(8,128)S(1)} %bitcast.6, f32[8,3,4,8,128]{4,3,2,1,0:T(8,128)S(1)} %get-tuple-element.40.refs_2_, f32[8,3,4,128,128]{4,3,2,1,0:T(8,128)S(1)} %get-tuple-element.41.refs_3_, ...), custom_call_target="tpu_custom_call" | custom-call | flops 1000 | bytes 1000 | tf_op jit(solution)/shard_map/pair_forces/pallas_call | solution.py:63
  17.1 0.0 collective-permute-done.refs_2_.refs_3_
  17.1 0.7 %collective-permute-done.1.refs_3_.refs_5_ = f32[4,32,256]{2,1,0:T(8,128)S(1)} collective-permute-done((f32[4,32,256]{2,1,0:T(8,128)S(1)}, f32[4,32,256]{2,1,0:T(8,128)S(1)}, u32[]{:S(2)}, u32[]{:S(2)}) %collective-permute-start.1) | collective-permute-done | bytes 131104 | tf_op jit(solution)/shard_map/ppermute | solution.py:608
  17.8 0.0 copy-done.2
  17.8 0.2 edges.1
  17.9 2.3 %collective-permute-start.3 = (f32[16,256]{1,0:T(8,128)S(1)}, f32[16,256]{1,0:T(8,128)S(1)}, u32[]{:S(2)}, u32[]{:S(2)}) collective-permute-start(f32[16,256]{1,0:T(8,128)S(1)} %get-tuple-element.47), channel_id=1, source_target_pairs={{0,28},{4,0},{8,4},{12,8},{16,12},{20,16},{24,20},{28,24},{1,29},{... | collective-permute-start | bytes 49160 | tf_op jit(solution)/shard_map/ppermute | solution.py:608
  20.2 0.0 collective-permute-start.5
  20.2 2.1 %pair_forces.4.refs_6_.refs_7_ = f32[3,8,512]{2,1,0:T(8,128)S(1)} custom-call(s32[8,2,8]{2,1,0:T(2,128)S(1)} %bitcast.11, f32[3,8,512]{2,1,0:T(8,128)S(1)} %bitcast.7, f32[8,3,4,8,128]{4,3,2,1,0:T(8,128)S(1)} %get-tuple-element.40.refs_2_, f32[8,3,4,128,128]{4,3,2,1,0:T(8,128)S(1)} %get-tuple-element.41.refs_3_, ...), custom_call_target="tpu_custom_call", output_to_operand_aliasing={{}: (7, {})} | custom-call | flops 1000 | bytes 1000 | tf_op jit(solution)/shard_map/pair_forces/pallas_call | solution.py:63
  22.3 1.6 %middle_layers.1 = (f32[19,4,88,256]{3,2,1,0:T(8,128)S(1)}, s32[4,72,256]{2,1,0:T(8,128)S(1)}) custom-call(f32[19,4,88,256]{3,2,1,0:T(8,128)S(1)} %get-tuple-element.44.refs_0_, s32[4,88,256]{2,1,0:T(8,128)S(1)} %get-tuple-element.45.refs_1_.refs_8_), custom_call_target="tpu_custom_call" | custom-call | flops 1000 | bytes 1000 | tf_op jit(solution)/shard_map/middle_layers/pallas_call | solution.py:63
  23.9 0.0 collective-permute-done.6.refs_9_.refs_4_
  24.0 0.0 collective-permute-done.3.refs_8_.refs_3_
  24.0 0.3 collective-permute-done.5.refs_3_
  24.3 0.0 collective-permute-done.2.refs_7_.refs_2_
  24.3 0.0 collective-permute-done.4.refs_2_
  24.3 0.9 %first_layer.1 = (f32[19,4,88,256]{3,2,1,0:T(8,128)S(1)}, s32[4,72,256]{2,1,0:T(8,128)S(1)}, f32[328,256]{1,0:T(8,128)S(1)}) custom-call(f32[19,4,88,256]{3,2,1,0:T(8,128)S(1)} %get-tuple-element.44.refs_0_, s32[4,88,256]{2,1,0:T(8,128)S(1)} %get-tuple-element.45.refs_1_.refs_8_, ...), custom_call_target="tpu_custom_call", output_to_operand_aliasing={{0}: (4, {}), {1}: (5, {})} | custom-call | flops 1000 | bytes 1000 | tf_op jit(solution)/shard_map/first_layer/pallas_call | solution.py:63
  25.2 0.9 %last_layer.1 = (f32[19,4,88,256]{3,2,1,0:T(8,128)S(1)}, s32[4,72,256]{2,1,0:T(8,128)S(1)}, f32[328,256]{1,0:T(8,128)S(1)}) custom-call(f32[19,4,88,256]{3,2,1,0:T(8,128)S(1)} %get-tuple-element.44.refs_0_, s32[4,88,256]{2,1,0:T(8,128)S(1)} %get-tuple-element.45.refs_1_.refs_8_, ...), custom_call_target="tpu_custom_call", output_to_operand_aliasing={{0}: (4, {}), {1}: (5, {})} | custom-call | flops 1000 | bytes 1000 | tf_op jit(solution)/shard_map/last_layer/pallas_call | solution.py:63
  26.0 0.0 copy-start.3
  26.0 0.1 collective-permute-start.8
  26.1 0.0 copy-start.6
  26.1 2.6 %collective-permute-start.7 = (f32[328,256]{1,0:T(8,128)S(1)}, f32[328,256]{1,0:T(8,128)S(1)}, u32[]{:S(2)}, u32[]{:S(2)}) collective-permute-start(f32[328,256]{1,0:T(8,128)S(1)} %get-tuple-element.60), channel_id=1, source_target_pairs={{0,28},{4,0},{8,4},{12,8},{16,12},{20,16},{24,20},{28,24},{1,29},{... | collective-permute-start | bytes 1007624 | tf_op jit(solution)/shard_map/ppermute | solution.py:608
  28.7 1.4 %pair_forces.5.refs_10_.refs_1_ = f32[3,8,512]{2,1,0:T(8,128)S(1)} custom-call(s32[8,2,8]{2,1,0:T(2,128)S(1)} %bitcast.12, f32[3,8,512]{2,1,0:T(8,128)S(1)} %bitcast.8, f32[8,3,4,8,128]{4,3,2,1,0:T(8,128)S(1)} %get-tuple-element.40.refs_2_, f32[8,3,4,128,128]{4,3,2,1,0:T(8,128)S(1)} %get-tuple-element.41.refs_3_, ...), custom_call_target="tpu_custom_call", output_to_operand_aliasing={{}: (7, {})} | custom-call | flops 1000 | bytes 1000 | tf_op jit(solution)/shard_map/pair_forces/pallas_call | solution.py:63
  30.2 0.0 copy-done.3
  30.2 2.4 %final_middle.1 = (f32[19,4,64,256]{3,2,1,0:T(8,128)}, f32[3,4,64,256]{3,2,1,0:T(8,128)S(1)}, f32[8,8,512]{2,1,0:T(8,128)S(1)}) custom-call(f32[19,4,88,256]{3,2,1,0:T(8,128)S(1)} %get-tuple-element.55.refs_0_.refs_2_, s32[4,72,256]{2,1,0:T(8,128)S(1)} %get-tuple-element.56.refs_1_.refs_3_, s32[8,512]{1,0:T(8,128)S(1)} %copy-done.3, ...), custom_call_target="tpu_custom_call" | custom-call | flops 1000 | bytes 1000 | tf_op jit(solution)/shard_map/final_middle/pallas_call | solution.py:63
  32.7 0.0 copy-done.6
  32.7 4.5 %bead_sums.1.refs_9_.refs_0_ = f32[4,256,256]{2,1,0:T(8,128)S(1)} custom-call(s32[8]{0:T(128)S(1)} %copy-done.6, s32[8,512]{1,0:T(8,128)S(1)} %copy-done.3, f32[3,8,512]{2,1,0:T(8,128)S(1)} %bitcast.9, f32[4,32,256]{2,1,0:T(8,128)S(1)} %collective-permute-done.refs_2_.refs_3_, f32[16,256]{1,0:T(8,128)S(1)} %collective-permute-done.6.refs_9_.refs_4_, ...), custom_call_target="tpu_custom_call" | custom-call | flops 1000 | bytes 1000 | tf_op jit(solution)/shard_map/bead_sums/pallas_call | solution.py:63
  37.2 0.0 collective-permute-done.8.refs_5_
  37.2 0.0 collective-permute-done.7.refs_4_
  37.2 0.0 copy-start.5
  37.2 4.2 %final_outer.1 = (f32[19,4,64,256]{3,2,1,0:T(8,128)}, f32[3,4,64,256]{3,2,1,0:T(8,128)S(1)}, f32[8,512]{1,0:T(8,128)S(1)}, f32[8,512]{1,0:T(8,128)S(1)}, f32[8,512]{1,0:T(8,128)S(1)}, /*index=5*/f32[8,512]{1,0:T(8,128)S(1)}) custom-call(f32[19,4,64,256]{3,2,1,0:T(8,128)} %get-tuple-element.58.refs_0_, ...), custom_call_target="tpu_custom_call", output_to_operand_aliasing={{0}: (0, {}), {1}: (1, {})} | custom-call | flops 1000 | bytes 1000 | tf_op jit(solution)/shard_map/final_outer/pallas_call | solution.py:63
  41.5 2.0 %collective-permute-start.9 = (f32[8,512]{1,0:T(8,128)S(1)}, f32[8,512]{1,0:T(8,128)S(1)}, u32[]{:S(2)}, u32[]{:S(2)}) collective-permute-start(f32[8,512]{1,0:T(8,128)S(1)} %get-tuple-element.63), channel_id=1, source_target_pairs={{0,3},{1,2},{2,1},{3,0},{4,7},{5,6},{6,5},{7,4},{8,11},{9,10},{10,... | collective-permute-start | bytes 49160 | tf_op jit(solution)/shard_map/ppermute | solution.py:613
  43.4 0.6 %collective-permute-start.10 = (f32[8,512]{1,0:T(8,128)S(1)}, f32[8,512]{1,0:T(8,128)S(1)}, u32[]{:S(2)}, u32[]{:S(2)}) collective-permute-start(f32[8,512]{1,0:T(8,128)S(1)} %get-tuple-element.64), channel_id=1, source_target_pairs={{0,2},{1,3},{2,0},{3,1},{4,6},{5,7},{6,4},{7,5},{8,10},{9,11},{10,... | collective-permute-start | bytes 49160 | tf_op jit(solution)/shard_map/ppermute | solution.py:613
  44.1 1.9 %collective-permute-start.11 = (f32[8,512]{1,0:T(8,128)S(1)}, f32[8,512]{1,0:T(8,128)S(1)}, u32[]{:S(2)}, u32[]{:S(2)}) collective-permute-start(f32[8,512]{1,0:T(8,128)S(1)} %get-tuple-element.65.refs_2_), channel_id=1, source_target_pairs={{0,1},{1,0},{2,3},{3,2},{4,5},{5,4},{6,7},{7,6},{8,9},{9,8},{10,11... | collective-permute-start | bytes 49160 | tf_op jit(solution)/shard_map/ppermute | solution.py:613
  45.9 1.0 %drag_field.1 = f32[3,4,64,256]{3,2,1,0:T(8,128)} custom-call(f32[4,256,256]{2,1,0:T(8,128)S(1)} %bead_sums.1.refs_9_.refs_0_, f32[3,4,64,256]{3,2,1,0:T(8,128)S(1)} %get-tuple-element.69.refs_1_, f32[8,512]{1,0:T(8,128)S(1)} %get-tuple-element.65.refs_2_), custom_call_target="tpu_custom_call" | custom-call | flops 1000 | bytes 1000 | tf_op jit(solution)/shard_map/drag_field/pallas_call | solution.py:63
  46.9 0.3 collective-permute-done.9.refs_2_
  47.2 0.8 %collective-permute-done.10.refs_3_ = f32[8,512]{1,0:T(8,128)S(1)} collective-permute-done((f32[8,512]{1,0:T(8,128)S(1)}, f32[8,512]{1,0:T(8,128)S(1)}, u32[]{:S(2)}, u32[]{:S(2)}) %collective-permute-start.10) | collective-permute-done | bytes 16416 | tf_op jit(solution)/shard_map/ppermute | solution.py:613
  48.1 0.0 collective-permute-done.11.refs_4_
  48.1 0.0 copy-done.5
  48.1 0.7 %bead_update.1 = (f32[3,8,512]{2,1,0:T(8,128)}, f32[3,8,512]{2,1,0:T(8,128)}) custom-call(f32[3,8,512]{2,1,0:T(8,128)S(1)} %bitcast.14, f32[3,8,512]{2,1,0:T(8,128)S(1)} %pair_forces.5.refs_10_.refs_1_, f32[8,512]{1,0:T(8,128)S(1)} %collective-permute-done.9.refs_2_, f32[8,512]{1,0:T(8,128)S(1)} %collective-permute-done.10.refs_3_, ...), custom_call_target="tpu_custom_call" | custom-call | flops 1000 | bytes 1000 | tf_op jit(solution)/shard_map/bead_update/pallas_call | solution.py:63
Async XLA Ops:
  0.6 12.4 %copy-start.1 = (f32[8,3,512]{2,0,1:T(8,128)S(1)}, f32[8,3,512]{2,0,1:T(8,128)}, u32[]{:S(2)}) copy-start(f32[8,3,512]{2,0,1:T(8,128)} %param.13) | copy-start | bytes 147460
  0.6 12.4 %copy-start = (bf16[8,8,128,128]{3,2,1,0:T(8,128)(2,1)S(1)}, bf16[8,8,128,128]{3,2,1,0:T(8,128)(2,1)}, u32[]{:S(2)}) copy-start(bf16[8,8,128,128]{3,2,1,0:T(8,128)(2,1)} %refs_6_.6) | copy-start | bytes 6291460
  0.7 12.4 %copy-start.4 = (s32[8,8,2]{1,2,0:T(2,128)S(1)}, s32[8,8,2]{1,2,0:T(2,128)}, u32[]{:S(2)}) copy-start(s32[8,8,2]{1,2,0:T(2,128)} %param.14) | copy-start | bytes 1540
  5.1 12.7 %copy-start.2 = (s32[4,64,256]{2,1,0:T(8,128)S(1)}, s32[4,64,256]{2,1,0:T(8,128)}, u32[]{:S(2)}) copy-start(s32[4,64,256]{2,1,0:T(8,128)} %refs_1_.4) | copy-start | bytes 786436
  5.1 19.2 %collective-permute-start.2 = (f32[384,256]{1,0:T(8,128)S(1)}, f32[384,256]{1,0:T(8,128)S(1)}, u32[]{:S(2)}, u32[]{:S(2)}) collective-permute-start(f32[384,256]{1,0:T(8,128)S(1)} %get-tuple-element.46), channel_id=1, source_target_pairs={{0,28},{4,0},{8,4},{12,8},{16,12},{20,16},{24,20},{28,24},{1,29},{... | collective-permute-start | bytes 1179656 | tf_op jit(solution)/shard_map/ppermute | solution.py:608
  8.5 15.8 %collective-permute-start.4 = (f32[384,256]{1,0:T(8,128)S(1)}, f32[384,256]{1,0:T(8,128)S(1)}, u32[]{:S(2)}, u32[]{:S(2)}) collective-permute-start(f32[384,256]{1,0:T(8,128)S(1)} %get-tuple-element.48), channel_id=1, source_target_pairs={{0,4},{4,8},{8,12},{12,16},{16,20},{20,24},{24,28},{28,0},{1,5},{5... | collective-permute-start | bytes 1179656 | tf_op jit(solution)/shard_map/ppermute | solution.py:608
  8.5 8.6 %collective-permute-start = (f32[4,32,256]{2,1,0:T(8,128)S(1)}, f32[4,32,256]{2,1,0:T(8,128)S(1)}, u32[]{:S(2)}, u32[]{:S(2)}) collective-permute-start(f32[4,32,256]{2,1,0:T(8,128)S(1)} %get-tuple-element.38), channel_id=1, source_target_pairs={{0,1},{1,2},{2,3},{3,0},{4,5},{5,6},{6,7},{7,4},{8,9},{9,10},{10,1... | collective-permute-start | bytes 393224 | tf_op jit(solution)/shard_map/ppermute | solution.py:608
  10.0 7.7 %collective-permute-start.1 = (f32[4,32,256]{2,1,0:T(8,128)S(1)}, f32[4,32,256]{2,1,0:T(8,128)S(1)}, u32[]{:S(2)}, u32[]{:S(2)}) collective-permute-start(f32[4,32,256]{2,1,0:T(8,128)S(1)} %get-tuple-element.39.refs_7_), channel_id=1, source_target_pairs={{0,3},{1,0},{2,1},{3,2},{4,7},{5,4},{6,5},{7,6},{8,11},{9,8},{10,9... | collective-permute-start | bytes 393224 | tf_op jit(solution)/shard_map/ppermute | solution.py:608
  12.3 11.7 %collective-permute-start.6 = (f32[16,256]{1,0:T(8,128)S(1)}, f32[16,256]{1,0:T(8,128)S(1)}, u32[]{:S(2)}, u32[]{:S(2)}) collective-permute-start(f32[16,256]{1,0:T(8,128)S(1)} %get-tuple-element.52), channel_id=1, source_target_pairs={{0,2},{1,3},{2,0},{3,1},{4,6},{5,7},{6,4},{7,5},{8,10},{9,11},{10,... | collective-permute-start | bytes 49160 | tf_op jit(solution)/shard_map/ppermute | solution.py:608
  17.9 6.0 %collective-permute-start.3 = (f32[16,256]{1,0:T(8,128)S(1)}, f32[16,256]{1,0:T(8,128)S(1)}, u32[]{:S(2)}, u32[]{:S(2)}) collective-permute-start(f32[16,256]{1,0:T(8,128)S(1)} %get-tuple-element.47), channel_id=1, source_target_pairs={{0,28},{4,0},{8,4},{12,8},{16,12},{20,16},{24,20},{28,24},{1,29},{... | collective-permute-start | bytes 49160 | tf_op jit(solution)/shard_map/ppermute | solution.py:608
  20.2 4.1 %collective-permute-start.5 = (f32[16,256]{1,0:T(8,128)S(1)}, f32[16,256]{1,0:T(8,128)S(1)}, u32[]{:S(2)}, u32[]{:S(2)}) collective-permute-start(f32[16,256]{1,0:T(8,128)S(1)} %get-tuple-element.49), channel_id=1, source_target_pairs={{0,4},{4,8},{8,12},{12,16},{16,20},{20,24},{24,28},{28,0},{1,5},{5... | collective-permute-start | bytes 49160 | tf_op jit(solution)/shard_map/ppermute | solution.py:608
  26.0 4.2 %copy-start.3 = (s32[8,512]{1,0:T(8,128)S(1)}, s32[8,512]{1,0:T(8,128)}, u32[]{:S(2)}) copy-start(s32[8,512]{1,0:T(8,128)} %refs_6_.7) | copy-start | bytes 49156
  26.0 11.2 %collective-permute-start.8 = (f32[328,256]{1,0:T(8,128)S(1)}, f32[328,256]{1,0:T(8,128)S(1)}, u32[]{:S(2)}, u32[]{:S(2)}) collective-permute-start(f32[328,256]{1,0:T(8,128)S(1)} %get-tuple-element.57.refs_3_.refs_6_.refs_8_), channel_id=1, source_target_pairs={{0,4},{4,8},{8,12},{12,16},{16,20},{20,24},{24,28},{28,0},{1,5},{5... | collective-permute-start | bytes 1007624 | tf_op jit(solution)/shard_map/ppermute | solution.py:608
  26.1 6.5 %copy-start.6 = (s32[8]{0:T(128)S(1)}, s32[8]{0:T(128)}, u32[]{:S(2)}) copy-start(s32[8]{0:T(128)} %refs_7_.1) | copy-start | bytes 100
  26.1 11.1 %collective-permute-start.7 = (f32[328,256]{1,0:T(8,128)S(1)}, f32[328,256]{1,0:T(8,128)S(1)}, u32[]{:S(2)}, u32[]{:S(2)}) collective-permute-start(f32[328,256]{1,0:T(8,128)S(1)} %get-tuple-element.60), channel_id=1, source_target_pairs={{0,28},{4,0},{8,4},{12,8},{16,12},{20,16},{24,20},{28,24},{1,29},{... | collective-permute-start | bytes 1007624 | tf_op jit(solution)/shard_map/ppermute | solution.py:608
  37.2 10.8 %copy-start.5 = (f32[8,3,512]{2,0,1:T(8,128)S(1)}, f32[8,3,512]{2,0,1:T(8,128)}, u32[]{:S(2)}) copy-start(f32[8,3,512]{2,0,1:T(8,128)} %param.12) | copy-start | bytes 147460
  41.5 5.7 %collective-permute-start.9 = (f32[8,512]{1,0:T(8,128)S(1)}, f32[8,512]{1,0:T(8,128)S(1)}, u32[]{:S(2)}, u32[]{:S(2)}) collective-permute-start(f32[8,512]{1,0:T(8,128)S(1)} %get-tuple-element.63), channel_id=1, source_target_pairs={{0,3},{1,2},{2,1},{3,0},{4,7},{5,6},{6,5},{7,4},{8,11},{9,10},{10,... | collective-permute-start | bytes 49160 | tf_op jit(solution)/shard_map/ppermute | solution.py:613
  43.4 4.6 %collective-permute-start.10 = (f32[8,512]{1,0:T(8,128)S(1)}, f32[8,512]{1,0:T(8,128)S(1)}, u32[]{:S(2)}, u32[]{:S(2)}) collective-permute-start(f32[8,512]{1,0:T(8,128)S(1)} %get-tuple-element.64), channel_id=1, source_target_pairs={{0,2},{1,3},{2,0},{3,1},{4,6},{5,7},{6,4},{7,5},{8,10},{9,11},{10,... | collective-permute-start | bytes 49160 | tf_op jit(solution)/shard_map/ppermute | solution.py:613
  44.1 4.0 %collective-permute-start.11 = (f32[8,512]{1,0:T(8,128)S(1)}, f32[8,512]{1,0:T(8,128)S(1)}, u32[]{:S(2)}, u32[]{:S(2)}) collective-permute-start(f32[8,512]{1,0:T(8,128)S(1)} %get-tuple-element.65.refs_2_), channel_id=1, source_target_pairs={{0,1},{1,0},{2,3},{3,2},{4,5},{5,4},{6,7},{7,6},{8,9},{9,8},{10,11... | collective-permute-start | bytes 49160 | tf_op jit(solution)/shard_map/ppermute | solution.py:613

commit v6 on v5

--- a/solution.py
+++ b/solution.py
@@ -457,7 +457,13 @@
         copy.wait()
 
 
-def pair_kernel(begin, end, pair_tiles, vel, rows, cols, left, right, noise, *refs):
+def pair_kernel(begin, end, *refs):
+    one_pair, steps, finish = pair_parts(begin, end, *refs)
+    lax.fori_loop(0, steps, lambda i, carry: one_pair(i), None, unroll=4)
+    finish()
+
+
+def pair_parts(begin, end, pair_tiles, vel, rows, cols, left, right, noise, *refs):
     base, theta, along, acc = refs[-4:]
     tile = noise.shape[-1]
     count = cols.shape[2]
@@ -476,7 +482,7 @@
                 left[begin + g, second], right[begin + g, first], preferred_element_type=F32
             )
 
-    def one_pair(i, carry):
+    def one_pair(i):
         g, p = i // pairs, i % pairs
         first = pair_tiles[begin + g, 0, p]
         second = pair_tiles[begin + g, 1, p]
@@ -492,16 +498,31 @@
             total = here if not total else [a + b for a, b in zip(total, here)]
         for c in range(3):
             acc[g, first, c] += total[c]
-        return carry
-
-    lax.fori_loop(0, patches * pairs, one_pair, 0, unroll=4)
-    for g in range(patches):
-        for c in range(3):
-            force = jnp.concatenate(
-                [jnp.sum(acc[g, j, c], axis=0, keepdims=True) for j in range(count)], axis=1
-            )
-            speed = vel[c, begin + g : begin + g + 1, :]
-            base[c, begin + g : begin + g + 1, :] = 0.5 * speed + 0.04 * force
+
+    def finish():
+        for g in range(patches):
+            for c in range(3):
+                force = jnp.concatenate(
+                    [jnp.sum(acc[g, j, c], axis=0, keepdims=True) for j in range(count)], axis=1
+                )
+                speed = vel[c, begin + g : begin + g + 1, :]
+                base[c, begin + g : begin + g + 1, :] = 0.5 * speed + 0.04 * force
+
+    return one_pair, patches * pairs, finish
+
+
+def sums_and_pairs_kernel(n, per, begin, end, *refs):
+    sums, rest = refs[: n + 2], refs[n + 2 :]
+    pairs, (total, base, table, theta, along, acc) = rest[:7], rest[8:]
+    one_pair, steps, finish = pair_parts(begin, end, *pairs, base, theta, along, acc)
+    patches = sums[1].shape[0]
+
+    def beside(g):
+        for i in range(g * steps // patches, (g + 1) * steps // patches):
+            one_pair(i)
+
+    scatter_kernel(n, per, beside, *sums, total, table)
+    finish()
 
 
 def split(value):
@@ -525,7 +546,7 @@
     return place == want
 
 
-def scatter_kernel(n, per, owner, voxel, vel, *refs):
+def scatter_kernel(n, per, beside, owner, voxel, vel, *refs):
     sent, out, table = refs[: n - 1], refs[n - 1], refs[n]
     me = lax.axis_index("xs")
     beads = voxel.shape[1]
@@ -556,6 +577,7 @@
         out[3] += lax.dot_general(
             jnp.where(at_row, one, zero), lanes, (((1,), (1,)), ((), ())), preferred_element_type=F32
         )
+        beside(g)
 
 
 def found_flow(voxel, flow, layers, field, store):
@@ -564,8 +586,8 @@
     for c in range(3):
         for i, x in enumerate(layers):
             high, low = split(flow[c, x])
-            field[c, i * ROWS : (i + 1) * ROWS, 0:256] = high
-            field[c, i * ROWS : (i + 1) * ROWS, 256:512] = low
+            field[c * rows + i * ROWS : c * rows + (i + 1) * ROWS, 0:256] = high
+            field[c * rows + i * ROWS : c * rows + (i + 1) * ROWS, 256:512] = low
     place = lax.broadcasted_iota(I32, (rows, beads), 0)
     step = (layers[1] - layers[0] - 1) * ROWS
     place = place + layers[0] * ROWS + jnp.where(place >= ROWS, step, 0)
@@ -575,11 +597,10 @@
         lanes = jnp.where(one_hot(index & 255, 256), one, zero)
         lanes2 = jnp.concatenate([lanes, lanes], axis=0)
         at_row = place == (index >> 8)
+        found = jnp.dot(field[...], lanes2, preferred_element_type=F32)
         for c in range(3):
-            found = lax.dot_general(
-                field[c], lanes2, (((1,), (0,)), ((), ())), preferred_element_type=F32
-            )
-            store(g, c, jnp.sum(jnp.where(at_row, found, 0.0), axis=0, keepdims=True))
+            part = jnp.where(at_row, found[c * rows : (c + 1) * rows], 0.0)
+            store(g, c, jnp.sum(part, axis=0, keepdims=True))
 
 
 def field_kernel(total, flow, field):
@@ -725,7 +746,6 @@
     post2, bits, fwd2 = outer(False, after, edge_after, post2, bits, [])
     before2 = shift(fwd2, "ax", 1)
 
-    base = pair_call(cuts[1], patches, *bead_args, [base], [fwd2])
     out, flow, part = call(
         functools.partial(final_middle_kernel, nx),
         [post2, bits, patch_voxel],
@@ -736,20 +756,27 @@
         out_specs=[ANY_SPEC, VMEM_SPEC, VMEM_SPEC],
         scratch_shapes=[
             vmem((nx - 2, 19, ROWS, lanes), F32),
-            vmem((3, (nx - 2) * ROWS, 2 * lanes), BF16),
+            vmem((3 * (nx - 2) * ROWS, 2 * lanes), BF16),
             dma((nx - 2,)),
         ],
     )
-    total = call(
-        functools.partial(scatter_kernel, n, per),
-        [patch_owner, patch_voxel, velocities] + sent,
-        arr(4, nx * ROWS, lanes),
+    last_pairs = (patches - cuts[1]) * pair_noise.shape[1]
+    total, base = call(
+        functools.partial(sums_and_pairs_kernel, n, per, cuts[1], patches),
+        [patch_owner, patch_voxel, velocities] + sent + list(bead_args) + [base],
+        [arr(4, nx * ROWS, lanes), arr(*velocities.shape)],
         "bead_sums",
         cost(1000, 1000),
         after=[fwd2],
-        specs={0: SMEM_SPEC},
-        out_specs=VMEM_SPEC,
-        scratch_shapes=[vmem((n, per, 8, beads), F32)],
+        specs={0: SMEM_SPEC, n + 2: SMEM_SPEC},
+        out_specs=[VMEM_SPEC] * 2,
+        input_output_aliases={n + 9: 1},
+        scratch_shapes=[
+            vmem((n, per, 8, beads), F32),
+            vmem((last_pairs, 128, 128), F32),
+            vmem((last_pairs, 128, 128), F32),
+            vmem((patches - cuts[1], tiles, 3, 8, 128), F32),
+        ],
     )
     out, flow, *flows = call(
         functools.partial(final_outer_kernel, n, per, nx),
@@ -765,7 +792,7 @@
             vmem((2, 5, PAD, lanes), F32),
             vmem((2, 19, ROWS, lanes), F32),
             vmem((patches, 8, beads), F32),
-            vmem((3, 2 * ROWS, 2 * lanes), BF16),
+            vmem((3 * 2 * ROWS, 2 * lanes), BF16),
             dma((2,)),
         ],
     )

time: 48.9 us -> 48.4 us (0.990)
  Pallas kernels: 28.3 us -> 27.3 us
  waiting for transfers between devices: 2.18 us -> 2.78 us
    pallas_call x13 -> x12, Pallas kernels: 28.3 us -> 27.3 us  [call(): pl.pallas_call(body, in_specs=[specs.get(i, VMEM_SPEC) for i in range(cou...]
    ppermute x9, waiting for transfers between devices: 1.01 us -> 1.6 us  [shift(): return lax.ppermute(value, axis, [(i, (i + by) % n) for i in range(n)])]
  transfers between devices with their start and end apart: 12 -> 12, of which waited for: 4 -> 5; matrix products, arithmetic and copies ran while one was open for 0% -> 0% of each run, Pallas kernels for 35% -> 34%
where the time goes in v6:
time: 48.4 us; the launch traced here: 48.3 us
  Pallas kernels  27.3 us (56%)
  starting transfers between devices  17.4 us (36%)
  waiting for transfers between devices  2.78 us (6%)
  between operations  0.79 us (2%)
    pallas_call x12, Pallas kernels, call(): pl.pallas_call(body, in_specs=[specs.get(i, VMEM_SPEC) for i in range(cou...  27.3 us
    ppermute x9, starting transfers between devices, shift(): return lax.ppermute(value, axis, [(i, (i + by) % n) for i in range(n)])  13 us
    ppermute x3, starting transfers between devices, swap(): return lax.ppermute(value, axis, [(i, i ^ by) for i in range(n)])  4.45 us
    ppermute x9, waiting for transfers between devices, shift(): return lax.ppermute(value, axis, [(i, (i + by) % n) for i in range(n)])  1.6 us
    ppermute x3, waiting for transfers between devices, swap(): return lax.ppermute(value, axis, [(i, i ^ by) for i in range(n)])  1.17 us
  transfers between devices with their start and end apart: 12, of which 5 were waited for; matrix products, arithmetic and copies ran while one was open for 0% of the time, Pallas kernels for 34%

profile of v6, /device:TPU:0, one launch (start us, length us, event | category | flops | bytes accessed | tf_op | source)
XLA Modules:
  0.0 48.3 jit_solution(4467778949299629608)
XLA Ops:
  0.6 0.0 copy-start.1
  0.6 0.0 copy-start
  0.7 0.0 copy-start.4
  0.7 4.4 %collide_first.1 = (f32[19,4,88,256]{3,2,1,0:T(8,128)S(1)}, f32[384,256]{1,0:T(8,128)S(1)}, f32[384,256]{1,0:T(8,128)S(1)}, f32[4,32,256]{2,1,0:T(8,128)S(1)}, f...) custom-call(f32[19,4,64,256]{3,2,1,0:T(8,128)} %refs_0_.2, ...), custom_call_target="tpu_custom_call" | custom-call | flops 3000000000 | bytes 11000000 | tf_op jit(solution)/shard_map/collide_first/pallas_call | solution.py:63
  5.1 0.0 copy-start.2
  5.1 3.4 %collective-permute-start.2 = (f32[384,256]{1,0:T(8,128)S(1)}, f32[384,256]{1,0:T(8,128)S(1)}, u32[]{:S(2)}, u32[]{:S(2)}) collective-permute-start(f32[384,256]{1,0:T(8,128)S(1)} %get-tuple-element.48), channel_id=1, source_target_pairs={{0,28},{4,0},{8,4},{12,8},{16,12},{20,16},{24,20},{28,24},{1,29},{... | collective-permute-start | bytes 1179656 | tf_op jit(solution)/shard_map/ppermute | solution.py:629
  8.5 0.0 collective-permute-start.4
  8.5 1.6 %collective-permute-start = (f32[4,32,256]{2,1,0:T(8,128)S(1)}, f32[4,32,256]{2,1,0:T(8,128)S(1)}, u32[]{:S(2)}, u32[]{:S(2)}) collective-permute-start(f32[4,32,256]{2,1,0:T(8,128)S(1)} %get-tuple-element.40), channel_id=1, source_target_pairs={{0,1},{1,2},{2,3},{3,0},{4,5},{5,6},{6,7},{7,4},{8,9},{9,10},{10,1... | collective-permute-start | bytes 393224 | tf_op jit(solution)/shard_map/ppermute | solution.py:629
  10.0 2.2 %collective-permute-start.1 = (f32[4,32,256]{2,1,0:T(8,128)S(1)}, f32[4,32,256]{2,1,0:T(8,128)S(1)}, u32[]{:S(2)}, u32[]{:S(2)}) collective-permute-start(f32[4,32,256]{2,1,0:T(8,128)S(1)} %get-tuple-element.41.refs_7_), channel_id=1, source_target_pairs={{0,3},{1,0},{2,1},{3,2},{4,7},{5,4},{6,5},{7,6},{8,11},{9,8},{10,9... | collective-permute-start | bytes 393224 | tf_op jit(solution)/shard_map/ppermute | solution.py:629
  12.3 0.8 %collective-permute-start.6 = (f32[16,256]{1,0:T(8,128)S(1)}, f32[16,256]{1,0:T(8,128)S(1)}, u32[]{:S(2)}, u32[]{:S(2)}) collective-permute-start(f32[16,256]{1,0:T(8,128)S(1)} %get-tuple-element.54), channel_id=1, source_target_pairs={{0,2},{1,3},{2,0},{3,1},{4,6},{5,7},{6,4},{7,5},{8,10},{9,11},{10,... | collective-permute-start | bytes 49160 | tf_op jit(solution)/shard_map/ppermute | solution.py:629
  13.1 0.0 copy-done.1
  13.1 0.0 copy-done
  13.1 0.0 copy-done.4
  13.1 4.0 %pair_forces.2.refs_4_.refs_7_ = f32[3,8,512]{2,1,0:T(8,128)S(1)} custom-call(s32[8,2,8]{2,1,0:T(2,128)S(1)} %bitcast.10, f32[3,8,512]{2,1,0:T(8,128)S(1)} %bitcast.6, f32[8,3,4,8,128]{4,3,2,1,0:T(8,128)S(1)} %get-tuple-element.42.refs_2_.refs_8_, f32[8,3,4,128,128]{4,3,2,1,0:T(8,128)S(1)} %get-tuple-element.43.refs_3_.refs_9_, ...), custom_call_target="tpu_custom_call" | custom-call | flops 1000 | bytes 1000 | tf_op jit(solution)/shard_map/pair_forces/pallas_call | solution.py:63
  17.1 0.0 collective-permute-done.refs_2_.refs_3_
  17.1 0.7 %collective-permute-done.1.refs_3_.refs_5_ = f32[4,32,256]{2,1,0:T(8,128)S(1)} collective-permute-done((f32[4,32,256]{2,1,0:T(8,128)S(1)}, f32[4,32,256]{2,1,0:T(8,128)S(1)}, u32[]{:S(2)}, u32[]{:S(2)}) %collective-permute-start.1) | collective-permute-done | bytes 131104 | tf_op jit(solution)/shard_map/ppermute | solution.py:629
  17.8 0.0 copy-done.2
  17.8 0.2 edges.1
  17.9 2.3 %collective-permute-start.3 = (f32[16,256]{1,0:T(8,128)S(1)}, f32[16,256]{1,0:T(8,128)S(1)}, u32[]{:S(2)}, u32[]{:S(2)}) collective-permute-start(f32[16,256]{1,0:T(8,128)S(1)} %get-tuple-element.49), channel_id=1, source_target_pairs={{0,28},{4,0},{8,4},{12,8},{16,12},{20,16},{24,20},{28,24},{1,29},{... | collective-permute-start | bytes 49160 | tf_op jit(solution)/shard_map/ppermute | solution.py:629
  20.2 0.0 collective-permute-start.5
  20.2 2.1 %pair_forces.3.refs_6_.refs_13_ = f32[3,8,512]{2,1,0:T(8,128)S(1)} custom-call(s32[8,2,8]{2,1,0:T(2,128)S(1)} %bitcast.11, f32[3,8,512]{2,1,0:T(8,128)S(1)} %bitcast.7, f32[8,3,4,8,128]{4,3,2,1,0:T(8,128)S(1)} %get-tuple-element.42.refs_2_.refs_8_, f32[8,3,4,128,128]{4,3,2,1,0:T(8,128)S(1)} %get-tuple-element.43.refs_3_.refs_9_, ...), custom_call_target="tpu_custom_call", output_to_operand_aliasing={{}: (7, {})} | custom-call | flops 1000 | bytes 1000 | tf_op jit(solution)/shard_map/pair_forces/pallas_call | solution.py:63
  22.3 1.6 %middle_layers.1 = (f32[19,4,88,256]{3,2,1,0:T(8,128)S(1)}, s32[4,72,256]{2,1,0:T(8,128)S(1)}) custom-call(f32[19,4,88,256]{3,2,1,0:T(8,128)S(1)} %get-tuple-element.46.refs_0_, s32[4,88,256]{2,1,0:T(8,128)S(1)} %get-tuple-element.47.refs_1_.refs_8_), custom_call_target="tpu_custom_call" | custom-call | flops 1000 | bytes 1000 | tf_op jit(solution)/shard_map/middle_layers/pallas_call | solution.py:63
  23.9 0.0 collective-permute-done.6.refs_9_.refs_4_
  24.0 0.0 collective-permute-done.3.refs_8_.refs_3_
  24.0 0.3 collective-permute-done.5.refs_3_
  24.3 0.0 collective-permute-done.2.refs_7_.refs_2_
  24.3 0.0 collective-permute-done.4.refs_2_
  24.3 0.9 %first_layer.1 = (f32[19,4,88,256]{3,2,1,0:T(8,128)S(1)}, s32[4,72,256]{2,1,0:T(8,128)S(1)}, f32[328,256]{1,0:T(8,128)S(1)}) custom-call(f32[19,4,88,256]{3,2,1,0:T(8,128)S(1)} %get-tuple-element.46.refs_0_, s32[4,88,256]{2,1,0:T(8,128)S(1)} %get-tuple-element.47.refs_1_.refs_8_, ...), custom_call_target="tpu_custom_call", output_to_operand_aliasing={{0}: (4, {}), {1}: (5, {})} | custom-call | flops 1000 | bytes 1000 | tf_op jit(solution)/shard_map/first_layer/pallas_call | solution.py:63
  25.2 0.0 copy-start.3
  25.2 0.9 %last_layer.1 = (f32[19,4,88,256]{3,2,1,0:T(8,128)S(1)}, s32[4,72,256]{2,1,0:T(8,128)S(1)}, f32[328,256]{1,0:T(8,128)S(1)}) custom-call(f32[19,4,88,256]{3,2,1,0:T(8,128)S(1)} %get-tuple-element.46.refs_0_, s32[4,88,256]{2,1,0:T(8,128)S(1)} %get-tuple-element.47.refs_1_.refs_8_, ...), custom_call_target="tpu_custom_call", output_to_operand_aliasing={{0}: (4, {}), {1}: (5, {})} | custom-call | flops 1000 | bytes 1000 | tf_op jit(solution)/shard_map/last_layer/pallas_call | solution.py:63
  26.0 0.0 copy-start.6
  26.0 0.1 collective-permute-start.8
  26.1 2.6 %collective-permute-start.7 = (f32[328,256]{1,0:T(8,128)S(1)}, f32[328,256]{1,0:T(8,128)S(1)}, u32[]{:S(2)}, u32[]{:S(2)}) collective-permute-start(f32[328,256]{1,0:T(8,128)S(1)} %get-tuple-element.62), channel_id=1, source_target_pairs={{0,28},{4,0},{8,4},{12,8},{16,12},{20,16},{24,20},{28,24},{1,29},{... | collective-permute-start | bytes 1007624 | tf_op jit(solution)/shard_map/ppermute | solution.py:629
  28.7 0.0 copy-done.3
  28.7 2.4 %final_middle.1 = (f32[19,4,64,256]{3,2,1,0:T(8,128)}, f32[3,4,64,256]{3,2,1,0:T(8,128)S(1)}, f32[8,8,512]{2,1,0:T(8,128)S(1)}) custom-call(f32[19,4,88,256]{3,2,1,0:T(8,128)S(1)} %get-tuple-element.57.refs_0_.refs_2_, s32[4,72,256]{2,1,0:T(8,128)S(1)} %get-tuple-element.58.refs_1_.refs_3_, s32[8,512]{1,0:T(8,128)S(1)} %copy-done.3, ...), custom_call_target="tpu_custom_call" | custom-call | flops 1000 | bytes 1000 | tf_op jit(solution)/shard_map/final_middle/pallas_call | solution.py:63
  31.2 0.0 copy-done.6
  31.2 5.1 %bead_sums.1 = (f32[4,256,256]{2,1,0:T(8,128)S(1)}, f32[3,8,512]{2,1,0:T(8,128)S(1)}) custom-call(s32[8]{0:T(128)S(1)} %copy-done.6, s32[8,512]{1,0:T(8,128)S(1)} %copy-done.3, f32[3,8,512]{2,1,0:T(8,128)S(1)} %bitcast.8, f32[4,32,256]{2,1,0:T(8,128)S(1)} %collective-permute-done.refs_2_.refs_3_, ...), custom_call_target="tpu_custom_call", output_to_operand_aliasing={{1}: (13, {})} | custom-call | flops 1000 | bytes 1000 | tf_op jit(solution)/shard_map/bead_sums/pallas_call | solution.py:63
  36.3 0.6 %collective-permute-done.8.refs_5_ = f32[328,256]{1,0:T(8,128)S(1)} collective-permute-done((f32[328,256]{1,0:T(8,128)S(1)}, f32[328,256]{1,0:T(8,128)S(1)}, u32[]{:S(2)}, u32[]{:S(2)}) %collective-permute-start.8) | collective-permute-done | bytes 335904 | tf_op jit(solution)/shard_map/ppermute | solution.py:629
  36.9 0.0 collective-permute-done.7.refs_4_
  36.9 0.0 copy-start.5
  36.9 4.1 %final_outer.1 = (f32[19,4,64,256]{3,2,1,0:T(8,128)}, f32[3,4,64,256]{3,2,1,0:T(8,128)S(1)}, f32[8,512]{1,0:T(8,128)S(1)}, f32[8,512]{1,0:T(8,128)S(1)}, f32[8,512]{1,0:T(8,128)S(1)}, /*index=5*/f32[8,512]{1,0:T(8,128)S(1)}) custom-call(f32[19,4,64,256]{3,2,1,0:T(8,128)} %get-tuple-element.60.refs_0_, ...), custom_call_target="tpu_custom_call", output_to_operand_aliasing={{0}: (0, {}), {1}: (1, {})} | custom-call | flops 1000 | bytes 1000 | tf_op jit(solution)/shard_map/final_outer/pallas_call | solution.py:63
  41.0 2.0 %collective-permute-start.9 = (f32[8,512]{1,0:T(8,128)S(1)}, f32[8,512]{1,0:T(8,128)S(1)}, u32[]{:S(2)}, u32[]{:S(2)}) collective-permute-start(f32[8,512]{1,0:T(8,128)S(1)} %get-tuple-element.67), channel_id=1, source_target_pairs={{0,3},{1,2},{2,1},{3,0},{4,7},{5,6},{6,5},{7,4},{8,11},{9,10},{10,... | collective-permute-start | bytes 49160 | tf_op jit(solution)/shard_map/ppermute | solution.py:634
  43.0 0.6 %collective-permute-start.10 = (f32[8,512]{1,0:T(8,128)S(1)}, f32[8,512]{1,0:T(8,128)S(1)}, u32[]{:S(2)}, u32[]{:S(2)}) collective-permute-start(f32[8,512]{1,0:T(8,128)S(1)} %get-tuple-element.68), channel_id=1, source_target_pairs={{0,2},{1,3},{2,0},{3,1},{4,6},{5,7},{6,4},{7,5},{8,10},{9,11},{10,... | collective-permute-start | bytes 49160 | tf_op jit(solution)/shard_map/ppermute | solution.py:634
  43.6 1.9 %collective-permute-start.11 = (f32[8,512]{1,0:T(8,128)S(1)}, f32[8,512]{1,0:T(8,128)S(1)}, u32[]{:S(2)}, u32[]{:S(2)}) collective-permute-start(f32[8,512]{1,0:T(8,128)S(1)} %get-tuple-element.69.refs_2_), channel_id=1, source_target_pairs={{0,1},{1,0},{2,3},{3,2},{4,5},{5,4},{6,7},{7,6},{8,9},{9,8},{10,11... | collective-permute-start | bytes 49160 | tf_op jit(solution)/shard_map/ppermute | solution.py:634
  45.5 1.0 %drag_field.1 = f32[3,4,64,256]{3,2,1,0:T(8,128)} custom-call(f32[4,256,256]{2,1,0:T(8,128)S(1)} %get-tuple-element.64.refs_9_.refs_0_, f32[3,4,64,256]{3,2,1,0:T(8,128)S(1)} %get-tuple-element.73.refs_1_, f32[8,512]{1,0:T(8,128)S(1)} %get-tuple-element.69.refs_2_), custom_call_target="tpu_custom_call" | custom-call | flops 1000 | bytes 1000 | tf_op jit(solution)/shard_map/drag_field/pallas_call | solution.py:63
  46.4 0.2 collective-permute-done.9.refs_2_
  46.6 1.0 %collective-permute-done.10.refs_3_ = f32[8,512]{1,0:T(8,128)S(1)} collective-permute-done((f32[8,512]{1,0:T(8,128)S(1)}, f32[8,512]{1,0:T(8,128)S(1)}, u32[]{:S(2)}, u32[]{:S(2)}) %collective-permute-start.10) | collective-permute-done | bytes 16416 | tf_op jit(solution)/shard_map/ppermute | solution.py:634
  47.6 0.0 collective-permute-done.11.refs_4_
  47.6 0.0 copy-done.5
  47.6 0.7 %bead_update.1 = (f32[3,8,512]{2,1,0:T(8,128)}, f32[3,8,512]{2,1,0:T(8,128)}) custom-call(f32[3,8,512]{2,1,0:T(8,128)S(1)} %bitcast.14, f32[3,8,512]{2,1,0:T(8,128)S(1)} %get-tuple-element.65.refs_10_.refs_1_, f32[8,512]{1,0:T(8,128)S(1)} %collective-permute-done.9.refs_2_, f32[8,512]{1,0:T(8,128)S(1)} %collective-permute-done.10.refs_3_, ...), custom_call_target="tpu_custom_call" | custom-call | flops 1000 | bytes 1000 | tf_op jit(solution)/shard_map/bead_update/pallas_call | solution.py:63
Async XLA Ops:
  0.6 12.4 %copy-start.1 = (f32[8,3,512]{2,0,1:T(8,128)S(1)}, f32[8,3,512]{2,0,1:T(8,128)}, u32[]{:S(2)}) copy-start(f32[8,3,512]{2,0,1:T(8,128)} %param.13) | copy-start | bytes 147460
  0.6 12.4 %copy-start = (bf16[8,8,128,128]{3,2,1,0:T(8,128)(2,1)S(1)}, bf16[8,8,128,128]{3,2,1,0:T(8,128)(2,1)}, u32[]{:S(2)}) copy-start(bf16[8,8,128,128]{3,2,1,0:T(8,128)(2,1)} %refs_12_.1) | copy-start | bytes 6291460
  0.7 12.4 %copy-start.4 = (s32[8,8,2]{1,2,0:T(2,128)S(1)}, s32[8,8,2]{1,2,0:T(2,128)}, u32[]{:S(2)}) copy-start(s32[8,8,2]{1,2,0:T(2,128)} %param.14) | copy-start | bytes 1540
  5.1 12.7 %copy-start.2 = (s32[4,64,256]{2,1,0:T(8,128)S(1)}, s32[4,64,256]{2,1,0:T(8,128)}, u32[]{:S(2)}) copy-start(s32[4,64,256]{2,1,0:T(8,128)} %refs_1_.4) | copy-start | bytes 786436
  5.1 19.2 %collective-permute-start.2 = (f32[384,256]{1,0:T(8,128)S(1)}, f32[384,256]{1,0:T(8,128)S(1)}, u32[]{:S(2)}, u32[]{:S(2)}) collective-permute-start(f32[384,256]{1,0:T(8,128)S(1)} %get-tuple-element.48), channel_id=1, source_target_pairs={{0,28},{4,0},{8,4},{12,8},{16,12},{20,16},{24,20},{28,24},{1,29},{... | collective-permute-start | bytes 1179656 | tf_op jit(solution)/shard_map/ppermute | solution.py:629
  8.5 15.8 %collective-permute-start.4 = (f32[384,256]{1,0:T(8,128)S(1)}, f32[384,256]{1,0:T(8,128)S(1)}, u32[]{:S(2)}, u32[]{:S(2)}) collective-permute-start(f32[384,256]{1,0:T(8,128)S(1)} %get-tuple-element.50), channel_id=1, source_target_pairs={{0,4},{4,8},{8,12},{12,16},{16,20},{20,24},{24,28},{28,0},{1,5},{5... | collective-permute-start | bytes 1179656 | tf_op jit(solution)/shard_map/ppermute | solution.py:629
  8.5 8.6 %collective-permute-start = (f32[4,32,256]{2,1,0:T(8,128)S(1)}, f32[4,32,256]{2,1,0:T(8,128)S(1)}, u32[]{:S(2)}, u32[]{:S(2)}) collective-permute-start(f32[4,32,256]{2,1,0:T(8,128)S(1)} %get-tuple-element.40), channel_id=1, source_target_pairs={{0,1},{1,2},{2,3},{3,0},{4,5},{5,6},{6,7},{7,4},{8,9},{9,10},{10,1... | collective-permute-start | bytes 393224 | tf_op jit(solution)/shard_map/ppermute | solution.py:629
  10.0 7.7 %collective-permute-start.1 = (f32[4,32,256]{2,1,0:T(8,128)S(1)}, f32[4,32,256]{2,1,0:T(8,128)S(1)}, u32[]{:S(2)}, u32[]{:S(2)}) collective-permute-start(f32[4,32,256]{2,1,0:T(8,128)S(1)} %get-tuple-element.41.refs_7_), channel_id=1, source_target_pairs={{0,3},{1,0},{2,1},{3,2},{4,7},{5,4},{6,5},{7,6},{8,11},{9,8},{10,9... | collective-permute-start | bytes 393224 | tf_op jit(solution)/shard_map/ppermute | solution.py:629
  12.3 11.7 %collective-permute-start.6 = (f32[16,256]{1,0:T(8,128)S(1)}, f32[16,256]{1,0:T(8,128)S(1)}, u32[]{:S(2)}, u32[]{:S(2)}) collective-permute-start(f32[16,256]{1,0:T(8,128)S(1)} %get-tuple-element.54), channel_id=1, source_target_pairs={{0,2},{1,3},{2,0},{3,1},{4,6},{5,7},{6,4},{7,5},{8,10},{9,11},{10,... | collective-permute-start | bytes 49160 | tf_op jit(solution)/shard_map/ppermute | solution.py:629
  17.9 6.0 %collective-permute-start.3 = (f32[16,256]{1,0:T(8,128)S(1)}, f32[16,256]{1,0:T(8,128)S(1)}, u32[]{:S(2)}, u32[]{:S(2)}) collective-permute-start(f32[16,256]{1,0:T(8,128)S(1)} %get-tuple-element.49), channel_id=1, source_target_pairs={{0,28},{4,0},{8,4},{12,8},{16,12},{20,16},{24,20},{28,24},{1,29},{... | collective-permute-start | bytes 49160 | tf_op jit(solution)/shard_map/ppermute | solution.py:629
  20.2 4.1 %collective-permute-start.5 = (f32[16,256]{1,0:T(8,128)S(1)}, f32[16,256]{1,0:T(8,128)S(1)}, u32[]{:S(2)}, u32[]{:S(2)}) collective-permute-start(f32[16,256]{1,0:T(8,128)S(1)} %get-tuple-element.51), channel_id=1, source_target_pairs={{0,4},{4,8},{8,12},{12,16},{16,20},{20,24},{24,28},{28,0},{1,5},{5... | collective-permute-start | bytes 49160 | tf_op jit(solution)/shard_map/ppermute | solution.py:629
  25.2 3.6 %copy-start.3 = (s32[8,512]{1,0:T(8,128)S(1)}, s32[8,512]{1,0:T(8,128)}, u32[]{:S(2)}) copy-start(s32[8,512]{1,0:T(8,128)} %refs_6_.5) | copy-start | bytes 49156
  26.0 5.1 %copy-start.6 = (s32[8]{0:T(128)S(1)}, s32[8]{0:T(128)}, u32[]{:S(2)}) copy-start(s32[8]{0:T(128)} %refs_7_.1) | copy-start | bytes 100
  26.0 10.8 %collective-permute-start.8 = (f32[328,256]{1,0:T(8,128)S(1)}, f32[328,256]{1,0:T(8,128)S(1)}, u32[]{:S(2)}, u32[]{:S(2)}) collective-permute-start(f32[328,256]{1,0:T(8,128)S(1)} %get-tuple-element.59.refs_3_.refs_14_), channel_id=1, source_target_pairs={{0,4},{4,8},{8,12},{12,16},{16,20},{20,24},{24,28},{28,0},{1,5},{5... | collective-permute-start | bytes 1007624 | tf_op jit(solution)/shard_map/ppermute | solution.py:629
  26.1 10.8 %collective-permute-start.7 = (f32[328,256]{1,0:T(8,128)S(1)}, f32[328,256]{1,0:T(8,128)S(1)}, u32[]{:S(2)}, u32[]{:S(2)}) collective-permute-start(f32[328,256]{1,0:T(8,128)S(1)} %get-tuple-element.62), channel_id=1, source_target_pairs={{0,28},{4,0},{8,4},{12,8},{16,12},{20,16},{24,20},{28,24},{1,29},{... | collective-permute-start | bytes 1007624 | tf_op jit(solution)/shard_map/ppermute | solution.py:629
  36.9 10.7 %copy-start.5 = (f32[8,3,512]{2,0,1:T(8,128)S(1)}, f32[8,3,512]{2,0,1:T(8,128)}, u32[]{:S(2)}) copy-start(f32[8,3,512]{2,0,1:T(8,128)} %param.12) | copy-start | bytes 147460
  41.0 5.6 %collective-permute-start.9 = (f32[8,512]{1,0:T(8,128)S(1)}, f32[8,512]{1,0:T(8,128)S(1)}, u32[]{:S(2)}, u32[]{:S(2)}) collective-permute-start(f32[8,512]{1,0:T(8,128)S(1)} %get-tuple-element.67), channel_id=1, source_target_pairs={{0,3},{1,2},{2,1},{3,0},{4,7},{5,6},{6,5},{7,4},{8,11},{9,10},{10,... | collective-permute-start | bytes 49160 | tf_op jit(solution)/shard_map/ppermute | solution.py:634
  43.0 4.6 %collective-permute-start.10 = (f32[8,512]{1,0:T(8,128)S(1)}, f32[8,512]{1,0:T(8,128)S(1)}, u32[]{:S(2)}, u32[]{:S(2)}) collective-permute-start(f32[8,512]{1,0:T(8,128)S(1)} %get-tuple-element.68), channel_id=1, source_target_pairs={{0,2},{1,3},{2,0},{3,1},{4,6},{5,7},{6,4},{7,5},{8,10},{9,11},{10,... | collective-permute-start | bytes 49160 | tf_op jit(solution)/shard_map/ppermute | solution.py:634
  43.6 4.0 %collective-permute-start.11 = (f32[8,512]{1,0:T(8,128)S(1)}, f32[8,512]{1,0:T(8,128)S(1)}, u32[]{:S(2)}, u32[]{:S(2)}) collective-permute-start(f32[8,512]{1,0:T(8,128)S(1)} %get-tuple-element.69.refs_2_), channel_id=1, source_target_pairs={{0,1},{1,0},{2,3},{3,2},{4,5},{5,4},{6,7},{7,6},{8,9},{9,8},{10,11... | collective-permute-start | bytes 49160 | tf_op jit(solution)/shard_map/ppermute | solution.py:634

commit v7 on v6

--- a/solution.py
+++ b/solution.py
@@ -209,8 +209,8 @@
                 cols[g, c, j] = wide[:, c * tile : (c + 1) * tile]
 
 
-def collide_kernel(n, per, nx, pop, mask, pos, vel, post, fwd, bwd, up, down, rows, cols, left, right, *rest):
-    others, (here, flags, spots, speeds, sems, small) = rest[: n - 3], rest[n - 3 :]
+def collide_kernel(n, per, nx, pop, mask, vel, post, fwd, bwd, up, down, *rest):
+    others, (here, flags, speeds, sems, small) = rest[: n - 3], rest[n - 3 :]
     order = [(x, h) for x in [0, nx - 1] + list(range(1, nx - 1)) for h in range(1)]
     span = ROWS // 1
     copies = [
@@ -221,11 +221,10 @@
     ]
     extra = [
         pltpu.make_async_copy(vel, speeds, small.at[0]),
-        pltpu.make_async_copy(pos, spots, small.at[1]),
-        pltpu.make_async_copy(mask, flags, small.at[2]),
+        pltpu.make_async_copy(mask, flags, small.at[1]),
     ]
     ahead = 3
-    for copy in extra[:2] + copies[:ahead] + extra[2:]:
+    for copy in copies[:ahead] + extra:
         copy.start()
     me = lax.axis_index("xs")
     extra[0].wait()
@@ -243,8 +242,6 @@
                     else:
                         others[d - 2][i : i + 1, :] = piece
     extra[1].wait()
-    spread_beads(spots, speeds, rows, cols, left, right)
-    extra[2].wait()
     for i, (x, h) in enumerate(order):
         copies[i].wait()
         if i + ahead < len(copies):
@@ -458,8 +455,13 @@
 
 
 def pair_kernel(begin, end, *refs):
-    one_pair, steps, finish = pair_parts(begin, end, *refs)
-    lax.fori_loop(0, steps, lambda i, carry: one_pair(i), None, unroll=4)
+    prepare, one_pair, steps, finish = pair_parts(begin, end, *refs)
+    ahead = steps // (end - begin)
+    for i in range(-ahead, steps):
+        if i + ahead < steps:
+            prepare(i + ahead)
+        if i >= 0:
+            one_pair(i)
     finish()
 
 
@@ -472,15 +474,16 @@
     eye = lax.broadcasted_iota(I32, (tile, tile), 0) == lax.broadcasted_iota(I32, (tile, tile), 1)
     scale = jnp.where(eye, 15.0, 0.0).astype(BF16)
     acc[...] = jnp.zeros_like(acc)
-    for g in range(patches):
-        for p in range(pairs):
-            theta[g * pairs + p] = lax.dot_general(
-                scale, noise[begin + g, p], (((1,), (1,)), ((), ())), preferred_element_type=F32
-            )
-            first, second = pair_tiles[begin + g, 0, p], pair_tiles[begin + g, 1, p]
-            along[g * pairs + p] = jnp.dot(
-                left[begin + g, second], right[begin + g, first], preferred_element_type=F32
-            )
+
+    def prepare(i):
+        g, p = i // pairs, i % pairs
+        theta[i] = lax.dot_general(
+            scale, noise[begin + g, p], (((1,), (1,)), ((), ())), preferred_element_type=F32
+        )
+        first, second = pair_tiles[begin + g, 0, p], pair_tiles[begin + g, 1, p]
+        along[i] = jnp.dot(
+            left[begin + g, second], right[begin + g, first], preferred_element_type=F32
+        )
 
     def one_pair(i):
         g, p = i // pairs, i % pairs
@@ -508,13 +511,15 @@
                 speed = vel[c, begin + g : begin + g + 1, :]
                 base[c, begin + g : begin + g + 1, :] = 0.5 * speed + 0.04 * force
 
-    return one_pair, patches * pairs, finish
+    return prepare, one_pair, patches * pairs, finish
 
 
 def sums_and_pairs_kernel(n, per, begin, end, *refs):
     sums, rest = refs[: n + 2], refs[n + 2 :]
     pairs, (total, base, table, theta, along, acc) = rest[:7], rest[8:]
-    one_pair, steps, finish = pair_parts(begin, end, *pairs, base, theta, along, acc)
+    prepare, one_pair, steps, finish = pair_parts(begin, end, *pairs, base, theta, along, acc)
+    for i in range(steps):
+        prepare(i)
     patches = sums[1].shape[0]
 
     def beside(g):
@@ -670,39 +675,45 @@
     velocities = jnp.transpose(velocities, (1, 0, 2))
     pair_tiles = jnp.transpose(pair_tiles, (0, 2, 1))
 
-    post, fwd, bwd, up, down, *layouts = call(
+    post, fwd, bwd, up, down, *others = call(
         functools.partial(collide_kernel, n, per, nx),
-        [in_hbm(value) for value in (populations, fluid_mask, positions, velocities)],
+        [in_hbm(value) for value in (populations, fluid_mask, velocities)],
         [arr(19, nx, PAD, lanes), arr(384, lanes), arr(384, lanes)]
         + [arr(nx, 32, lanes)] * 2
-        + [
+        + [arr(16, lanes)] * (n - 3),
+        "collide_first",
+        cost(3_000_000_000, 11_000_000),
+        specs={i: ANY_SPEC for i in range(3)},
+        out_specs=[VMEM_SPEC] * (n + 2),
+        scratch_shapes=[
+            vmem((nx, 19, ROWS, lanes), F32),
+            vmem((nx, ROWS, lanes), I32),
+            vmem(velocities.shape, F32),
+            dma((2 * nx,)),
+            dma((2,)),
+        ],
+    )
+    before = shift(fwd, "ax", 1)
+    after = shift(bwd, "ax", -1)
+    layouts = call(
+        spread_beads,
+        [positions, velocities],
+        [
             arr(patches, 3, tiles, 8, 128),
             arr(patches, 3, tiles, 128, 128),
             jax.ShapeDtypeStruct((patches, tiles, 128, 48), BF16),
             jax.ShapeDtypeStruct((patches, tiles, 48, 128), BF16),
-        ]
-        + [arr(16, lanes)] * (n - 3),
-        "collide_first",
-        cost(3_000_000_000, 11_000_000),
-        specs={i: ANY_SPEC for i in range(4)},
-        out_specs=[VMEM_SPEC] * (n + 6),
-        scratch_shapes=[
-            vmem((nx, 19, ROWS, lanes), F32),
-            vmem((nx, ROWS, lanes), I32),
-            vmem(positions.shape, F32),
-            vmem(velocities.shape, F32),
-            dma((2 * nx,)),
-            dma((3,)),
         ],
-    )
-    before = shift(fwd, "ax", 1)
-    after = shift(bwd, "ax", -1)
-    layouts, others = layouts[:4], layouts[4:]
+        "bead_layouts",
+        cost(1000, 1000),
+        after=[down],
+        out_specs=[VMEM_SPEC] * 4,
+    )
     below = shift(up, "xs", 1)
     above = shift(down, "xs", -1)
     sent = [below] + [shift(other, "xs", d + 2) for d, other in enumerate(others)] + [above]
 
-    cuts = (patches * 5 // 8, patches * 7 // 8)
+    cuts = (patches * 5 // 8, patches * 6 // 8)
     bead_args = (pair_tiles, velocities, *layouts, pair_noise)
     base = pair_call(0, cuts[0], *bead_args, [], [down])
 

time: 48.4 us -> 48.1 us (level)
    pallas_call x12 -> x13, Pallas kernels: 27.3 us -> 27 us  [call(): pl.pallas_call(body, in_specs=[specs.get(i, VMEM_SPEC) for i in range(cou...]
  transfers between devices with their start and end apart: 12 -> 12, of which waited for: 5 -> 4; matrix products, arithmetic and copies ran while one was open for 0% -> 0% of each run, Pallas kernels for 34% -> 34%
where the time goes in v7:
time: 48.1 us; the launch traced here: 48 us
  Pallas kernels  27 us (56%)
  starting transfers between devices  17.5 us (36%)
  waiting for transfers between devices  2.66 us (6%)
  between operations  0.84 us (2%)
    pallas_call x13, Pallas kernels, call(): pl.pallas_call(body, in_specs=[specs.get(i, VMEM_SPEC) for i in range(cou...  27 us
    ppermute x9, starting transfers between devices, shift(): return lax.ppermute(value, axis, [(i, (i + by) % n) for i in range(n)])  13 us
    ppermute x3, starting transfers between devices, swap(): return lax.ppermute(value, axis, [(i, i ^ by) for i in range(n)])  4.45 us
    ppermute x9, waiting for transfers between devices, shift(): return lax.ppermute(value, axis, [(i, (i + by) % n) for i in range(n)])  1.54 us
    ppermute x3, waiting for transfers between devices, swap(): return lax.ppermute(value, axis, [(i, i ^ by) for i in range(n)])  1.12 us
  transfers between devices with their start and end apart: 12, of which 4 were waited for; matrix products, arithmetic and copies ran while one was open for 0% of the time, Pallas kernels for 34%

profile of v7, /device:TPU:0, one launch (start us, length us, event | category | flops | bytes accessed | tf_op | source)
XLA Modules:
  0.0 48.0 jit_solution(6805980806386985419)
XLA Ops:
  0.6 0.0 copy-start.1
  0.6 0.0 copy-start.3
  0.7 0.0 copy-start
  0.7 0.0 copy-start.5
  0.7 4.1 %collide_first.1 = (f32[19,4,88,256]{3,2,1,0:T(8,128)S(1)}, f32[384,256]{1,0:T(8,128)S(1)}, f32[384,256]{1,0:T(8,128)S(1)}, f32[4,32,256]{2,1,0:T(8,128)S(1)}, f...) custom-call(f32[19,4,64,256]{3,2,1,0:T(8,128)} %refs_0_.2, s32[4,64,256]{2,1,0:T(8,128)} %refs_1_.4, f32[3,8,512]{2,1,0:T(8,128)} %bitcast.5), custom_call_target="tpu_custom_call" | custom-call | flops 3000000000 | bytes 11000000 | tf_op jit(solution)/shard_map/collide_first/pallas_call | solution.py:63
  4.8 0.0 copy-start.2
  4.8 3.4 %collective-permute-start.2 = (f32[384,256]{1,0:T(8,128)S(1)}, f32[384,256]{1,0:T(8,128)S(1)}, u32[]{:S(2)}, u32[]{:S(2)}) collective-permute-start(f32[384,256]{1,0:T(8,128)S(1)} %get-tuple-element.48), channel_id=1, source_target_pairs={{0,28},{4,0},{8,4},{12,8},{16,12},{20,16},{24,20},{28,24},{1,29},{... | collective-permute-start | bytes 1179656 | tf_op jit(solution)/shard_map/ppermute | solution.py:634
  8.2 0.0 collective-permute-start.4
  8.2 1.6 %collective-permute-start = (f32[4,32,256]{2,1,0:T(8,128)S(1)}, f32[4,32,256]{2,1,0:T(8,128)S(1)}, u32[]{:S(2)}, u32[]{:S(2)}) collective-permute-start(f32[4,32,256]{2,1,0:T(8,128)S(1)} %get-tuple-element.40), channel_id=1, source_target_pairs={{0,1},{1,2},{2,3},{3,0},{4,5},{5,6},{6,7},{7,4},{8,9},{9,10},{10,1... | collective-permute-start | bytes 393224 | tf_op jit(solution)/shard_map/ppermute | solution.py:634
  9.8 2.2 %collective-permute-start.1 = (f32[4,32,256]{2,1,0:T(8,128)S(1)}, f32[4,32,256]{2,1,0:T(8,128)S(1)}, u32[]{:S(2)}, u32[]{:S(2)}) collective-permute-start(f32[4,32,256]{2,1,0:T(8,128)S(1)} %get-tuple-element.41.refs_2_.refs_7_), channel_id=1, source_target_pairs={{0,3},{1,0},{2,1},{3,2},{4,7},{5,4},{6,5},{7,6},{8,11},{9,8},{10,9... | collective-permute-start | bytes 393224 | tf_op jit(solution)/shard_map/ppermute | solution.py:634
  12.0 0.8 %collective-permute-start.6 = (f32[16,256]{1,0:T(8,128)S(1)}, f32[16,256]{1,0:T(8,128)S(1)}, u32[]{:S(2)}, u32[]{:S(2)}) collective-permute-start(f32[16,256]{1,0:T(8,128)S(1)} %get-tuple-element.54), channel_id=1, source_target_pairs={{0,2},{1,3},{2,0},{3,1},{4,6},{5,7},{6,4},{7,5},{8,10},{9,11},{10,... | collective-permute-start | bytes 49160 | tf_op jit(solution)/shard_map/ppermute | solution.py:634
  12.8 0.0 copy-done.1
  12.8 0.0 copy-done.3
  12.8 1.2 %bead_layouts.1 = (f32[8,3,4,8,128]{4,3,2,1,0:T(8,128)S(1)}, f32[8,3,4,128,128]{4,3,2,1,0:T(8,128)S(1)}, bf16[8,4,128,48]{3,2,1,0:T(8,128)(2,1)S(1)}, bf16[8,4,48,128]{3,2,1,0:T(8,128)(2,1)S(1)}) custom-call(f32[3,8,512]{2,1,0:T(8,128)S(1)} %bitcast.11, f32[3,8,512]{2,1,0:T(8,128)S(1)} %bitcast.6, f32[4,32,256]{2,1,0:T(8,128)S(1)} %get-tuple-element.41.refs_2_.refs_7_), custom_call_target="tpu_custom_call" | custom-call | flops 1000 | bytes 1000 | tf_op jit(solution)/shard_map/bead_layouts/pallas_call | solution.py:63
  14.0 0.0 copy-done
  14.0 0.0 copy-done.5
  14.0 3.1 %pair_forces.2.refs_4_.refs_7_ = f32[3,8,512]{2,1,0:T(8,128)S(1)} custom-call(s32[8,2,8]{2,1,0:T(2,128)S(1)} %bitcast.13, f32[3,8,512]{2,1,0:T(8,128)S(1)} %bitcast.7, f32[8,3,4,8,128]{4,3,2,1,0:T(8,128)S(1)} %get-tuple-element.42.refs_2_.refs_8_, f32[8,3,4,128,128]{4,3,2,1,0:T(8,128)S(1)} %get-tuple-element.43.refs_3_.refs_9_, ...), custom_call_target="tpu_custom_call" | custom-call | flops 1000 | bytes 1000 | tf_op jit(solution)/shard_map/pair_forces/pallas_call | solution.py:63
  17.2 0.0 collective-permute-done.refs_2_.refs_3_
  17.2 0.3 collective-permute-done.1.refs_3_.refs_5_
  17.5 0.0 copy-done.2
  17.5 0.2 edges.1
  17.6 2.3 %collective-permute-start.3 = (f32[16,256]{1,0:T(8,128)S(1)}, f32[16,256]{1,0:T(8,128)S(1)}, u32[]{:S(2)}, u32[]{:S(2)}) collective-permute-start(f32[16,256]{1,0:T(8,128)S(1)} %get-tuple-element.49), channel_id=1, source_target_pairs={{0,28},{4,0},{8,4},{12,8},{16,12},{20,16},{24,20},{28,24},{1,29},{... | collective-permute-start | bytes 49160 | tf_op jit(solution)/shard_map/ppermute | solution.py:634
  19.9 0.0 collective-permute-start.5
  20.0 1.2 %pair_forces.3.refs_6_.refs_13_ = f32[3,8,512]{2,1,0:T(8,128)S(1)} custom-call(s32[8,2,8]{2,1,0:T(2,128)S(1)} %bitcast.14, f32[3,8,512]{2,1,0:T(8,128)S(1)} %bitcast.8, f32[8,3,4,8,128]{4,3,2,1,0:T(8,128)S(1)} %get-tuple-element.42.refs_2_.refs_8_, f32[8,3,4,128,128]{4,3,2,1,0:T(8,128)S(1)} %get-tuple-element.43.refs_3_.refs_9_, ...), custom_call_target="tpu_custom_call", output_to_operand_aliasing={{}: (7, {})} | custom-call | flops 1000 | bytes 1000 | tf_op jit(solution)/shard_map/pair_forces/pallas_call | solution.py:63
  21.1 1.6 %middle_layers.1 = (f32[19,4,88,256]{3,2,1,0:T(8,128)S(1)}, s32[4,72,256]{2,1,0:T(8,128)S(1)}) custom-call(f32[19,4,88,256]{3,2,1,0:T(8,128)S(1)} %get-tuple-element.46.refs_0_, s32[4,88,256]{2,1,0:T(8,128)S(1)} %get-tuple-element.47.refs_1_.refs_8_), custom_call_target="tpu_custom_call" | custom-call | flops 1000 | bytes 1000 | tf_op jit(solution)/shard_map/middle_layers/pallas_call | solution.py:63
  22.8 0.0 collective-permute-done.6.refs_9_.refs_4_
  22.8 0.0 collective-permute-done.3.refs_8_.refs_3_
  22.8 1.2 %collective-permute-done.5.refs_3_ = f32[16,256]{1,0:T(8,128)S(1)} collective-permute-done((f32[16,256]{1,0:T(8,128)S(1)}, f32[16,256]{1,0:T(8,128)S(1)}, u32[]{:S(2)}, u32[]{:S(2)}) %collective-permute-start.5) | collective-permute-done | bytes 16416 | tf_op jit(solution)/shard_map/ppermute | solution.py:634
  24.0 0.0 collective-permute-done.2.refs_7_.refs_2_
  24.0 0.0 collective-permute-done.4.refs_2_
  24.0 0.9 %first_layer.1 = (f32[19,4,88,256]{3,2,1,0:T(8,128)S(1)}, s32[4,72,256]{2,1,0:T(8,128)S(1)}, f32[328,256]{1,0:T(8,128)S(1)}) custom-call(f32[19,4,88,256]{3,2,1,0:T(8,128)S(1)} %get-tuple-element.46.refs_0_, s32[4,88,256]{2,1,0:T(8,128)S(1)} %get-tuple-element.47.refs_1_.refs_8_, ...), custom_call_target="tpu_custom_call", output_to_operand_aliasing={{0}: (4, {}), {1}: (5, {})} | custom-call | flops 1000 | bytes 1000 | tf_op jit(solution)/shard_map/first_layer/pallas_call | solution.py:63
  24.9 0.0 copy-start.4
  24.9 0.9 %last_layer.1 = (f32[19,4,88,256]{3,2,1,0:T(8,128)S(1)}, s32[4,72,256]{2,1,0:T(8,128)S(1)}, f32[328,256]{1,0:T(8,128)S(1)}) custom-call(f32[19,4,88,256]{3,2,1,0:T(8,128)S(1)} %get-tuple-element.46.refs_0_, s32[4,88,256]{2,1,0:T(8,128)S(1)} %get-tuple-element.47.refs_1_.refs_8_, ...), custom_call_target="tpu_custom_call", output_to_operand_aliasing={{0}: (4, {}), {1}: (5, {})} | custom-call | flops 1000 | bytes 1000 | tf_op jit(solution)/shard_map/last_layer/pallas_call | solution.py:63
  25.8 0.0 copy-start.6
  25.8 0.1 collective-permute-start.8
  25.9 2.6 %collective-permute-start.7 = (f32[328,256]{1,0:T(8,128)S(1)}, f32[328,256]{1,0:T(8,128)S(1)}, u32[]{:S(2)}, u32[]{:S(2)}) collective-permute-start(f32[328,256]{1,0:T(8,128)S(1)} %get-tuple-element.62), channel_id=1, source_target_pairs={{0,28},{4,0},{8,4},{12,8},{16,12},{20,16},{24,20},{28,24},{1,29},{... | collective-permute-start | bytes 1007624 | tf_op jit(solution)/shard_map/ppermute | solution.py:634
  28.5 0.0 copy-done.4
  28.5 2.4 %final_middle.1 = (f32[19,4,64,256]{3,2,1,0:T(8,128)}, f32[3,4,64,256]{3,2,1,0:T(8,128)S(1)}, f32[8,8,512]{2,1,0:T(8,128)S(1)}) custom-call(f32[19,4,88,256]{3,2,1,0:T(8,128)S(1)} %get-tuple-element.57.refs_0_.refs_2_, s32[4,72,256]{2,1,0:T(8,128)S(1)} %get-tuple-element.58.refs_1_.refs_3_, s32[8,512]{1,0:T(8,128)S(1)} %copy-done.4, ...), custom_call_target="tpu_custom_call" | custom-call | flops 1000 | bytes 1000 | tf_op jit(solution)/shard_map/final_middle/pallas_call | solution.py:63
  31.0 0.0 copy-done.6
  31.0 5.6 %bead_sums.1 = (f32[4,256,256]{2,1,0:T(8,128)S(1)}, f32[3,8,512]{2,1,0:T(8,128)S(1)}) custom-call(s32[8]{0:T(128)S(1)} %copy-done.6, s32[8,512]{1,0:T(8,128)S(1)} %copy-done.4, f32[3,8,512]{2,1,0:T(8,128)S(1)} %bitcast.9, f32[4,32,256]{2,1,0:T(8,128)S(1)} %collective-permute-done.refs_2_.refs_3_, ...), custom_call_target="tpu_custom_call", output_to_operand_aliasing={{1}: (13, {})} | custom-call | flops 1000 | bytes 1000 | tf_op jit(solution)/shard_map/bead_sums/pallas_call | solution.py:63
  36.6 0.0 collective-permute-done.8.refs_5_
  36.6 0.0 collective-permute-done.7.refs_4_
  36.6 4.2 %final_outer.1 = (f32[19,4,64,256]{3,2,1,0:T(8,128)}, f32[3,4,64,256]{3,2,1,0:T(8,128)S(1)}, f32[8,512]{1,0:T(8,128)S(1)}, f32[8,512]{1,0:T(8,128)S(1)}, f32[8,512]{1,0:T(8,128)S(1)}, /*index=5*/f32[8,512]{1,0:T(8,128)S(1)}) custom-call(f32[19,4,64,256]{3,2,1,0:T(8,128)} %get-tuple-element.60.refs_0_, ...), custom_call_target="tpu_custom_call", output_to_operand_aliasing={{0}: (0, {}), {1}: (1, {})} | custom-call | flops 1000 | bytes 1000 | tf_op jit(solution)/shard_map/final_outer/pallas_call | solution.py:63
  40.8 1.9 %collective-permute-start.9 = (f32[8,512]{1,0:T(8,128)S(1)}, f32[8,512]{1,0:T(8,128)S(1)}, u32[]{:S(2)}, u32[]{:S(2)}) collective-permute-start(f32[8,512]{1,0:T(8,128)S(1)} %get-tuple-element.67), channel_id=1, source_target_pairs={{0,3},{1,2},{2,1},{3,0},{4,7},{5,6},{6,5},{7,4},{8,11},{9,10},{10,... | collective-permute-start | bytes 49160 | tf_op jit(solution)/shard_map/ppermute | solution.py:639
  42.7 0.7 %collective-permute-start.10 = (f32[8,512]{1,0:T(8,128)S(1)}, f32[8,512]{1,0:T(8,128)S(1)}, u32[]{:S(2)}, u32[]{:S(2)}) collective-permute-start(f32[8,512]{1,0:T(8,128)S(1)} %get-tuple-element.68), channel_id=1, source_target_pairs={{0,2},{1,3},{2,0},{3,1},{4,6},{5,7},{6,4},{7,5},{8,10},{9,11},{10,... | collective-permute-start | bytes 49160 | tf_op jit(solution)/shard_map/ppermute | solution.py:639
  43.3 1.9 %collective-permute-start.11 = (f32[8,512]{1,0:T(8,128)S(1)}, f32[8,512]{1,0:T(8,128)S(1)}, u32[]{:S(2)}, u32[]{:S(2)}) collective-permute-start(f32[8,512]{1,0:T(8,128)S(1)} %get-tuple-element.69.refs_2_), channel_id=1, source_target_pairs={{0,1},{1,0},{2,3},{3,2},{4,5},{5,4},{6,7},{7,6},{8,9},{9,8},{10,11... | collective-permute-start | bytes 49160 | tf_op jit(solution)/shard_map/ppermute | solution.py:639
  45.2 1.0 %drag_field.1 = f32[3,4,64,256]{3,2,1,0:T(8,128)} custom-call(f32[4,256,256]{2,1,0:T(8,128)S(1)} %get-tuple-element.64.refs_9_.refs_0_, f32[3,4,64,256]{3,2,1,0:T(8,128)S(1)} %get-tuple-element.73.refs_1_, f32[8,512]{1,0:T(8,128)S(1)} %get-tuple-element.69.refs_2_), custom_call_target="tpu_custom_call" | custom-call | flops 1000 | bytes 1000 | tf_op jit(solution)/shard_map/drag_field/pallas_call | solution.py:63
  46.2 0.2 collective-permute-done.9.refs_2_
  46.4 0.9 %collective-permute-done.10.refs_3_ = f32[8,512]{1,0:T(8,128)S(1)} collective-permute-done((f32[8,512]{1,0:T(8,128)S(1)}, f32[8,512]{1,0:T(8,128)S(1)}, u32[]{:S(2)}, u32[]{:S(2)}) %collective-permute-start.10) | collective-permute-done | bytes 16416 | tf_op jit(solution)/shard_map/ppermute | solution.py:639
  47.3 0.0 collective-permute-done.11.refs_4_
  47.3 0.7 %bead_update.1 = (f32[3,8,512]{2,1,0:T(8,128)}, f32[3,8,512]{2,1,0:T(8,128)}) custom-call(f32[3,8,512]{2,1,0:T(8,128)S(1)} %bitcast.12, f32[3,8,512]{2,1,0:T(8,128)S(1)} %get-tuple-element.65.refs_10_.refs_1_, f32[8,512]{1,0:T(8,128)S(1)} %collective-permute-done.9.refs_2_, f32[8,512]{1,0:T(8,128)S(1)} %collective-permute-done.10.refs_3_, ...), custom_call_target="tpu_custom_call" | custom-call | flops 1000 | bytes 1000 | tf_op jit(solution)/shard_map/bead_update/pallas_call | solution.py:63
Async XLA Ops:
  0.6 12.2 %copy-start.1 = (f32[8,3,512]{2,0,1:T(8,128)S(1)}, f32[8,3,512]{2,0,1:T(8,128)}, u32[]{:S(2)}) copy-start(f32[8,3,512]{2,0,1:T(8,128)} %param.13) | copy-start | bytes 147460
  0.6 12.2 %copy-start.3 = (f32[8,3,512]{2,0,1:T(8,128)S(1)}, f32[8,3,512]{2,0,1:T(8,128)}, u32[]{:S(2)}) copy-start(f32[8,3,512]{2,0,1:T(8,128)} %param.12) | copy-start | bytes 147460
  0.7 13.3 %copy-start = (bf16[8,8,128,128]{3,2,1,0:T(8,128)(2,1)S(1)}, bf16[8,8,128,128]{3,2,1,0:T(8,128)(2,1)}, u32[]{:S(2)}) copy-start(bf16[8,8,128,128]{3,2,1,0:T(8,128)(2,1)} %refs_12_.1) | copy-start | bytes 6291460
  0.7 13.3 %copy-start.5 = (s32[8,8,2]{1,2,0:T(2,128)S(1)}, s32[8,8,2]{1,2,0:T(2,128)}, u32[]{:S(2)}) copy-start(s32[8,8,2]{1,2,0:T(2,128)} %param.14) | copy-start | bytes 1540
  4.8 12.7 %copy-start.2 = (s32[4,64,256]{2,1,0:T(8,128)S(1)}, s32[4,64,256]{2,1,0:T(8,128)}, u32[]{:S(2)}) copy-start(s32[4,64,256]{2,1,0:T(8,128)} %refs_1_.4) | copy-start | bytes 786436
  4.8 19.2 %collective-permute-start.2 = (f32[384,256]{1,0:T(8,128)S(1)}, f32[384,256]{1,0:T(8,128)S(1)}, u32[]{:S(2)}, u32[]{:S(2)}) collective-permute-start(f32[384,256]{1,0:T(8,128)S(1)} %get-tuple-element.48), channel_id=1, source_target_pairs={{0,28},{4,0},{8,4},{12,8},{16,12},{20,16},{24,20},{28,24},{1,29},{... | collective-permute-start | bytes 1179656 | tf_op jit(solution)/shard_map/ppermute | solution.py:634
  8.2 15.8 %collective-permute-start.4 = (f32[384,256]{1,0:T(8,128)S(1)}, f32[384,256]{1,0:T(8,128)S(1)}, u32[]{:S(2)}, u32[]{:S(2)}) collective-permute-start(f32[384,256]{1,0:T(8,128)S(1)} %get-tuple-element.50), channel_id=1, source_target_pairs={{0,4},{4,8},{8,12},{12,16},{16,20},{20,24},{24,28},{28,0},{1,5},{5... | collective-permute-start | bytes 1179656 | tf_op jit(solution)/shard_map/ppermute | solution.py:634
  8.2 9.0 %collective-permute-start = (f32[4,32,256]{2,1,0:T(8,128)S(1)}, f32[4,32,256]{2,1,0:T(8,128)S(1)}, u32[]{:S(2)}, u32[]{:S(2)}) collective-permute-start(f32[4,32,256]{2,1,0:T(8,128)S(1)} %get-tuple-element.40), channel_id=1, source_target_pairs={{0,1},{1,2},{2,3},{3,0},{4,5},{5,6},{6,7},{7,4},{8,9},{9,10},{10,1... | collective-permute-start | bytes 393224 | tf_op jit(solution)/shard_map/ppermute | solution.py:634
  9.8 7.7 %collective-permute-start.1 = (f32[4,32,256]{2,1,0:T(8,128)S(1)}, f32[4,32,256]{2,1,0:T(8,128)S(1)}, u32[]{:S(2)}, u32[]{:S(2)}) collective-permute-start(f32[4,32,256]{2,1,0:T(8,128)S(1)} %get-tuple-element.41.refs_2_.refs_7_), channel_id=1, source_target_pairs={{0,3},{1,0},{2,1},{3,2},{4,7},{5,4},{6,5},{7,6},{8,11},{9,8},{10,9... | collective-permute-start | bytes 393224 | tf_op jit(solution)/shard_map/ppermute | solution.py:634
  12.0 10.8 %collective-permute-start.6 = (f32[16,256]{1,0:T(8,128)S(1)}, f32[16,256]{1,0:T(8,128)S(1)}, u32[]{:S(2)}, u32[]{:S(2)}) collective-permute-start(f32[16,256]{1,0:T(8,128)S(1)} %get-tuple-element.54), channel_id=1, source_target_pairs={{0,2},{1,3},{2,0},{3,1},{4,6},{5,7},{6,4},{7,5},{8,10},{9,11},{10,... | collective-permute-start | bytes 49160 | tf_op jit(solution)/shard_map/ppermute | solution.py:634
  17.6 5.1 %collective-permute-start.3 = (f32[16,256]{1,0:T(8,128)S(1)}, f32[16,256]{1,0:T(8,128)S(1)}, u32[]{:S(2)}, u32[]{:S(2)}) collective-permute-start(f32[16,256]{1,0:T(8,128)S(1)} %get-tuple-element.49), channel_id=1, source_target_pairs={{0,28},{4,0},{8,4},{12,8},{16,12},{20,16},{24,20},{28,24},{1,29},{... | collective-permute-start | bytes 49160 | tf_op jit(solution)/shard_map/ppermute | solution.py:634
  19.9 4.1 %collective-permute-start.5 = (f32[16,256]{1,0:T(8,128)S(1)}, f32[16,256]{1,0:T(8,128)S(1)}, u32[]{:S(2)}, u32[]{:S(2)}) collective-permute-start(f32[16,256]{1,0:T(8,128)S(1)} %get-tuple-element.51), channel_id=1, source_target_pairs={{0,4},{4,8},{8,12},{12,16},{16,20},{20,24},{24,28},{28,0},{1,5},{5... | collective-permute-start | bytes 49160 | tf_op jit(solution)/shard_map/ppermute | solution.py:634
  24.9 3.6 %copy-start.4 = (s32[8,512]{1,0:T(8,128)S(1)}, s32[8,512]{1,0:T(8,128)}, u32[]{:S(2)}) copy-start(s32[8,512]{1,0:T(8,128)} %refs_6_.5) | copy-start | bytes 49156
  25.8 5.2 %copy-start.6 = (s32[8]{0:T(128)S(1)}, s32[8]{0:T(128)}, u32[]{:S(2)}) copy-start(s32[8]{0:T(128)} %refs_7_.1) | copy-start | bytes 100
  25.8 10.7 %collective-permute-start.8 = (f32[328,256]{1,0:T(8,128)S(1)}, f32[328,256]{1,0:T(8,128)S(1)}, u32[]{:S(2)}, u32[]{:S(2)}) collective-permute-start(f32[328,256]{1,0:T(8,128)S(1)} %get-tuple-element.59.refs_3_.refs_14_), channel_id=1, source_target_pairs={{0,4},{4,8},{8,12},{12,16},{16,20},{20,24},{24,28},{28,0},{1,5},{5... | collective-permute-start | bytes 1007624 | tf_op jit(solution)/shard_map/ppermute | solution.py:634
  25.9 10.7 %collective-permute-start.7 = (f32[328,256]{1,0:T(8,128)S(1)}, f32[328,256]{1,0:T(8,128)S(1)}, u32[]{:S(2)}, u32[]{:S(2)}) collective-permute-start(f32[328,256]{1,0:T(8,128)S(1)} %get-tuple-element.62), channel_id=1, source_target_pairs={{0,28},{4,0},{8,4},{12,8},{16,12},{20,16},{24,20},{28,24},{1,29},{... | collective-permute-start | bytes 1007624 | tf_op jit(solution)/shard_map/ppermute | solution.py:634
  40.8 5.6 %collective-permute-start.9 = (f32[8,512]{1,0:T(8,128)S(1)}, f32[8,512]{1,0:T(8,128)S(1)}, u32[]{:S(2)}, u32[]{:S(2)}) collective-permute-start(f32[8,512]{1,0:T(8,128)S(1)} %get-tuple-element.67), channel_id=1, source_target_pairs={{0,3},{1,2},{2,1},{3,0},{4,7},{5,6},{6,5},{7,4},{8,11},{9,10},{10,... | collective-permute-start | bytes 49160 | tf_op jit(solution)/shard_map/ppermute | solution.py:639
  42.7 4.6 %collective-permute-start.10 = (f32[8,512]{1,0:T(8,128)S(1)}, f32[8,512]{1,0:T(8,128)S(1)}, u32[]{:S(2)}, u32[]{:S(2)}) collective-permute-start(f32[8,512]{1,0:T(8,128)S(1)} %get-tuple-element.68), channel_id=1, source_target_pairs={{0,2},{1,3},{2,0},{3,1},{4,6},{5,7},{6,4},{7,5},{8,10},{9,11},{10,... | collective-permute-start | bytes 49160 | tf_op jit(solution)/shard_map/ppermute | solution.py:639
  43.3 4.0 %collective-permute-start.11 = (f32[8,512]{1,0:T(8,128)S(1)}, f32[8,512]{1,0:T(8,128)S(1)}, u32[]{:S(2)}, u32[]{:S(2)}) collective-permute-start(f32[8,512]{1,0:T(8,128)S(1)} %get-tuple-element.69.refs_2_), channel_id=1, source_target_pairs={{0,1},{1,0},{2,3},{3,2},{4,5},{5,4},{6,7},{7,6},{8,9},{9,8},{10,11... | collective-permute-start | bytes 49160 | tf_op jit(solution)/shard_map/ppermute | solution.py:639
